TPU v7x, 128 devices: a whole 4x4x4 slice. The times are simulated.
128 devices in a mesh: dp: 64 (over z, y_lo, x, core), tensor: 2 (over y_hi).
Axes of the slice: x: 4, y: 4 (y_hi: 2, y_lo: 2; y = y_hi * 2 + y_lo), z: 4, core: 2. Of those that a mesh axis runs over, the one named last changes fastest.
Arguments:
- tokens: bfloat16 [65536, 8192], P('dp', 'tensor'), may hold values from -16 to 16
- cotangent: bfloat16 [65536, 1024], P('dp'), may hold values from -6 to 6
- old_weight: bfloat16 [2, 4096, 1024], P('tensor', 'dp'), may hold values from -0.0625 to 0.0625
- old_first: float32 [2, 4096, 1024], P('tensor', 'dp'), may hold values from -6 to 6
- old_second: float32 [2, 4096, 1024], P('tensor', 'dp'), may hold values from 0.25 to 4
- landing: int32 [64, 64], replicated, may hold values from 0 to 63, as said below
Outputs:
- keys: bfloat16 [65536, 1024], P('dp', 'tensor')
- back: bfloat16 [65536, 8192], P('dp', 'tensor')
- new_weight: bfloat16 [2, 4096, 1024], P('tensor', 'dp')
- new_first: float32 [2, 4096, 1024], P('tensor', 'dp')
- new_second: float32 [2, 4096, 1024], P('tensor', 'dp')
Inputs may be any that keep to these rules, and one draw needn't show every extreme that they name: Every column of landing is a permutation of 0..63.
All inputs are finite; a program needn't handle non-finite values.
Results may differ from a plain program's by a relative error of at most 0.0012.
Values may be sent and summed in bfloat16 or wider, within the bound.
No kernel may reach another device: no remote copies, remote signals or barrier semaphores. Data moves between devices by JAX's collectives and lax.ppermute only.
A program may use at most 128 MiB of HBM per device.

v0:
```python
import math

import jax
import jax.numpy as jnp
from jax import lax
from jax.sharding import PartitionSpec as P

beta_first = 0.9
beta_second = 0.95
learn_rate = 0.001
decay_rate = 0.1
epsilon = 1e-08
bias_first = 1.0 - math.exp(100.0 * math.log(beta_first))
bias_second = 1.0 - math.exp(100.0 * math.log(beta_second))


def positions(landing):
    count = landing.shape[0]
    lanes = jnp.arange(count, dtype=jnp.int32)
    hits = landing[None, :, :] == lanes[:, None, None]
    source = jnp.sum(jnp.where(hits, lanes[None, :, None], 0), axis=1)
    newidx = (lanes[None, :] * count + landing).reshape(-1)
    oldidx = (source * count + lanes[None, :]).T.reshape(-1)
    return (source, newidx, oldidx)


def shards(tokens, cotangent, old_weight, old_first, old_second, landing):
    count = lax.axis_size("dp")
    me = lax.axis_index("dp")
    rows = old_weight.shape[1]
    width = old_weight.shape[2]
    block = rows // count
    token_rows = tokens.shape[0]
    scale = 1.0 / math.sqrt(token_rows * count)
    source, newidx, oldidx = positions(landing)
    source_col = lax.dynamic_slice_in_dim(source, me, 1, 1)[:, 0]
    got_first = lax.all_to_all(
        old_first.reshape(count, block, width), "dp", split_axis=0, concat_axis=0, tiled=True
    )
    got_second = lax.all_to_all(
        old_second.reshape(count, block, width), "dp", split_axis=0, concat_axis=0, tiled=True
    )
    first_now = jnp.take(got_first, source_col, axis=0).reshape(rows, width)
    second_now = jnp.take(got_second, source_col, axis=0).reshape(rows, width)
    got = lax.all_to_all(
        old_weight.reshape(count, block, width), "dp", split_axis=0, concat_axis=0, tiled=True
    )
    own = jnp.take(got, source_col, axis=0).reshape(rows, width)
    held = jnp.zeros((rows, width), jnp.float32)
    picked = tokens
    total = jnp.dot(
        picked, lax.all_gather(own, "dp", axis=0, tiled=True), preferred_element_type=jnp.float32
    )
    partial_keys, held = (total, held)
    back_out = lax.dot_general(
        cotangent,
        lax.all_gather(own, "dp", axis=0, tiled=True),
        (((1,), (1,)), ((), ())),
        preferred_element_type=jnp.float32,
    ).astype(jnp.bfloat16)
    keys = lax.psum_scatter(partial_keys, "tensor", scatter_dimension=1, tiled=True).astype(
        jnp.bfloat16
    )
    picked = tokens
    grad = lax.psum_scatter(
        lax.dot_general(
            picked, cotangent, (((0,), (0,)), ((), ())), preferred_element_type=jnp.float32
        )
        * scale,
        "dp",
        scatter_dimension=0,
        tiled=True,
    )
    new_first = beta_first * first_now + (1.0 - beta_first) * grad
    new_second = beta_second * second_now + (1.0 - beta_second) * grad * grad
    step = new_first / bias_first / (jnp.sqrt(new_second / bias_second) + epsilon)
    base = own.astype(jnp.float32)
    new_weight = (base - learn_rate * (step + decay_rate * base)).astype(jnp.bfloat16)
    return (keys, back_out, new_weight[None], new_first[None], new_second[None])


def solution(mesh):
    in_specs = (
        P("dp", "tensor"),
        P("dp", None),
        P("tensor", "dp", None),
        P("tensor", "dp", None),
        P("tensor", "dp", None),
        P(),
    )
    out_specs = (
        P("dp", "tensor"),
        P("dp", "tensor"),
        P("tensor", "dp", None),
        P("tensor", "dp", None),
        P("tensor", "dp", None),
    )
    return jax.shard_map(shards, mesh=mesh, in_specs=in_specs, out_specs=out_specs, check_vma=False)
```

profile of v0, /device:TPU:0, one launch (start us, length us, event | category | flops | bytes accessed | tf_op | source)
XLA Modules:
  0.0 532.2 jit_solution(15748539529034174789)
XLA Ops:
  7.2 1.5 copy-done
  8.8 14.6 %convolution_multiply_fusion = f32[4096,1024]{1,0:T(8,128)} fusion(bf16[1024,4096]{1,0:T(8,128)(2,1)} %param.8, bf16[1024,1024]{1,0:T(8,128)(2,1)S(1)} %copy-done), kind=kOutput, calls=%fused_computation.3 | convolution fusion | flops 8594128896 | bytes 27262976 | tf_op jit(solution)/shard_map/dot_general | solution.py:66
  24.2 0.7 reduce.6
  24.9 0.7 reshape.117
  25.6 9.9 %all-to-all-start = ((bf16[64,2,512]{2,1,0:T(2,128)(2,1)}), bf16[64,2,512]{2,1,0:T(2,128)(2,1)S(1)}, u32[]{:S(2)}, u32[]{:S(2)}) async-start(bf16[64,2,512]{2,1,0:T(2,128)(2,1)} %reshape.117), calls=%async_computation | async-start | bytes 262144 | tf_op jit(solution)/shard_map/all_to_all | solution.py:45
  35.5 0.9 reshape.71
  36.4 0.9 reshape.72
  37.9 6.1 %all-to-all-done = bf16[64,2,512]{2,1,0:T(2,128)(2,1)S(1)} async-done(((bf16[64,2,512]{2,1,0:T(2,128)(2,1)}), bf16[64,2,512]{2,1,0:T(2,128)(2,1)S(1)}, u32[]{:S(2)}, u32[]{:S(2)}) %all-to-all-start) | async-done | bytes 131104 | tf_op jit(solution)/shard_map/all_to_all | solution.py:45
  44.0 5.3 all-to-all-start.1
  49.3 11.2 %all-to-all-done.1 = f32[64,1,1024]{2,1,0:T(1,128)S(1)} async-done(((f32[64,1,1024]{2,1,0:T(1,128)}), f32[64,1,1024]{2,1,0:T(1,128)S(1)}, u32[]{:S(2)}, u32[]{:S(2)}) %all-to-all-start.1) | async-done | bytes 262176 | tf_op jit(solution)/shard_map/all_to_all | solution.py:37
  60.6 4.6 all-to-all-start.2
  65.6 0.7 gather_fusion
  66.4 0.7 gather_fusion.1
  67.1 8.3 %all-to-all-done.2 = f32[64,1,1024]{2,1,0:T(1,128)S(1)} async-done(((f32[64,1,1024]{2,1,0:T(1,128)}), f32[64,1,1024]{2,1,0:T(1,128)S(1)}, u32[]{:S(2)}, u32[]{:S(2)}) %all-to-all-start.2) | async-done | bytes 262176 | tf_op jit(solution)/shard_map/all_to_all | solution.py:40
  75.4 0.7 gather_fusion.2
  76.1 263.6 %reduce-scatter.5.cloned.1.call-done = f32[64,1024]{1,0:T(8,128)} async-done(((f32[4096,1024]{1,0:T(8,128)}), f32[64,1024]{1,0:T(8,128)}) %reduce-scatter.5.cloned.1.call-update) | async-done | bytes 262160 | tf_op jit(solution)/shard_map/reduce_scatter | solution.py:65
  339.7 2.1 fusion.6
  342.1 108.4 %all-gather.2.cloned.1.call-done = bf16[4096,1024]{1,0:T(8,128)(2,1)} async-done(((bf16[64,1024]{1,0:T(8,128)(2,1)}), bf16[4096,1024]{1,0:T(8,128)(2,1)}) %all-gather.2.cloned.1.call-update) | async-done | bytes 8388624 | tf_op jit(solution)/shard_map/all_gather | solution.py:52
  450.5 15.1 %convolution_bitcast_fusion = f32[1024,1024]{0,1:T(8,128)} fusion(bf16[4096,1024]{1,0:T(8,128)(2,1)} %all-gather.2.cloned.1.call-done, bf16[1024,4096]{1,0:T(8,128)(2,1)} %param.8), kind=kOutput, calls=%fused_computation.5 | convolution fusion | flops 8589934592 | bytes 20971520 | tf_op jit(solution)/shard_map/dot_general | solution.py:51
  465.6 14.6 %convert_bitcast_fusion = bf16[1024,4096]{0,1:T(8,128)(2,1)} fusion(bf16[4096,1024]{1,0:T(8,128)(2,1)} %all-gather.2.cloned.1.call-done, bf16[1024,1024]{1,0:T(8,128)(2,1)S(1)} %copy-done), kind=kOutput, calls=%fused_computation.4 | convolution fusion | flops 8594128896 | bytes 18874368 | tf_op jit(solution)/shard_map/dot_general | solution.py:55
  480.2 11.9 %copy.23 = bf16[1024,4096]{1,0:T(8,128)(2,1)} copy(bf16[1024,4096]{0,1:T(8,128)(2,1)} %convert_bitcast_fusion) | data formatting | bytes 16777216
  492.1 30.4 %reduce-scatter.3.cloned.1.call-done = f32[1024,512]{0,1:T(8,128)} async-done(((f32[1024,1024]{0,1:T(8,128)}), f32[1024,512]{0,1:T(8,128)}) %reduce-scatter.3.cloned.1.call-update) | async-done | bytes 2097168 | tf_op jit(solution)/shard_map/reduce_scatter | solution.py:61
  522.6 1.7 convert_element_type.15
  524.3 1.3 copy.22
  (27 shorter events, 2.3 us)
Async XLA Ops:
  7.2 1.6 copy-start
  7.2 332.6 %reduce-scatter.5.cloned.1.call-start = ((), (), s32[]{:S(2)}) async-start(), calls=%async_computation.7 | async-start | bytes 17039360 | tf_op jit(solution)/shard_map/reduce_scatter | solution.py:65
  23.3 0.9 copy-start.3
  23.3 12.2 %copy-start.1 = (f32[1,64,1024]{2,1,0:T(8,128)S(1)}, f32[1,64,1024]{2,1,0:T(8,128)}, u32[]{:S(2)}) copy-start(f32[1,64,1024]{2,1,0:T(8,128)} %param.11) | copy-start | bytes 786436
  23.3 13.1 %copy-start.2 = (f32[1,64,1024]{2,1,0:T(8,128)S(1)}, f32[1,64,1024]{2,1,0:T(8,128)}, u32[]{:S(2)}) copy-start(f32[1,64,1024]{2,1,0:T(8,128)} %param.12) | copy-start | bytes 786436
  23.3 14.0 %copy-start.4 = (s32[64,64]{1,0:T(8,128)S(1)}, s32[64,64]{1,0:T(8,128)}, u32[]{:S(2)}) copy-start(s32[64,64]{1,0:T(8,128)} %param.13) | copy-start | bytes 49156
  25.6 18.4 %all-to-all-start = ((bf16[64,2,512]{2,1,0:T(2,128)(2,1)}), bf16[64,2,512]{2,1,0:T(2,128)(2,1)S(1)}, u32[]{:S(2)}, u32[]{:S(2)}) async-start(bf16[64,2,512]{2,1,0:T(2,128)(2,1)} %reshape.117), calls=%async_computation | async-start | bytes 262144 | tf_op jit(solution)/shard_map/all_to_all | solution.py:45
  44.0 16.5 %all-to-all-start.1 = ((f32[64,1,1024]{2,1,0:T(1,128)}), f32[64,1,1024]{2,1,0:T(1,128)S(1)}, u32[]{:S(2)}, u32[]{:S(2)}) async-start(f32[64,1,1024]{2,1,0:T(1,128)} %reshape.71), calls=%async_computation.2 | async-start | bytes 524288 | tf_op jit(solution)/shard_map/all_to_all | solution.py:37
  60.6 14.8 %all-to-all-start.2 = ((f32[64,1,1024]{2,1,0:T(1,128)}), f32[64,1,1024]{2,1,0:T(1,128)S(1)}, u32[]{:S(2)}, u32[]{:S(2)}) async-start(f32[64,1,1024]{2,1,0:T(1,128)} %reshape.72), calls=%async_computation.4 | async-start | bytes 524288 | tf_op jit(solution)/shard_map/all_to_all | solution.py:40
  65.2 385.3 %all-gather.2.cloned.1.call-start = ((), (), s32[]{:S(2)}) async-start(), calls=%async_computation.5 | async-start | bytes 8519680 | tf_op jit(solution)/shard_map/all_gather | solution.py:52
  341.9 180.7 %reduce-scatter.3.cloned.1.call-start = ((), (), s32[]{:S(2)}) async-start(), calls=%async_computation.6 | async-start | bytes 6291456 | tf_op jit(solution)/shard_map/reduce_scatter | solution.py:61
Sparse Core Ops, SparseCore 0:
  23.5 316.2 reduce-scatter.4
  342.0 108.4 all-gather.1
  465.8 56.7 reduce-scatter.2
where the time goes:
time: 534 us; the launch traced here: 532 us
  waiting for transfers between devices  428 us (80%)
  matrix products  44.2 us (8%)
  local copies, waits for them, and re-layouts  20.5 us (4%)
  starting transfers between devices  20.1 us (4%)
  between operations  13.9 us (3%)
  other arithmetic  5.36 us (1%)
    reduce_scatter x1, waiting for transfers between devices, shards(): lax.psum_scatter(lax.dot_general(picked, cotangent, (((0,), (0,)), ((), (...  264 us
    all_gather x1, waiting for transfers between devices, shards(): lax.all_gather(own, 'dp', axis=0, tiled=True)  108 us
    reduce_scatter x1, waiting for transfers between devices, shards(): lax.psum_scatter(partial_keys, 'tensor', scatter_dimension=1, tiled=True)  30.4 us
    unnamed x17, local copies, waits for them, and re-layouts  16.1 us
    dot_general x1, matrix products, shards(): jnp.dot(picked, lax.all_gather(own, 'dp', axis=0, tiled=True), preferred_...  15.1 us
    dot_general x1, matrix products, shards(): lax.dot_general(cotangent, lax.all_gather(own, 'dp', axis=0, tiled=True),...  14.6 us
    dot_general x1, matrix products, shards(): lax.dot_general(picked, cotangent, (((0,), (0,)), ((), ())), preferred_el...  14.6 us
    all_to_all x1, waiting for transfers between devices, shards(): lax.all_to_all(old_first.reshape(count, block, width), 'dp', split_axis=0...  11.2 us
  transfers between devices with their start and end apart: 6, of which 6 were waited for; matrix products, arithmetic and copies ran while one was open for 6% of the time, Pallas kernels for 0%

commit v1 on v0

v1 whole, which is shorter than its diff:
```python
import math

import jax
import jax.numpy as jnp
from jax import lax
from jax.experimental import pallas as pl
from jax.experimental.pallas import tpu as pltpu
from jax.sharding import Mesh, PartitionSpec as P

beta_first = 0.9
beta_second = 0.95
learn_rate = 0.001
decay_rate = 0.1
epsilon = 1e-08
bias_first = 1.0 - math.exp(100.0 * math.log(beta_first))
bias_second = 1.0 - math.exp(100.0 * math.log(beta_second))

AXES = ("z", "l", "x", "c", "t")
SIZES = (4, 2, 4, 2, 2)
DP = AXES[:4]
NZ, NL, NX, NC, NT = SIZES
COUNT = NZ * NL * NX * NC
MIB = 1 << 20


def shift(value, axis, step):
    size = SIZES[AXES.index(axis)]
    return lax.ppermute(value, axis, [(i, (i + step) % size) for i in range(size)])


def gather_axis(value, axis):
    return [value] + [shift(value, axis, -k) for k in (1, 2, 3)]


def grad_kernel(place, tokens, cotangent, keep, send, held):
    x, c = place[2], place[3]
    term = lax.dot_general(
        tokens[...], cotangent[...], (((0,), (0,)), ((), ())), preferred_element_type=jnp.float32
    )
    held[...] = term.reshape(held.shape)
    for k in range(NX):
        at = lax.rem(x + k, NX)
        keep[0, k] = held[at, c]
        send[0, k] = held[at, 1 - c].astype(send.dtype)


def local_grad(place, tokens, cotangent):
    rows, half = tokens.shape
    width = cotangent.shape[1]
    groups = NZ * NL
    block = half // groups
    own = half // COUNT

    def columns(k, place):
        return (0, lax.rem(place[0] + k // NL, NZ) * NL + lax.rem(place[1] + k % NL, NL))

    out = (groups, NX, own, width)
    out_spec = pl.BlockSpec((1, NX, own, width), lambda k, place: (k, 0, 0, 0))
    return pl.pallas_call(
        grad_kernel,
        grid_spec=pltpu.PrefetchScalarGridSpec(
            num_scalar_prefetch=1,
            grid=(groups,),
            in_specs=[
                pl.BlockSpec((rows, block), columns),
                pl.BlockSpec((rows, width), lambda k, place: (0, 0)),
            ],
            out_specs=[out_spec, out_spec],
            scratch_shapes=[pltpu.VMEM((NX, NC, own, width), jnp.float32)],
        ),
        out_shape=[
            jax.ShapeDtypeStruct(out, jnp.float32),
            jax.ShapeDtypeStruct(out, jnp.bfloat16),
        ],
        compiler_params=pltpu.CompilerParams(vmem_limit_bytes=40 * MIB),
        cost_estimate=pl.CostEstimate(
            flops=2 * rows * half * width, bytes_accessed=rows * half * 2 + half * width * 3, transcendentals=0
        ),
    )(place, tokens, cotangent)


def keys_kernel(place, target, tokens, *refs):
    pieces, (full, keys_send, keys_keep, held) = refs[:-4], refs[-4:]
    o = pl.program_id(0)
    t = place[4]
    per_half = len(pieces) // 2
    block = full.shape[0]
    width = full.shape[1]

    def work(parts):
        rows = jnp.concatenate([p[...].reshape(-1, width) for p in parts], axis=0)
        pick = lax.broadcasted_iota(jnp.int32, (block, rows.shape[0]), 0) == target[0]
        pick = jnp.where(pick, 1.0, 0.0).astype(jnp.bfloat16)
        moved = jnp.dot(pick, rows, preferred_element_type=jnp.float32).astype(jnp.bfloat16)
        full[...] = moved
        for h in range(NT):
            held[h] = moved[:, h * (width // NT) : (h + 1) * (width // NT)]

    pl.when(o < 4)(lambda: work(pieces[:per_half]))
    pl.when(o >= 4)(lambda: work(pieces[per_half:]))

    @pl.when(o == 0)
    def _():
        keys_send[...] = jnp.zeros_like(keys_send)
        keys_keep[...] = jnp.zeros_like(keys_keep)

    keys_send[...] += jnp.dot(tokens[...], held[1 - t], preferred_element_type=jnp.float32)
    keys_keep[...] += jnp.dot(tokens[...], held[t], preferred_element_type=jnp.float32)


def reorder_and_keys(place, target, tokens, pieces_a, pieces_b):
    rows, half = tokens.shape
    width = pieces_a[0].shape[-1]
    block = half // 8
    inner = pieces_a[0].shape[:2]
    spec_a = pl.BlockSpec((*inner, 1, 8, width), lambda o, place: (0, 0, jnp.minimum(o, 3), 0, 0))
    spec_b = pl.BlockSpec((*inner, 1, 8, width), lambda o, place: (0, 0, jnp.maximum(o, 4) - 4, 0, 0))
    keys_spec = pl.BlockSpec((rows, width // NT), lambda o, place: (0, 0))
    keys_type = jax.ShapeDtypeStruct((rows, width // NT), jnp.float32)
    return pl.pallas_call(
        keys_kernel,
        grid_spec=pltpu.PrefetchScalarGridSpec(
            num_scalar_prefetch=1,
            grid=(8,),
            in_specs=[
                pl.BlockSpec((1, 1, block), lambda o, place: (o, 0, 0)),
                pl.BlockSpec((rows, block), lambda o, place: (0, o)),
            ]
            + [spec_a] * len(pieces_a)
            + [spec_b] * len(pieces_b),
            out_specs=[pl.BlockSpec((block, width), lambda o, place: (o, 0)), keys_spec, keys_spec],
            scratch_shapes=[pltpu.VMEM((NT, block, width // NT), jnp.bfloat16)],
        ),
        out_shape=[jax.ShapeDtypeStruct((half, width), jnp.bfloat16), keys_type, keys_type],
        compiler_params=pltpu.CompilerParams(vmem_limit_bytes=48 * MIB),
        cost_estimate=pl.CostEstimate(
            flops=3 * rows * half * width, bytes_accessed=rows * half * 2 + half * width * 6, transcendentals=0
        ),
    )(place, target, tokens, *pieces_a, *pieces_b)


def shards(tokens, cotangent, old_weight, old_first, old_second, landing):
    z, l, x, c, t = [lax.axis_index(a).astype(jnp.int32) for a in AXES]
    place = jnp.stack([z, l, x, c, t])
    me = ((z * NL + l) * NX + x) * NC + c
    rows, width = old_weight.shape[1:]
    scale = 1.0 / math.sqrt(tokens.shape[0] * COUNT)
    half_rows = rows // 2

    own = old_weight.reshape(rows, width)
    other = shift(own, "l", 1)
    pair = jnp.stack([own, other]).reshape(NL, 2, half_rows, width)

    def gathered(part, first, second):
        stage = jnp.stack(gather_axis(part, first))
        here = gather_axis(stage.reshape(NX * NL, half_rows // 8, 8, width), second)
        return here

    part_a = gathered(pair[:, 0], "z", "x")
    part_b = gathered(pair[:, 1], "x", "z")
    pieces_a = [v.reshape(NX, NL, half_rows // 8, 8, width) for v in part_a + [shift(v, "c", 1) for v in part_a]]
    pieces_b = [v.reshape(NX, NL, half_rows // 8, 8, width) for v in part_b + [shift(v, "c", 1) for v in part_b]]

    step4 = jnp.arange(4, dtype=jnp.int32)
    step2 = jnp.arange(2, dtype=jnp.int32)
    xs, zs, ls, cs = (x + step4) % NX, (z + step4) % NZ, (l + step2) % NL, (c + step2) % NC

    def owner(zi, li, xi, ci):
        return ((zi * NL + li) * NX + xi) * NC + ci

    order_a = owner(zs[None, None, :, None], ls[None, None, None, :], xs[None, :, None, None], cs[:, None, None, None])
    order_b = owner(zs[None, :, None, None], ls[None, None, None, :], xs[None, None, :, None], cs[:, None, None, None])

    def targets(order, at):
        spots = jnp.take(landing, order.reshape(-1), axis=0)[:, at : at + half_rows]
        spots = spots.reshape(COUNT, half_rows // 8, 8) + jnp.arange(8, dtype=jnp.int32) * COUNT
        return spots.transpose(1, 0, 2).reshape(half_rows // 8, 1, COUNT * 8)

    target = jnp.concatenate([targets(order_a, 0), targets(order_b, half_rows)])

    moments = jnp.concatenate([old_first.reshape(rows, width), old_second.reshape(rows, width)], axis=1)
    moments = lax.all_to_all(moments, DP, split_axis=0, concat_axis=0, tiled=True)

    keep, send = local_grad(place, tokens, cotangent)
    came = shift(send, "c", 1)
    shape = (NZ, NL, NX, rows, width)
    keep, came = keep.reshape(shape), came.reshape(shape)

    def both(index):
        return keep[index] + came[index].astype(jnp.float32)

    def reduced(terms, axis):
        total = terms[0]
        for k in (1, 2, 3):
            total = total + shift(terms[k].astype(jnp.bfloat16), axis, k).astype(jnp.float32)
        return total

    low, high = slice(0, half_rows), slice(half_rows, rows)
    sum_a = reduced([both((k, slice(None), slice(None), low)) for k in range(4)], "z")
    sum_b = reduced([both((slice(None), slice(None), k, high)) for k in range(4)], "x")
    sum_a = reduced([sum_a[:, k] for k in range(4)], "x")
    sum_b = reduced([sum_b[k] for k in range(4)], "z")
    sums = jnp.concatenate([sum_a, sum_b], axis=1)
    grad = (sums[0] + shift(sums[1].astype(jnp.bfloat16), "l", 1).astype(jnp.float32)) * scale

    full, keys_send, keys_keep = reorder_and_keys(place, target, tokens, pieces_a, pieces_b)
    keys = (keys_keep + shift(keys_send, "t", 1)).astype(jnp.bfloat16)
    back = lax.dot_general(
        cotangent, full, (((1,), (1,)), ((), ())), preferred_element_type=jnp.float32
    ).astype(jnp.bfloat16)

    column = lax.dynamic_slice_in_dim(landing, me, 1, 1)[:, 0]
    lanes = jnp.arange(COUNT, dtype=jnp.int32)
    source = jnp.sum(jnp.where(column[None, :] == lanes[:, None], lanes[None, :], 0), axis=1)
    moments = jnp.take(moments, source, axis=0)
    first_now, second_now = moments[:, :width], moments[:, width:]
    base = lax.dynamic_slice_in_dim(full, me * rows, rows, 0).astype(jnp.float32)
    new_first = beta_first * first_now + (1.0 - beta_first) * grad
    new_second = beta_second * second_now + (1.0 - beta_second) * grad * grad
    step = new_first / bias_first / (jnp.sqrt(new_second / bias_second) + epsilon)
    new_weight = (base - learn_rate * (step + decay_rate * base)).astype(jnp.bfloat16)
    return (keys, back, new_weight[None], new_first[None], new_second[None])


def solution(mesh):
    fine = Mesh(mesh.devices.reshape(SIZES), AXES)
    in_specs = (
        P(DP, "t"),
        P(DP, None),
        P("t", DP, None),
        P("t", DP, None),
        P("t", DP, None),
        P(),
    )
    out_specs = (
        P(DP, "t"),
        P(DP, "t"),
        P("t", DP, None),
        P("t", DP, None),
        P("t", DP, None),
    )
    return jax.shard_map(shards, mesh=fine, in_specs=in_specs, out_specs=out_specs, check_vma=False)
```

time: 534 us -> 233 us (0.44)
  waiting for transfers between devices: 428 us -> 77.5 us
  Pallas kernels: 0 us -> 36.1 us
  starting transfers between devices: 20.1 us -> 52 us
  matrix products: 44.2 us -> 14.6 us
  other arithmetic: 5.36 us -> 20.8 us
  between operations: 13.9 us -> 1.07 us
  local copies, waits for them, and re-layouts: 20.5 us -> 29.8 us
    reduce_scatter x2 -> x0, waiting for transfers between devices: 294 us -> none  [the longest x1 264 us: shards(): lax.psum_scatter(lax.dot_general(picked, cotangent, (((0,), (0,)), ((), (...]
    all_gather x1 -> x0, waiting for transfers between devices: 108 us -> none  [shards(): lax.all_gather(own, 'dp', axis=0, tiled=True)]
    ppermute x0 -> x36, waiting for transfers between devices: none -> 77.5 us  [shift(): lax.ppermute(value, axis, [(i, (i + step) % size) for i in range(size)])]
    ppermute x0 -> x36, starting transfers between devices: none -> 41.8 us  [shift(): lax.ppermute(value, axis, [(i, (i + step) % size) for i in range(size)])]
    pallas_call x0 -> x2, Pallas kernels: none -> 36.1 us  [the longest x1 20.8 us: reorder_and_keys(): pl.pallas_call(keys_kernel, grid_spec=pltpu.PrefetchScalarGridSpec(num_sc...]
    dot_general x3 -> x1, matrix products: 44.2 us -> 14.6 us  [shards(): lax.dot_general(cotangent, full, (((1,), (1,)), ((), ())), preferred_elem...]
    all_to_all x3 -> x1, waiting for transfers between devices: 25.7 us -> 0.01 us  [shards(): lax.all_to_all(moments, DP, split_axis=0, concat_axis=0, tiled=True)]
    all_to_all x3 -> x1, starting transfers between devices: 19.8 us -> 10.2 us  [shards(): lax.all_to_all(moments, DP, split_axis=0, concat_axis=0, tiled=True)]
  transfers between devices with their start and end apart: 6 -> 37, of which waited for: 6 -> 15; matrix products, arithmetic and copies ran while one was open for 6% -> 25% of each run, Pallas kernels for 0% -> 9%
where the time goes in v1:
time: 233 us; the launch traced here: 232 us
  waiting for transfers between devices  77.5 us (33%)
  starting transfers between devices  52 us (22%)
  Pallas kernels  36.1 us (15%)
  local copies, waits for them, and re-layouts  29.8 us (13%)
  other arithmetic  20.8 us (9%)
  matrix products  14.6 us (6%)
    ppermute x36, waiting for transfers between devices, shift(): lax.ppermute(value, axis, [(i, (i + step) % size) for i in range(size)])  77.5 us
    ppermute x36, starting transfers between devices, shift(): lax.ppermute(value, axis, [(i, (i + step) % size) for i in range(size)])  41.8 us
    pallas_call x1, Pallas kernels, reorder_and_keys(): pl.pallas_call(keys_kernel, grid_spec=pltpu.PrefetchScalarGridSpec(num_sc...  20.8 us
    unnamed x44, local copies, waits for them, and re-layouts  17.4 us
    pallas_call x1, Pallas kernels, local_grad(): pl.pallas_call(grad_kernel, grid_spec=pltpu.PrefetchScalarGridSpec(num_sc...  15.3 us
    dot_general x1, matrix products, shards(): lax.dot_general(cotangent, full, (((1,), (1,)), ((), ())), preferred_elem...  14.6 us
    all_to_all x1, starting transfers between devices, shards(): lax.all_to_all(moments, DP, split_axis=0, concat_axis=0, tiled=True)  10.2 us
    slice x2, local copies, waits for them, and re-layouts, both(): return keep[index] + came[index].astype(jnp.float32)  6.19 us
  transfers between devices with their start and end apart: 37, of which 15 were waited for; matrix products, arithmetic and copies ran while one was open for 25% of the time, Pallas kernels for 9%

profile of v1, /device:TPU:0, one launch (start us, length us, event | category | flops | bytes accessed | tf_op | source)
XLA Modules:
  0.0 231.9 jit_solution(11079895319321709399)
XLA Ops:
  2.3 15.3 %shard_map.102 = (f32[8,4,64,1024]{3,2,1,0:T(8,128)}, bf16[8,4,64,1024]{3,2,1,0:T(8,128)(2,1)}) custom-call(s32[5]{0:T(128)S(1)} %stack.75.place, bf16[1024,4096]{1,0:T(8,128)(2,1)} %tokens.3, bf16[1024,1024]{1,0:T(8,128)(2,1)S(1)} %copy-done.2), custom_call_target="tpu_custom_call" | custom-call | flops 8589934592 | bytes 20971520 | tf_op jit(solution)/shard_map/pallas_call | solution.py:59
  18.9 10.2 %all-to-all-start = ((f32[64,1,2048]{2,1,0:T(1,128)}), f32[64,1,2048]{2,1,0:T(1,128)}, u32[]{:S(2)}, u32[]{:S(2)}) async-start(f32[64,1,2048]{2,1,0:T(1,128)} %all_to_all.8), calls=%async_computation | async-start | bytes 1048576 | tf_op jit(solution)/shard_map/all_to_all | solution.py:182
  32.7 7.1 %collective-permute-done = bf16[64,1024]{1,0:T(8,128)(2,1)S(1)} collective-permute-done((bf16[64,1024]{1,0:T(8,128)(2,1)S(1)}, bf16[64,1024]{1,0:T(8,128)(2,1)S(1)}, u32[]{:S(2)}, u32[]{:S(2)}) %collective-permute-start) | collective-permute-done | bytes 131104 | tf_op jit(solution)/shard_map/ppermute | solution.py:28
  40.4 2.7 %collective-permute-start.11 = (bf16[2,32,1024]{2,1,0:T(8,128)(2,1)S(1)}, bf16[2,32,1024]{2,1,0:T(8,128)(2,1)S(1)}, u32[]{:S(2)}, u32[]{:S(2)}) collective-permute-start(bf16[2,32,1024]{2,1,0:T(8,128)(2,1)S(1)} %get-tuple-element.65), channel_id=1, source_target_pairs={{0,12},{4,0},{8,4},{12,8},{1,13},{5,1},{9,5},{13,9},{2,14},{6,2},{... | collective-permute-start | bytes 393224 | tf_op jit(solution)/shard_map/ppermute | solution.py:28
  45.0 3.0 %collective-permute-start.1 = (bf16[2,32,1024]{2,1,0:T(8,128)(2,1)S(1)}, bf16[2,32,1024]{2,1,0:T(8,128)(2,1)S(1)}, u32[]{:S(2)}, u32[]{:S(2)}) collective-permute-start(bf16[2,32,1024]{2,1,0:T(8,128)(2,1)S(1)} %get-tuple-element.62), channel_id=1, source_target_pairs={{0,96},{32,0},{64,32},{96,64},{1,97},{33,1},{65,33},{97,65},{2,98}... | collective-permute-start | bytes 393224 | tf_op jit(solution)/shard_map/ppermute | solution.py:28
  48.8 2.2 collective-permute-done.12
  53.4 2.9 %collective-permute-start.14 = (bf16[8,4,8,1024]{3,2,1,0:T(8,128)(2,1)}, bf16[8,4,8,1024]{3,2,1,0:T(8,128)(2,1)S(1)}, u32[]{:S(2)}, u32[]{:S(2)}) collective-permute-start(bf16[8,4,8,1024]{3,2,1,0:T(8,128)(2,1)} %bitcast.40), channel_id=1, source_target_pairs={{0,96},{32,0},{64,32},{96,64},{1,97},{33,1},{65,33},{97,65},{2,98}... | collective-permute-start | bytes 1572872 | tf_op jit(solution)/shard_map/ppermute | solution.py:28
  57.0 2.9 %collective-permute-start.2 = (bf16[2,32,1024]{2,1,0:T(8,128)(2,1)S(1)}, bf16[2,32,1024]{2,1,0:T(8,128)(2,1)S(1)}, u32[]{:S(2)}, u32[]{:S(2)}) collective-permute-start(bf16[2,32,1024]{2,1,0:T(8,128)(2,1)S(1)} %get-tuple-element.62), channel_id=1, source_target_pairs={{0,64},{32,96},{64,0},{96,32},{1,65},{33,97},{65,1},{97,33},{2,66}... | collective-permute-start | bytes 393224 | tf_op jit(solution)/shard_map/ppermute | solution.py:28
  60.7 15.0 %collective-permute-done.2 = bf16[2,32,1024]{2,1,0:T(8,128)(2,1)S(1)} collective-permute-done((bf16[2,32,1024]{2,1,0:T(8,128)(2,1)S(1)}, bf16[2,32,1024]{2,1,0:T(8,128)(2,1)S(1)}, u32[]{:S(2)}, u32[]{:S(2)}) %collective-permute-start.2) | collective-permute-done | bytes 131104 | tf_op jit(solution)/shard_map/ppermute | solution.py:28
  75.7 8.1 %collective-permute-start.16 = (bf16[8,4,8,1024]{3,2,1,0:T(8,128)(2,1)}, bf16[8,4,8,1024]{3,2,1,0:T(8,128)(2,1)S(1)}, u32[]{:S(2)}, u32[]{:S(2)}) collective-permute-start(bf16[8,4,8,1024]{3,2,1,0:T(8,128)(2,1)} %bitcast.40), channel_id=1, source_target_pairs={{0,32},{32,64},{64,96},{96,0},{1,33},{33,65},{65,97},{97,1},{2,34}... | collective-permute-start | bytes 1572872 | tf_op jit(solution)/shard_map/ppermute | solution.py:28
  86.9 4.4 %fusion.63 = (f32[1,2,4,32,1024]{4,3,2,1,0:T(8,128)}, f32[1,2,4,32,1024]{4,3,2,1,0:T(8,128)}, f32[1,2,4,32,1024]{4,3,2,1,0:T(8,128)}, f32[1,2,4,32,1024]{4,3,2,1,0:T(8,128)}) fusion(f32[4,2,4,64,1024]{4,3,2,1,0:T(8,128)} %bitcast.210), kind=kLoop, calls=%fused_computation.138 | loop fusion | bytes 8388608 | tf_op jit(solution)/shard_map/slice | solution.py:190
  91.3 4.1 %collective-permute-done.16 = bf16[8,4,8,1024]{3,2,1,0:T(8,128)(2,1)S(1)} collective-permute-done((bf16[8,4,8,1024]{3,2,1,0:T(8,128)(2,1)}, bf16[8,4,8,1024]{3,2,1,0:T(8,128)(2,1)S(1)}, u32[]{:S(2)}, u32[]{:S(2)}) %collective-permute-start.16) | collective-permute-done | bytes 524320 | tf_op jit(solution)/shard_map/ppermute | solution.py:28
  95.4 4.4 %collective-permute-done.4 = bf16[8,4,8,1024]{3,2,1,0:T(8,128)(2,1)S(1)} collective-permute-done((bf16[8,4,8,1024]{3,2,1,0:T(8,128)(2,1)}, bf16[8,4,8,1024]{3,2,1,0:T(8,128)(2,1)S(1)}, u32[]{:S(2)}, u32[]{:S(2)}) %collective-permute-start.4) | collective-permute-done | bytes 524320 | tf_op jit(solution)/shard_map/ppermute | solution.py:28
  101.4 9.0 %collective-permute-done.6 = bf16[8,4,8,1024]{3,2,1,0:T(8,128)(2,1)} collective-permute-done((bf16[8,4,8,1024]{3,2,1,0:T(8,128)(2,1)}, bf16[8,4,8,1024]{3,2,1,0:T(8,128)(2,1)}, u32[]{:S(2)}, u32[]{:S(2)}) %collective-permute-start.6) | collective-permute-done | bytes 524320 | tf_op jit(solution)/shard_map/ppermute | solution.py:28
  116.8 2.8 %gather_fusion = f32[64,2048]{1,0:T(8,128)} fusion(f32[64,2048]{1,0:T(8,128)} %bitcast.209, s32[1024]{0:T(1024)S(1)} %pad_clamp_fusion), kind=kCustom, calls=%fused_computation.2 | custom fusion | bytes 1048832 | tf_op jit(solution)/shard_map/jit(_take)/gather | solution.py:215
  122.7 20.8 %shard_map.101 = (bf16[4096,1024]{1,0:T(8,128)(2,1)}, f32[1024,512]{1,0:T(8,128)}, f32[1024,512]{1,0:T(8,128)}) custom-call(s32[5]{0:T(128)S(1)} %stack.75.place, s32[8,1,512]{2,1,0:T(1,128)S(1)} %pad_add_fusion.target, bf16[1024,4096]{1,0:T(8,128)(2,1)} %tokens.3, bf16[4,2,4,8,1024]{4,3,2,1,0:T(8,128)(2,1)S(1)} %pad_maximum_fusion.refs_0_, ...), custom_call_target="tpu_custom_call" | custom-call | flops 12884901888 | bytes 33554432 | tf_op jit(solution)/shard_map/pallas_call | solution.py:120
  143.4 3.0 %collective-permute-start.21 = (f32[1024,512]{1,0:T(8,128)}, f32[1024,512]{1,0:T(8,128)S(1)}, u32[]{:S(2)}, u32[]{:S(2)}) collective-permute-start(f32[1024,512]{1,0:T(8,128)} %get-tuple-element.12), channel_id=1, source_target_pairs={{0,1},{1,0},{2,3},{3,2},{4,5},{5,4},{6,7},{7,6},{8,9},{9,8},{10,11... | collective-permute-start | bytes 6291464 | tf_op jit(solution)/shard_map/ppermute | solution.py:28
  155.5 14.6 %convert_bitcast_fusion = bf16[1024,4096]{0,1:T(8,128)(2,1)} fusion(bf16[4096,1024]{1,0:T(8,128)(2,1)} %get-tuple-element.13, bf16[1024,1024]{1,0:T(8,128)(2,1)S(1)} %copy-done.3), kind=kOutput, calls=%fused_computation.3 | convolution fusion | flops 8594128896 | bytes 18874368 | tf_op jit(solution)/shard_map/dot_general | solution.py:208
  170.1 11.9 %copy.106 = bf16[1024,4096]{1,0:T(8,128)(2,1)} copy(bf16[1024,4096]{0,1:T(8,128)(2,1)} %convert_bitcast_fusion) | data formatting | bytes 16777216
  182.0 3.0 %fusion.21 = (bf16[4,2,32,1024]{3,2,1,0:T(8,128)(2,1)S(1)}, bf16[4,2,32,1024]{3,2,1,0:T(8,128)(2,1)S(1)}, bf16[4,2,32,1024]{3,2,1,0:T(8,128)(2,1)S(1)}) fusion(f32[4,2,4,64,1024]{4,3,2,1,0:T(8,128)} %bitcast.211, bf16[4,2,4,64,1024]{4,3,2,1,0:T(8,128)(2,1)} %bitcast.54), kind=kLoop, calls=%fused_computation.34 | loop fusion | flops 2359296 | bytes 6291456 | tf_op jit(solution)/shard_map/convert_element_type | solution.py:195
  185.1 2.8 %collective-permute-start.30 = (bf16[4,2,32,1024]{3,2,1,0:T(8,128)(2,1)S(1)}, bf16[4,2,32,1024]{3,2,1,0:T(8,128)(2,1)S(1)}, u32[]{:S(2)}, u32[]{:S(2)}) collective-permute-start(bf16[4,2,32,1024]{3,2,1,0:T(8,128)(2,1)S(1)} %get-tuple-element.44), channel_id=1, source_target_pairs={{0,8},{4,12},{8,0},{12,4},{1,9},{5,13},{9,1},{13,5},{2,10},{6,14},... | collective-permute-start | bytes 1572872 | tf_op jit(solution)/shard_map/ppermute | solution.py:28
  191.6 21.1 %collective-permute-done.29 = bf16[4,2,32,1024]{3,2,1,0:T(8,128)(2,1)S(1)} collective-permute-done((bf16[4,2,32,1024]{3,2,1,0:T(8,128)(2,1)S(1)}, bf16[4,2,32,1024]{3,2,1,0:T(8,128)(2,1)S(1)}, u32[]{:S(2)}, u32[]{:S(2)}) %collective-permute-start.29) | collective-permute-done | bytes 524320 | tf_op jit(solution)/shard_map/ppermute | solution.py:28
  219.7 3.0 %collective-permute-done.32 = bf16[2,32,1024]{2,1,0:T(8,128)(2,1)S(1)} collective-permute-done((bf16[2,32,1024]{2,1,0:T(8,128)(2,1)S(1)}, bf16[2,32,1024]{2,1,0:T(8,128)(2,1)S(1)}, u32[]{:S(2)}, u32[]{:S(2)}) %collective-permute-start.32) | collective-permute-done | bytes 131104 | tf_op jit(solution)/shard_map/ppermute | solution.py:28
  225.7 3.6 %collective-permute-done.35 = bf16[64,1024]{1,0:T(8,128)(2,1)S(1)} collective-permute-done((bf16[64,1024]{1,0:T(8,128)(2,1)S(1)}, bf16[64,1024]{1,0:T(8,128)(2,1)S(1)}, u32[]{:S(2)}, u32[]{:S(2)}) %collective-permute-start.35) | collective-permute-done | bytes 131104 | tf_op jit(solution)/shard_map/ppermute | solution.py:28
  (154 shorter events, 52.8 us)
Async XLA Ops:
  17.7 128.7 %collective-permute-start.22 = (bf16[8,4,64,1024]{3,2,1,0:T(8,128)(2,1)}, bf16[8,4,64,1024]{3,2,1,0:T(8,128)(2,1)}, u32[]{:S(2)}, u32[]{:S(2)}) collective-permute-start(bf16[8,4,64,1024]{3,2,1,0:T(8,128)(2,1)} %get-tuple-element.15), channel_id=1, source_target_pairs={{0,2},{2,0},{1,3},{3,1},{4,6},{6,4},{5,7},{7,5},{8,10},{10,8},{9,1... | collective-permute-start | bytes 12582920 | tf_op jit(solution)/shard_map/ppermute | solution.py:28
  18.9 96.0 %all-to-all-start = ((f32[64,1,2048]{2,1,0:T(1,128)}), f32[64,1,2048]{2,1,0:T(1,128)}, u32[]{:S(2)}, u32[]{:S(2)}) async-start(f32[64,1,2048]{2,1,0:T(1,128)} %all_to_all.8), calls=%async_computation | async-start | bytes 1048576 | tf_op jit(solution)/shard_map/all_to_all | solution.py:182
  29.1 10.6 %collective-permute-start = (bf16[64,1024]{1,0:T(8,128)(2,1)S(1)}, bf16[64,1024]{1,0:T(8,128)(2,1)S(1)}, u32[]{:S(2)}, u32[]{:S(2)}) collective-permute-start(bf16[64,1024]{1,0:T(8,128)(2,1)S(1)} %bitcast.227), channel_id=1, source_target_pairs={{0,16},{16,0},{1,17},{17,1},{2,18},{18,2},{3,19},{19,3},{4,20},{20... | collective-permute-start | bytes 393224 | tf_op jit(solution)/shard_map/ppermute | solution.py:28
  45.0 14.9 %collective-permute-start.1 = (bf16[2,32,1024]{2,1,0:T(8,128)(2,1)S(1)}, bf16[2,32,1024]{2,1,0:T(8,128)(2,1)S(1)}, u32[]{:S(2)}, u32[]{:S(2)}) collective-permute-start(bf16[2,32,1024]{2,1,0:T(8,128)(2,1)S(1)} %get-tuple-element.62), channel_id=1, source_target_pairs={{0,96},{32,0},{64,32},{96,64},{1,97},{33,1},{65,33},{97,65},{2,98}... | collective-permute-start | bytes 393224 | tf_op jit(solution)/shard_map/ppermute | solution.py:28
  53.4 31.4 %collective-permute-start.14 = (bf16[8,4,8,1024]{3,2,1,0:T(8,128)(2,1)}, bf16[8,4,8,1024]{3,2,1,0:T(8,128)(2,1)S(1)}, u32[]{:S(2)}, u32[]{:S(2)}) collective-permute-start(bf16[8,4,8,1024]{3,2,1,0:T(8,128)(2,1)} %bitcast.40), channel_id=1, source_target_pairs={{0,96},{32,0},{64,32},{96,64},{1,97},{33,1},{65,33},{97,65},{2,98}... | collective-permute-start | bytes 1572872 | tf_op jit(solution)/shard_map/ppermute | solution.py:28
  56.3 28.7 %collective-permute-start.15 = (bf16[8,4,8,1024]{3,2,1,0:T(8,128)(2,1)}, bf16[8,4,8,1024]{3,2,1,0:T(8,128)(2,1)S(1)}, u32[]{:S(2)}, u32[]{:S(2)}) collective-permute-start(bf16[8,4,8,1024]{3,2,1,0:T(8,128)(2,1)} %bitcast.40), channel_id=1, source_target_pairs={{0,64},{32,96},{64,0},{96,32},{1,65},{33,97},{65,1},{97,33},{2,66}... | collective-permute-start | bytes 1572872 | tf_op jit(solution)/shard_map/ppermute | solution.py:28
  57.0 18.8 %collective-permute-start.2 = (bf16[2,32,1024]{2,1,0:T(8,128)(2,1)S(1)}, bf16[2,32,1024]{2,1,0:T(8,128)(2,1)S(1)}, u32[]{:S(2)}, u32[]{:S(2)}) collective-permute-start(bf16[2,32,1024]{2,1,0:T(8,128)(2,1)S(1)} %get-tuple-element.62), channel_id=1, source_target_pairs={{0,64},{32,96},{64,0},{96,32},{1,65},{33,97},{65,1},{97,33},{2,66}... | collective-permute-start | bytes 393224 | tf_op jit(solution)/shard_map/ppermute | solution.py:28
  59.9 24.0 %collective-permute-start.3 = (bf16[2,32,1024]{2,1,0:T(8,128)(2,1)S(1)}, bf16[2,32,1024]{2,1,0:T(8,128)(2,1)S(1)}, u32[]{:S(2)}, u32[]{:S(2)}) collective-permute-start(bf16[2,32,1024]{2,1,0:T(8,128)(2,1)S(1)} %get-tuple-element.62), channel_id=1, source_target_pairs={{0,32},{32,64},{64,96},{96,0},{1,33},{33,65},{65,97},{97,1},{2,34}... | collective-permute-start | bytes 393224 | tf_op jit(solution)/shard_map/ppermute | solution.py:28
  75.7 19.7 %collective-permute-start.16 = (bf16[8,4,8,1024]{3,2,1,0:T(8,128)(2,1)}, bf16[8,4,8,1024]{3,2,1,0:T(8,128)(2,1)S(1)}, u32[]{:S(2)}, u32[]{:S(2)}) collective-permute-start(bf16[8,4,8,1024]{3,2,1,0:T(8,128)(2,1)} %bitcast.40), channel_id=1, source_target_pairs={{0,32},{32,64},{64,96},{96,0},{1,33},{33,65},{65,97},{97,1},{2,34}... | collective-permute-start | bytes 1572872 | tf_op jit(solution)/shard_map/ppermute | solution.py:28
  84.8 15.1 %collective-permute-start.4 = (bf16[8,4,8,1024]{3,2,1,0:T(8,128)(2,1)}, bf16[8,4,8,1024]{3,2,1,0:T(8,128)(2,1)S(1)}, u32[]{:S(2)}, u32[]{:S(2)}) collective-permute-start(bf16[8,4,8,1024]{3,2,1,0:T(8,128)(2,1)} %bitcast.23), channel_id=1, source_target_pairs={{0,12},{4,0},{8,4},{12,8},{1,13},{5,1},{9,5},{13,9},{2,14},{6,2},{... | collective-permute-start | bytes 1572872 | tf_op jit(solution)/shard_map/ppermute | solution.py:28
  84.8 16.6 %collective-permute-start.5 = (bf16[8,4,8,1024]{3,2,1,0:T(8,128)(2,1)}, bf16[8,4,8,1024]{3,2,1,0:T(8,128)(2,1)S(1)}, u32[]{:S(2)}, u32[]{:S(2)}) collective-permute-start(bf16[8,4,8,1024]{3,2,1,0:T(8,128)(2,1)} %bitcast.23), channel_id=1, source_target_pairs={{0,8},{4,12},{8,0},{12,4},{1,9},{5,13},{9,1},{13,5},{2,10},{6,14},... | collective-permute-start | bytes 1572872 | tf_op jit(solution)/shard_map/ppermute | solution.py:28
  85.0 25.4 %collective-permute-start.6 = (bf16[8,4,8,1024]{3,2,1,0:T(8,128)(2,1)}, bf16[8,4,8,1024]{3,2,1,0:T(8,128)(2,1)}, u32[]{:S(2)}, u32[]{:S(2)}) collective-permute-start(bf16[8,4,8,1024]{3,2,1,0:T(8,128)(2,1)} %bitcast.23), channel_id=1, source_target_pairs={{0,4},{4,8},{8,12},{12,0},{1,5},{5,9},{9,13},{13,1},{2,6},{6,10},{... | collective-permute-start | bytes 1572872 | tf_op jit(solution)/shard_map/ppermute | solution.py:28
  95.4 16.2 %collective-permute-start.17 = (bf16[8,4,8,1024]{3,2,1,0:T(8,128)(2,1)}, bf16[8,4,8,1024]{3,2,1,0:T(8,128)(2,1)}, u32[]{:S(2)}, u32[]{:S(2)}) collective-permute-start(bf16[8,4,8,1024]{3,2,1,0:T(8,128)(2,1)} %bitcast.40), channel_id=1, source_target_pairs={{0,2},{2,0},{1,3},{3,1},{4,6},{6,4},{5,7},{7,5},{8,10},{10,8},{9,1... | collective-permute-start | bytes 1572872 | tf_op jit(solution)/shard_map/ppermute | solution.py:28
  99.9 12.4 %collective-permute-start.7 = (bf16[8,4,8,1024]{3,2,1,0:T(8,128)(2,1)}, bf16[8,4,8,1024]{3,2,1,0:T(8,128)(2,1)S(1)}, u32[]{:S(2)}, u32[]{:S(2)}) collective-permute-start(bf16[8,4,8,1024]{3,2,1,0:T(8,128)(2,1)} %bitcast.23), channel_id=1, source_target_pairs={{0,2},{2,0},{1,3},{3,1},{4,6},{6,4},{5,7},{7,5},{8,10},{10,8},{9,1... | collective-permute-start | bytes 1572872 | tf_op jit(solution)/shard_map/ppermute | solution.py:28
  101.4 11.6 %collective-permute-start.18 = (bf16[8,4,8,1024]{3,2,1,0:T(8,128)(2,1)S(1)}, bf16[8,4,8,1024]{3,2,1,0:T(8,128)(2,1)}, u32[]{:S(2)}, u32[]{:S(2)}) collective-permute-start(bf16[8,4,8,1024]{3,2,1,0:T(8,128)(2,1)S(1)} %collective-permute-done.14), channel_id=1, source_target_pairs={{0,2},{2,0},{1,3},{3,1},{4,6},{6,4},{5,7},{7,5},{8,10},{10,8},{9,1... | collective-permute-start | bytes 1572872 | tf_op jit(solution)/shard_map/ppermute | solution.py:28
  111.7 9.9 %collective-permute-start.20 = (bf16[8,4,8,1024]{3,2,1,0:T(8,128)(2,1)}, bf16[8,4,8,1024]{3,2,1,0:T(8,128)(2,1)}, u32[]{:S(2)}, u32[]{:S(2)}) collective-permute-start(bf16[8,4,8,1024]{3,2,1,0:T(8,128)(2,1)} %copy-done.20), channel_id=1, source_target_pairs={{0,2},{2,0},{1,3},{3,1},{4,6},{6,4},{5,7},{7,5},{8,10},{10,8},{9,1... | collective-permute-start | bytes 1572872 | tf_op jit(solution)/shard_map/ppermute | solution.py:28
  143.4 80.9 %collective-permute-start.21 = (f32[1024,512]{1,0:T(8,128)}, f32[1024,512]{1,0:T(8,128)S(1)}, u32[]{:S(2)}, u32[]{:S(2)}) collective-permute-start(f32[1024,512]{1,0:T(8,128)} %get-tuple-element.12), channel_id=1, source_target_pairs={{0,1},{1,0},{2,3},{3,2},{4,5},{5,4},{6,7},{7,6},{8,9},{9,8},{10,11... | collective-permute-start | bytes 6291464 | tf_op jit(solution)/shard_map/ppermute | solution.py:28
  149.2 35.8 %collective-permute-start.23 = (bf16[2,4,32,1024]{3,2,0,1:T(8,128)(2,1)}, bf16[2,4,32,1024]{3,2,0,1:T(8,128)(2,1)S(1)}, u32[]{:S(2)}, u32[]{:S(2)}) collective-permute-start(bf16[2,4,32,1024]{3,2,0,1:T(8,128)(2,1)} %fusion.18), channel_id=1, source_target_pairs={{0,32},{32,64},{64,96},{96,0},{1,33},{33,65},{65,97},{97,1},{2,34}... | collective-permute-start | bytes 1572872 | tf_op jit(solution)/shard_map/ppermute | solution.py:28
  150.5 37.3 %collective-permute-start.24 = (bf16[2,4,32,1024]{3,2,0,1:T(8,128)(2,1)}, bf16[2,4,32,1024]{3,2,0,1:T(8,128)(2,1)}, u32[]{:S(2)}, u32[]{:S(2)}) collective-permute-start(bf16[2,4,32,1024]{3,2,0,1:T(8,128)(2,1)} %fusion.19), channel_id=1, source_target_pairs={{0,64},{32,96},{64,0},{96,32},{1,65},{33,97},{65,1},{97,33},{2,66}... | collective-permute-start | bytes 1572872 | tf_op jit(solution)/shard_map/ppermute | solution.py:28
  153.6 35.0 %collective-permute-start.25 = (bf16[2,4,32,1024]{3,2,0,1:T(8,128)(2,1)}, bf16[2,4,32,1024]{3,2,0,1:T(8,128)(2,1)}, u32[]{:S(2)}, u32[]{:S(2)}) collective-permute-start(bf16[2,4,32,1024]{3,2,0,1:T(8,128)(2,1)} %fusion.20), channel_id=1, source_target_pairs={{0,96},{32,0},{64,32},{96,64},{1,97},{33,1},{65,33},{97,65},{2,98}... | collective-permute-start | bytes 1572872 | tf_op jit(solution)/shard_map/ppermute | solution.py:28
  185.0 27.8 %collective-permute-start.29 = (bf16[4,2,32,1024]{3,2,1,0:T(8,128)(2,1)S(1)}, bf16[4,2,32,1024]{3,2,1,0:T(8,128)(2,1)S(1)}, u32[]{:S(2)}, u32[]{:S(2)}) collective-permute-start(bf16[4,2,32,1024]{3,2,1,0:T(8,128)(2,1)S(1)} %get-tuple-element.42), channel_id=1, source_target_pairs={{0,4},{4,8},{8,12},{12,0},{1,5},{5,9},{9,13},{13,1},{2,6},{6,10},{... | collective-permute-start | bytes 1572872 | tf_op jit(solution)/shard_map/ppermute | solution.py:28
  185.1 27.7 %collective-permute-start.30 = (bf16[4,2,32,1024]{3,2,1,0:T(8,128)(2,1)S(1)}, bf16[4,2,32,1024]{3,2,1,0:T(8,128)(2,1)S(1)}, u32[]{:S(2)}, u32[]{:S(2)}) collective-permute-start(bf16[4,2,32,1024]{3,2,1,0:T(8,128)(2,1)S(1)} %get-tuple-element.44), channel_id=1, source_target_pairs={{0,8},{4,12},{8,0},{12,4},{1,9},{5,13},{9,1},{13,5},{2,10},{6,14},... | collective-permute-start | bytes 1572872 | tf_op jit(solution)/shard_map/ppermute | solution.py:28
  187.8 25.4 %collective-permute-start.31 = (bf16[4,2,32,1024]{3,2,1,0:T(8,128)(2,1)S(1)}, bf16[4,2,32,1024]{3,2,1,0:T(8,128)(2,1)S(1)}, u32[]{:S(2)}, u32[]{:S(2)}) collective-permute-start(bf16[4,2,32,1024]{3,2,1,0:T(8,128)(2,1)S(1)} %get-tuple-element.43), channel_id=1, source_target_pairs={{0,12},{4,0},{8,4},{12,8},{1,13},{5,1},{9,5},{13,9},{2,14},{6,2},{... | collective-permute-start | bytes 1572872 | tf_op jit(solution)/shard_map/ppermute | solution.py:28
  190.3 25.0 %collective-permute-start.26 = (bf16[2,32,1024]{2,1,0:T(8,128)(2,1)S(1)}, bf16[2,32,1024]{2,1,0:T(8,128)(2,1)S(1)}, u32[]{:S(2)}, u32[]{:S(2)}) collective-permute-start(bf16[2,32,1024]{2,1,0:T(8,128)(2,1)S(1)} %get-tuple-element.55), channel_id=1, source_target_pairs={{0,4},{4,8},{8,12},{12,0},{1,5},{5,9},{9,13},{13,1},{2,6},{6,10},{... | collective-permute-start | bytes 393224 | tf_op jit(solution)/shard_map/ppermute | solution.py:28
  (34 other events, 429.8 us)

commit v2 on v0

v2 whole, which is shorter than its diff:
```python
import functools
import math

import jax
import jax.numpy as jnp
from jax import lax
from jax.experimental import pallas as pl
from jax.experimental.pallas import tpu as pltpu
from jax.sharding import Mesh, PartitionSpec as P

beta_first = 0.9
beta_second = 0.95
learn_rate = 0.001
decay_rate = 0.1
epsilon = 1e-08
bias_first = 1.0 - math.exp(100.0 * math.log(beta_first))
bias_second = 1.0 - math.exp(100.0 * math.log(beta_second))

AXES = ("z", "l", "x", "c", "t")
SIZES = (4, 2, 4, 2, 2)
DP = AXES[:4]
NZ, NL, NX, NC, NT = SIZES
COUNT = NZ * NL * NX * NC
NG = 2
SLOT = 64
MIB = 1 << 20


def shift(value, axis, step):
    size = SIZES[AXES.index(axis)]
    return lax.ppermute(value, axis, [(i, (i + step) % size) for i in range(size)])


def cross(value, stage, step):
    pairs = []
    for z in range(NZ):
        for x in range(NX):
            for c in range(NC):
                to = ((z + step) % NZ, x) if c == stage else (z, (x + step) % NX)
                pairs.append(((z * NX + x) * NC + c, (to[0] * NX + to[1]) * NC + c))
    return lax.ppermute(value, ("z", "x", "c"), pairs)


def gathered(value, stage):
    return [value] + [cross(value, stage, -k) for k in (1, 2, 3)]


def reduced(terms, stage):
    total = terms[0]
    for k in (1, 2, 3):
        total = total + cross(terms[k], stage, k).astype(jnp.float32)
    return total


def after(value, *others):
    return lax.optimization_barrier((value, *others))[0]


def select_kernel(place, tokens, mine, other):
    z, l, x, c = place[0], place[1], place[2], place[3]
    lanes = NC * SLOT
    below = lax.broadcasted_iota(jnp.int32, (tokens.shape[0], lanes), 1) < SLOT

    def column(core, slot):
        first, pair, second = slot // (NL * 4), slot // 4 % NL, slot % 4
        to_z = lax.rem(z + jnp.where(core == 0, first, second), NZ)
        to_x = lax.rem(x + jnp.where(core == 0, second, first), NX)
        at = (to_z * NL + lax.rem(l + pair, NL)) * NX + to_x
        return tokens[:, pl.ds(pl.multiple_of(at * lanes, lanes), lanes)]

    for core, out in ((c, mine), (1 - c, other)):
        for slot in range(0, COUNT // NC, NC):
            one = pltpu.roll(column(core, slot), SLOT * core, 1)
            two = pltpu.roll(column(core, slot + 1), SLOT * (1 - core), 1)
            out[:, slot * SLOT : (slot + 2) * SLOT] = jnp.where(below, one, two)


def selected(place, tokens):
    rows, half = tokens.shape
    block = 128
    out = jax.ShapeDtypeStruct((rows, half // NC), tokens.dtype)
    spec = pl.BlockSpec((block, half // NC), lambda k, place: (k, 0))
    return pl.pallas_call(
        select_kernel,
        grid_spec=pltpu.PrefetchScalarGridSpec(
            num_scalar_prefetch=1,
            grid=(rows // block,),
            in_specs=[pl.BlockSpec((block, half), lambda k, place: (k, 0))],
            out_specs=[spec, spec],
        ),
        out_shape=[out, out],
        compiler_params=pltpu.CompilerParams(vmem_limit_bytes=10 * MIB),
        cost_estimate=pl.CostEstimate(flops=0, bytes_accessed=4 * rows * half, transcendentals=0),
    )(place, tokens)


def grad_kernel(mine, theirs, cotangent, cotangent_theirs, own, *sends):
    term = lax.dot_general(
        mine[...], cotangent[...], (((0,), (0,)), ((), ())), preferred_element_type=jnp.float32
    )
    term += lax.dot_general(
        theirs[...], cotangent_theirs[...], (((0,), (0,)), ((), ())), preferred_element_type=jnp.float32
    )
    term = term.reshape(own.shape)
    k = pl.program_id(0)

    @pl.when(k == 0)
    def _():
        own[...] = term

    for at, send in enumerate(sends):

        @pl.when(k == at + 1)
        def _():
            send[...] = term.astype(send.dtype)


def chip_grad(mine, theirs, cotangent, cotangent_theirs):
    rows, half = mine.shape
    width = cotangent.shape[1]
    piece = (half // 4 // SLOT, SLOT, width)
    part = pl.BlockSpec((rows, half // 4), lambda k: (0, k))
    whole = pl.BlockSpec((rows, width), lambda k: (0, 0))
    return pl.pallas_call(
        grad_kernel,
        grid=(4,),
        in_specs=[part, part, whole, whole],
        out_specs=[pl.BlockSpec(piece, lambda k: (0, 0, 0))] * 4,
        out_shape=[jax.ShapeDtypeStruct(piece, jnp.bfloat16 if n else jnp.float32) for n in range(4)],
        compiler_params=pltpu.CompilerParams(vmem_limit_bytes=30 * MIB),
        cost_estimate=pl.CostEstimate(
            flops=rows * half * width // 2, bytes_accessed=(rows * half + half * width), transcendentals=0
        ),
    )(mine, theirs, cotangent, cotangent_theirs)


def reorder_kernel(place, target, tokens, *refs):
    pieces, (full, keys_send, held) = refs[:-3], refs[-3:]
    t = place[4]
    block, width = full.shape
    for group in range(NG):
        size = block // NG
        each = pieces[0].shape[0] // NG
        rows = jnp.concatenate(
            [p[group * each : (group + 1) * each].reshape(-1, width) for p in pieces], axis=0
        )
        pick = lax.broadcasted_iota(jnp.int32, (size, rows.shape[0]), 0) == target[group]
        pick = jnp.where(pick, 1.0, 0.0).astype(jnp.bfloat16)
        moved = jnp.dot(pick, rows, preferred_element_type=jnp.float32).astype(jnp.bfloat16)
        at = pl.ds(group * size, size)
        full[at, :] = moved
        for h in range(NT):
            held[h, at, :] = moved[:, h * (width // NT) : (h + 1) * (width // NT)]

    @pl.when(pl.program_id(0) == 0)
    def _():
        keys_send[...] = jnp.zeros_like(keys_send)

    keys_send[...] += jnp.dot(tokens[...], held[1 - t], preferred_element_type=jnp.float32)


def reorder_and_send(place, target, tokens, pieces):
    rows, half = tokens.shape
    width = pieces[0].shape[-1]
    octets = target.shape[0] // NG
    block = half // octets
    lines, line, _ = pieces[0].shape
    piece = pl.BlockSpec((lines // octets, line, width), lambda o, place: (o, 0, 0))
    return pl.pallas_call(
        reorder_kernel,
        grid_spec=pltpu.PrefetchScalarGridSpec(
            num_scalar_prefetch=1,
            grid=(octets,),
            in_specs=[
                pl.BlockSpec((NG, 1, block // NG), lambda o, place: (o, 0, 0)),
                pl.BlockSpec((rows, block), lambda o, place: (0, o)),
            ]
            + [piece] * len(pieces),
            out_specs=[
                pl.BlockSpec((block, width), lambda o, place: (o, 0)),
                pl.BlockSpec((rows, width // NT), lambda o, place: (0, 0)),
            ],
            scratch_shapes=[pltpu.VMEM((NT, block, width // NT), jnp.bfloat16)],
        ),
        out_shape=[
            jax.ShapeDtypeStruct((half, width), jnp.bfloat16),
            jax.ShapeDtypeStruct((rows, width // NT), jnp.float32),
        ],
        compiler_params=pltpu.CompilerParams(vmem_limit_bytes=22 * MIB),
        cost_estimate=pl.CostEstimate(
            flops=2 * rows * half * width, bytes_accessed=rows * half * 2 + half * width * 4, transcendentals=0
        ),
    )(place, target, tokens, *pieces)


def keep_kernel(place, tokens, full, keys):
    @pl.when(pl.program_id(0) == 0)
    def _():
        keys[...] = jnp.zeros_like(keys)

    keys[...] += jnp.dot(tokens[...], full[...], preferred_element_type=jnp.float32)


def keys_kept(place, tokens, full):
    rows, half = tokens.shape
    width = full.shape[1]
    block = 512
    return pl.pallas_call(
        keep_kernel,
        grid_spec=pltpu.PrefetchScalarGridSpec(
            num_scalar_prefetch=1,
            grid=(half // block,),
            in_specs=[
                pl.BlockSpec((rows, block), lambda o, place: (0, o)),
                pl.BlockSpec((block, width // NT), lambda o, place: (o, place[4])),
            ],
            out_specs=pl.BlockSpec((rows, width // NT), lambda o, place: (0, 0)),
        ),
        out_shape=jax.ShapeDtypeStruct((rows, width // NT), jnp.float32),
        compiler_params=pltpu.CompilerParams(vmem_limit_bytes=14 * MIB),
        cost_estimate=pl.CostEstimate(
            flops=0, bytes_accessed=0, transcendentals=0
        ),
    )(place, tokens, full)


def back_kernel(cotangent, full, *refs):
    out = refs[-1]
    out[...] = lax.dot_general(
        cotangent[...], full[...], (((1,), (1,)), ((), ())), preferred_element_type=jnp.float32
    ).astype(out.dtype)


def back_part(cotangent, full, first, last, held):
    rows, width = cotangent.shape
    half = full.shape[0]
    block = 512
    return pl.pallas_call(
        back_kernel,
        grid=(last - first,),
        in_specs=[
            pl.BlockSpec((rows, width), lambda o: (0, 0)),
            pl.BlockSpec((block, width), lambda o: (o + first, 0)),
        ]
        + [pl.BlockSpec(memory_space=pl.ANY)] * len(held),
        out_specs=pl.BlockSpec((rows, block), lambda o: (0, o + first)),
        out_shape=jax.ShapeDtypeStruct((rows, half), jnp.bfloat16),
        input_output_aliases={2: 0} if held else {},
        compiler_params=pltpu.CompilerParams(vmem_limit_bytes=14 * MIB),
        cost_estimate=pl.CostEstimate(
            flops=0, bytes_accessed=0, transcendentals=0
        ),
    )(cotangent, full, *held)


def pack_kernel(first, second, out):
    for n, moment in enumerate((first, second)):
        for k in range(8):
            out[:, n * 8 + k, :] = moment[:, k * 128 : (k + 1) * 128]


def packed(first, second):
    rows, width = first.shape
    return pl.pallas_call(
        pack_kernel,
        out_shape=jax.ShapeDtypeStruct((rows, 16, width // 8), jnp.float32),
        compiler_params=pltpu.CompilerParams(vmem_limit_bytes=4 * MIB),
        cost_estimate=pl.CostEstimate(flops=0, bytes_accessed=4 * MIB // 4, transcendentals=0),
    )(first, second)


def update_kernel(scale, me, source, moments, own, came, full, weight, first, second, held):
    rows = held.shape[0]

    def move(p, carry):
        held[p] = moments[source[p]]
        return carry

    lax.fori_loop(0, rows, move, 0, unroll=8)
    for k in range(8):
        at = slice(k * 128, (k + 1) * 128)
        grad = (own[:, at] + came[:, at].astype(jnp.float32)) * scale
        base = full[:, at].astype(jnp.float32)
        new_first = beta_first * held[:, k, :] + (1.0 - beta_first) * grad
        new_second = beta_second * held[:, 8 + k, :] + (1.0 - beta_second) * grad * grad
        step = new_first / bias_first / (jnp.sqrt(new_second / bias_second) + epsilon)
        weight[:, at] = (base - learn_rate * (step + decay_rate * base)).astype(weight.dtype)
        first[:, at] = new_first
        second[:, at] = new_second


def updated(me, source, moments, own, came, full, scale):
    rows, width = own.shape
    whole = pl.BlockSpec((rows, width), lambda i, me, source: (0, 0))
    return pl.pallas_call(
        functools.partial(update_kernel, scale),
        grid_spec=pltpu.PrefetchScalarGridSpec(
            num_scalar_prefetch=2,
            grid=(1,),
            in_specs=[
                pl.BlockSpec(moments.shape, lambda i, me, source: (0, 0, 0)),
                whole,
                whole,
                pl.BlockSpec((rows, width), lambda i, me, source: (me[0], 0)),
            ],
            out_specs=[whole] * 3,
            scratch_shapes=[pltpu.VMEM(moments.shape, jnp.float32)],
        ),
        out_shape=[jax.ShapeDtypeStruct((rows, width), k) for k in (jnp.bfloat16, jnp.float32, jnp.float32)],
        compiler_params=pltpu.CompilerParams(vmem_limit_bytes=8 * MIB),
        cost_estimate=pl.CostEstimate(flops=0, bytes_accessed=MIB, transcendentals=0),
    )(me, source, moments, own, came, full)


def targets(landing, place, rows):
    z, l, x, c = place[0], place[1], place[2], place[3]
    steps = jnp.arange(4, dtype=jnp.int32)
    zs, xs = (z + steps) % NZ, (x + steps) % NX
    ls = (l + jnp.arange(NL, dtype=jnp.int32)) % NL

    def owners(core):
        along_z = (zs[None, :, None] * NL + ls) * NX + xs[:, None, None]
        along_x = (zs[:, None, None] * NL + ls) * NX + xs[None, :, None]
        return (jnp.where(core == 0, along_z, along_x) * NC + core).reshape(-1)

    order = jnp.concatenate([owners(c), owners(1 - c)])
    groups = 8 * NG
    each = COUNT // groups
    spots = jnp.take(landing, order, axis=0).reshape(COUNT // (4 * NL), 4 * NL, groups, each)
    spots = spots + jnp.arange(each, dtype=jnp.int32) * rows
    return spots.transpose(2, 0, 3, 1).reshape(groups, 1, each * COUNT)


def shards(tokens, cotangent, old_weight, old_first, old_second, landing):
    z, l, x, c, t = [lax.axis_index(a).astype(jnp.int32) for a in AXES]
    place = jnp.stack([z, l, x, c, t])
    me = ((z * NL + l) * NX + x) * NC + c
    rows, width = old_weight.shape[1:]
    scale = 1.0 / math.sqrt(tokens.shape[0] * COUNT)

    own = old_weight.reshape(rows, width)
    pair = jnp.stack([own, shift(own, "l", 1)])
    moments = packed(old_first.reshape(rows, width), old_second.reshape(rows, width))
    target = targets(landing, place, rows)
    pair, moments, target, tokens_1 = lax.optimization_barrier((pair, moments, target, tokens))
    line = jnp.stack(gathered(pair, 0)).reshape(4 * NL, rows, width)
    mine, other = selected(place, tokens_1)
    line, mine, other, cotangent_1, moments = lax.optimization_barrier((line, mine, other, cotangent, moments))
    theirs = shift(other, "c", 1)
    cotangent_theirs = shift(cotangent_1, "c", 1)
    line = line.transpose(1, 0, 2)
    here = gathered(line, 1)
    there = shift(line, "c", 1)
    moments = lax.all_to_all(moments, DP, split_axis=0, concat_axis=0, tiled=True)
    terms = chip_grad(mine, theirs, cotangent, cotangent_theirs)
    here, terms, moments = lax.optimization_barrier((here, terms, moments))
    pieces = here + [there] + [shift(v, "c", 1) for v in here[1:]]

    total = reduced(terms, 0).reshape(NL, 4, rows, width)
    full, keys_send = reorder_and_send(place, target, tokens, pieces)
    keys_came = shift(keys_send, "t", 1)
    keys_keep = keys_kept(place, tokens, full)
    total, keys_keep = lax.optimization_barrier((total, keys_keep))
    terms = [total[:, 0]] + [total[:, k].astype(jnp.bfloat16) for k in (1, 2, 3)]
    terms, full_1 = lax.optimization_barrier((terms, full))
    total = reduced(terms, 1)
    back = back_part(cotangent, full_1, 0, 8, ())
    total, back = lax.optimization_barrier((total, back))
    came = shift(total[1].astype(jnp.bfloat16), "l", 1)

    column = lax.dynamic_slice_in_dim(landing, me, 1, 1)[:, 0]
    lanes = jnp.arange(COUNT, dtype=jnp.int32)
    source = jnp.sum(jnp.where(column[None, :] == lanes[:, None], lanes[None, :], 0), axis=1, dtype=jnp.int32)
    new_weight, new_first, new_second = updated(me[None], source, moments, total[0], came, full, scale)
    keys = (keys_keep + keys_came).astype(jnp.bfloat16)
    return (keys, back, new_weight[None], new_first[None], new_second[None])


def solution(mesh):
    fine = Mesh(mesh.devices.reshape(SIZES), AXES)
    in_specs = (
        P(DP, "t"),
        P(DP, None),
        P("t", DP, None),
        P("t", DP, None),
        P("t", DP, None),
        P(),
    )
    out_specs = (
        P(DP, "t"),
        P(DP, "t"),
        P("t", DP, None),
        P("t", DP, None),
        P("t", DP, None),
    )
    return jax.shard_map(shards, mesh=fine, in_specs=in_specs, out_specs=out_specs, check_vma=False)
```

time: 534 us -> 147 us (0.28)
  waiting for transfers between devices: 428 us -> 22.2 us
  Pallas kernels: 0 us -> 54.4 us
  matrix products: 44.2 us -> 0 us
  between operations: 13.9 us -> 0.96 us
  starting transfers between devices: 20.1 us -> 32.4 us
  local copies, waits for them, and re-layouts: 20.5 us -> 26.7 us
    reduce_scatter x2 -> x0, waiting for transfers between devices: 294 us -> none  [the longest x1 264 us: shards(): lax.psum_scatter(lax.dot_general(picked, cotangent, (((0,), (0,)), ((), (...]
    all_gather x1 -> x0, waiting for transfers between devices: 108 us -> none  [shards(): lax.all_gather(own, 'dp', axis=0, tiled=True)]
    pallas_call x0 -> x7, Pallas kernels: none -> 54.4 us  [the longest x1 13.5 us: reorder_and_send(): pl.pallas_call(reorder_kernel, grid_spec=pltpu.PrefetchScalarGridSpec(num...]
    dot_general x3 -> x0, matrix products: 44.2 us -> none  [the longest x1 15.1 us: shards(): jnp.dot(picked, lax.all_gather(own, 'dp', axis=0, tiled=True), preferred_...]
    ppermute x0 -> x21, starting transfers between devices: none -> 27.8 us  [the longest x12 22 us: cross(): return lax.ppermute(value, ('z', 'x', 'c'), pairs)]
    all_to_all x3 -> x1, waiting for transfers between devices: 25.7 us -> 6.1 us  [shards(): lax.all_to_all(moments, DP, split_axis=0, concat_axis=0, tiled=True)]
    ppermute x0 -> x21, waiting for transfers between devices: none -> 16.1 us  [the longest x9 16.1 us: shift(): lax.ppermute(value, axis, [(i, (i + step) % size) for i in range(size)])]
    all_to_all x3 -> x1, starting transfers between devices: 19.8 us -> 4.63 us  [shards(): lax.all_to_all(moments, DP, split_axis=0, concat_axis=0, tiled=True)]
  transfers between devices with their start and end apart: 6 -> 22, of which waited for: 6 -> 2; matrix products, arithmetic and copies ran while one was open for 6% -> 6% of each run, Pallas kernels for 0% -> 38%
where the time goes in v2:
time: 147 us; the launch traced here: 145 us
  Pallas kernels  54.4 us (37%)
  starting transfers between devices  32.4 us (22%)
  local copies, waits for them, and re-layouts  26.7 us (18%)
  waiting for transfers between devices  22.2 us (15%)
  other arithmetic  8.2 us (6%)
    unnamed x45, local copies, waits for them, and re-layouts  22.3 us
    ppermute x12, starting transfers between devices, cross(): return lax.ppermute(value, ('z', 'x', 'c'), pairs)  22 us
    ppermute x9, waiting for transfers between devices, shift(): lax.ppermute(value, axis, [(i, (i + step) % size) for i in range(size)])  16.1 us
    pallas_call x1, Pallas kernels, reorder_and_send(): pl.pallas_call(reorder_kernel, grid_spec=pltpu.PrefetchScalarGridSpec(num...  13.5 us
    pallas_call x1, Pallas kernels, chip_grad(): pl.pallas_call(grad_kernel, grid=(4,), in_specs=[part, part, whole, whole...  12.1 us
    pallas_call x1, Pallas kernels, back_part(): pl.pallas_call(back_kernel, grid=(last - first,), in_specs=[pl.BlockSpec(...  11.3 us
    pallas_call x1, Pallas kernels, keys_kept(): pl.pallas_call(keep_kernel, grid_spec=pltpu.PrefetchScalarGridSpec(num_sc...  7.39 us
    pallas_call x1, Pallas kernels, selected(): pl.pallas_call(select_kernel, grid_spec=pltpu.PrefetchScalarGridSpec(num_...  6.91 us
  transfers between devices with their start and end apart: 22, of which 2 were waited for; matrix products, arithmetic and copies ran while one was open for 6% of the time, Pallas kernels for 38%

profile of v2, /device:TPU:0, one launch (start us, length us, event | category | flops | bytes accessed | tf_op | source)
XLA Modules:
  0.0 144.8 jit_solution(17521317583976028079)
XLA Ops:
  0.7 1.7 %collective-permute-start = (bf16[64,1024]{1,0:T(8,128)(2,1)}, bf16[64,1024]{1,0:T(8,128)(2,1)S(1)}, u32[]{:S(2)}, u32[]{:S(2)}) collective-permute-start(bf16[64,1024]{1,0:T(8,128)(2,1)} %bitcast.50), channel_id=1, source_target_pairs={{0,16},{16,0},{1,17},{17,1},{2,18},{18,2},{3,19},{19,3},{4,20},{20... | collective-permute-start | bytes 393224 | tf_op jit(solution)/shard_map/ppermute | solution.py:31
  7.6 2.0 %collective-permute-start.3 = (bf16[2,64,1024]{2,1,0:T(8,128)(2,1)S(1)}, bf16[2,64,1024]{2,1,0:T(8,128)(2,1)S(1)}, u32[]{:S(2)}, u32[]{:S(2)}) collective-permute-start(bf16[2,64,1024]{2,1,0:T(8,128)(2,1)S(1)} %pad_maximum_fusion.1), channel_id=1, source_target_pairs={{0,32},{2,6},{4,36},{6,10},{8,40},{10,14},{12,44},{14,2},{32,64},{... | collective-permute-start | bytes 786440 | tf_op jit(solution)/shard_map/ppermute | solution.py:41
  9.6 3.6 %collective-permute-start.2 = (bf16[2,64,1024]{2,1,0:T(8,128)(2,1)S(1)}, bf16[2,64,1024]{2,1,0:T(8,128)(2,1)S(1)}, u32[]{:S(2)}, u32[]{:S(2)}) collective-permute-start(bf16[2,64,1024]{2,1,0:T(8,128)(2,1)S(1)} %pad_maximum_fusion.1), channel_id=1, source_target_pairs={{0,64},{2,10},{4,68},{6,14},{8,72},{10,2},{12,76},{14,6},{32,96},{... | collective-permute-start | bytes 786440 | tf_op jit(solution)/shard_map/ppermute | solution.py:41
  14.3 3.4 %copy-done.4 = bf16[1024,4096]{1,0:T(8,128)(2,1)S(1)} copy-done((bf16[1024,4096]{1,0:T(8,128)(2,1)S(1)}, bf16[1024,4096]{1,0:T(8,128)(2,1)}, u32[]{:S(2)}) %copy-start.4) | copy-done | bytes 8388632
  17.7 6.9 %shard_map.102 = (bf16[1024,2048]{1,0:T(8,128)(2,1)S(1)}, bf16[1024,2048]{1,0:T(8,128)(2,1)}) custom-call(s32[5]{0:T(128)S(1)} %stack.51.place, bf16[1024,4096]{1,0:T(8,128)(2,1)S(1)} %copy-done.4), custom_call_target="tpu_custom_call" | custom-call | bytes 16777216 | tf_op jit(solution)/shard_map/pallas_call | solution.py:83
  24.7 1.5 %copy.31 = bf16[8,64,1024]{2,0,1:T(8,128)(2,1)} copy(bf16[8,64,1024]{2,1,0:T(8,128)(2,1)S(1)} %bitcast.44) | data formatting | bytes 2097152 | tf_op jit(solution)/shard_map/reshape | solution.py:346
  29.3 2.7 %collective-permute-start.5 = (bf16[64,8,1024]{2,1,0:T(8,128)(2,1)}, bf16[64,8,1024]{2,1,0:T(8,128)(2,1)}, u32[]{:S(2)}, u32[]{:S(2)}) collective-permute-start(bf16[64,8,1024]{2,1,0:T(8,128)(2,1)} %bitcast.18.refs_0_), channel_id=1, source_target_pairs={{0,8},{2,66},{4,12},{6,70},{8,0},{10,74},{12,4},{14,78},{32,40},{3... | collective-permute-start | bytes 3145736 | tf_op jit(solution)/shard_map/ppermute | solution.py:41
  33.4 4.6 %all-to-all-start = ((f32[64,16,128]{2,1,0:T(8,128)}), f32[64,16,128]{2,1,0:T(8,128)S(1)}, u32[]{:S(2)}, u32[]{:S(2)}) async-start(f32[64,16,128]{2,1,0:T(8,128)} %shard_map.101), calls=%async_computation | async-start | bytes 1048576 | tf_op jit(solution)/shard_map/all_to_all | solution.py:354
  38.2 2.2 %copy-done.11 = bf16[1024,2048]{1,0:T(8,128)(2,1)S(1)} copy-done((bf16[1024,2048]{1,0:T(8,128)(2,1)S(1)}, bf16[1024,2048]{1,0:T(8,128)(2,1)}, u32[]{:S(2)}) %copy-start.11) | copy-done | bytes 4194328
  40.4 12.1 %shard_map.103 = (f32[8,64,1024]{2,1,0:T(8,128)S(1)}, bf16[8,64,1024]{2,1,0:T(8,128)(2,1)S(1)}, bf16[8,64,1024]{2,1,0:T(8,128)(2,1)S(1)}, bf16[8,64,1024]{2,1,0:T(8,128)(2,1)S(1)}) custom-call(bf16[1024,2048]{1,0:T(8,128)(2,1)S(1)} %copy-done.11, bf16[1024,2048]{1,0:T(8,128)(2,1)} %collective-permute-done.7.theirs, bf16[1024,1024]{1,0:T(8,128)(2,1)S(1)} %copy-done.7, ...), custom_call_target="tpu_custom_call" | custom-call | flops 1073741824 | bytes 4194304 | tf_op jit(solution)/shard_map/pallas_call | solution.py:124
  56.8 6.1 %all-to-all-done.moments = f32[64,16,128]{2,1,0:T(8,128)S(1)} async-done(((f32[64,16,128]{2,1,0:T(8,128)}), f32[64,16,128]{2,1,0:T(8,128)S(1)}, u32[]{:S(2)}, u32[]{:S(2)}) %all-to-all-start) | async-done | bytes 524320 | tf_op jit(solution)/shard_map/all_to_all | solution.py:354
  64.3 2.4 %collective-permute-start.10 = (bf16[8,64,1024]{2,1,0:T(8,128)(2,1)}, bf16[8,64,1024]{2,1,0:T(8,128)(2,1)}, u32[]{:S(2)}, u32[]{:S(2)}) collective-permute-start(bf16[8,64,1024]{2,1,0:T(8,128)(2,1)} %copy-done.17), channel_id=1, source_target_pairs={{0,64},{2,10},{4,68},{6,14},{8,72},{10,2},{12,76},{14,6},{32,96},{... | collective-permute-start | bytes 3145736 | tf_op jit(solution)/shard_map/ppermute | solution.py:41
  69.2 3.4 %copy-done.5 = bf16[1024,4096]{1,0:T(8,128)(2,1)S(1)} copy-done((bf16[1024,4096]{1,0:T(8,128)(2,1)S(1)}, bf16[1024,4096]{1,0:T(8,128)(2,1)}, u32[]{:S(2)}) %copy-start.5) | copy-done | bytes 8388632
  73.8 13.5 %shard_map.104 = (bf16[4096,1024]{1,0:T(8,128)(2,1)S(1)}, f32[1024,512]{1,0:T(8,128)}) custom-call(s32[5]{0:T(128)S(1)} %stack.51.place, s32[16,1,256]{2,1,0:T(1,128)S(1)} %copy.28.target, bf16[1024,4096]{1,0:T(8,128)(2,1)S(1)} %copy-done.5, bf16[64,8,1024]{2,1,0:T(8,128)(2,1)} %bitcast.18.refs_0_, bf16[64,8,1024]{2,1,0:T(8,128)(2,1)} %collective-permute-done.4.refs_1_, ...), custom_call_target="tpu_custom_call" | custom-call | flops 8589934592 | bytes 25165824 | tf_op jit(solution)/shard_map/pallas_call | solution.py:169
  87.3 3.0 %collective-permute-start.16 = (f32[1024,512]{1,0:T(8,128)}, f32[1024,512]{1,0:T(8,128)}, u32[]{:S(2)}, u32[]{:S(2)}) collective-permute-start(f32[1024,512]{1,0:T(8,128)} %get-tuple-element.68), channel_id=1, source_target_pairs={{0,1},{1,0},{2,3},{3,2},{4,5},{5,4},{6,7},{7,6},{8,9},{9,8},{10,11... | collective-permute-start | bytes 6291464 | tf_op jit(solution)/shard_map/ppermute | solution.py:31
  90.3 7.4 %shard_map.105 = f32[1024,512]{1,0:T(8,128)S(1)} custom-call(s32[5]{0:T(128)S(1)} %stack.51.place, bf16[1024,4096]{1,0:T(8,128)(2,1)S(1)} %copy-done.6, bf16[4096,1024]{1,0:T(8,128)(2,1)S(1)} %get-tuple-element.74.full), custom_call_target="tpu_custom_call" | custom-call | tf_op jit(solution)/shard_map/pallas_call | solution.py:208
  97.8 3.3 %convert_add_fusion = f32[8,64,1024]{2,1,0:T(8,128)S(1)} fusion(bf16[8,64,1024]{2,1,0:T(8,128)(2,1)} %collective-permute-done.11, bf16[8,64,1024]{2,1,0:T(8,128)(2,1)} %collective-permute-done.10, f32[8,64,1024]{2,1,0:T(8,128)S(1)} %copy-done.13, bf16[8,64,1024]{2,1,0:T(8,128)(2,1)} %collective-permute-done.9), kind=kLoop, calls=%fused_computation.2 | loop fusion | flops 3145728 | bytes 7340032 | tf_op jit(solution)/shard_map/add | solution.py:51
  102.0 2.2 %collective-permute-start.17 = (bf16[2,64,1024]{2,1,0:T(8,128)(2,1)}, bf16[2,64,1024]{2,1,0:T(8,128)(2,1)S(1)}, u32[]{:S(2)}, u32[]{:S(2)}) collective-permute-start(bf16[2,64,1024]{2,1,0:T(8,128)(2,1)} %get-tuple-element.71), channel_id=1, source_target_pairs={{0,4},{2,34},{4,8},{6,38},{8,12},{10,42},{12,0},{14,46},{32,36},{3... | collective-permute-start | bytes 786440 | tf_op jit(solution)/shard_map/ppermute | solution.py:41
  104.2 1.8 %collective-permute-start.18 = (bf16[2,64,1024]{2,1,0:T(8,128)(2,1)}, bf16[2,64,1024]{2,1,0:T(8,128)(2,1)}, u32[]{:S(2)}, u32[]{:S(2)}) collective-permute-start(bf16[2,64,1024]{2,1,0:T(8,128)(2,1)} %get-tuple-element.72), channel_id=1, source_target_pairs={{0,8},{2,66},{4,12},{6,70},{8,0},{10,74},{12,4},{14,78},{32,40},{3... | collective-permute-start | bytes 786440 | tf_op jit(solution)/shard_map/ppermute | solution.py:41
  107.6 3.4 %copy-done.2 = bf16[4096,1024]{1,0:T(8,128)(2,1)S(1)} copy-done((bf16[4096,1024]{1,0:T(8,128)(2,1)S(1)}, bf16[4096,1024]{1,0:T(8,128)(2,1)}, u32[]{:S(2)}) %copy-start.2) | copy-done | bytes 8388632
  111.0 11.3 %shard_map.106 = bf16[1024,4096]{1,0:T(8,128)(2,1)} custom-call(bf16[1024,1024]{1,0:T(8,128)(2,1)S(1)} %copy-done.7, bf16[4096,1024]{1,0:T(8,128)(2,1)S(1)} %copy-done.2), custom_call_target="tpu_custom_call" | custom-call | tf_op jit(solution)/shard_map/pallas_call | solution.py:238
  123.8 16.0 %collective-permute-done.20.came = bf16[64,1024]{1,0:T(8,128)(2,1)S(1)} collective-permute-done((bf16[64,1024]{1,0:T(8,128)(2,1)S(1)}, bf16[64,1024]{1,0:T(8,128)(2,1)S(1)}, u32[]{:S(2)}, u32[]{:S(2)}) %collective-permute-start.20) | collective-permute-done | bytes 131104 | tf_op jit(solution)/shard_map/ppermute | solution.py:31
  139.9 2.0 %shard_map.107 = (bf16[64,1024]{1,0:T(8,128)(2,1)}, f32[64,1024]{1,0:T(8,128)}, f32[64,1024]{1,0:T(8,128)}) custom-call(s32[1]{0:T(128)} %bitcast.24.me, s32[64]{0:T(128)S(1)} %select_reduce_fusion.source, f32[64,16,128]{2,1,0:T(8,128)S(1)} %all-to-all-done.moments, f32[64,1024]{1,0:T(8,128)S(1)} %slice_bitcast_fusion.4.own, ...), custom_call_target="tpu_custom_call" | custom-call | bytes 1048576 | tf_op jit(solution)/shard_map/pallas_call | solution.py:295
  141.9 2.9 %add_convert_fusion = bf16[1024,512]{1,0:T(8,128)(2,1)} fusion(f32[1024,512]{1,0:T(8,128)S(1)} %copy-done.9, f32[1024,512]{1,0:T(8,128)} %collective-permute-done.16), kind=kLoop, calls=%fused_computation.1 | loop fusion | flops 1048576 | bytes 5242880 | tf_op jit(solution)/shard_map/convert_element_type | solution.py:375
  (108 shorter events, 24.3 us)
Async XLA Ops:
  0.7 6.9 %collective-permute-start = (bf16[64,1024]{1,0:T(8,128)(2,1)}, bf16[64,1024]{1,0:T(8,128)(2,1)S(1)}, u32[]{:S(2)}, u32[]{:S(2)}) collective-permute-start(bf16[64,1024]{1,0:T(8,128)(2,1)} %bitcast.50), channel_id=1, source_target_pairs={{0,16},{16,0},{1,17},{17,1},{2,18},{18,2},{3,19},{19,3},{4,20},{20... | collective-permute-start | bytes 393224 | tf_op jit(solution)/shard_map/ppermute | solution.py:31
  7.6 17.0 %collective-permute-start.3 = (bf16[2,64,1024]{2,1,0:T(8,128)(2,1)S(1)}, bf16[2,64,1024]{2,1,0:T(8,128)(2,1)S(1)}, u32[]{:S(2)}, u32[]{:S(2)}) collective-permute-start(bf16[2,64,1024]{2,1,0:T(8,128)(2,1)S(1)} %pad_maximum_fusion.1), channel_id=1, source_target_pairs={{0,32},{2,6},{4,36},{6,10},{8,40},{10,14},{12,44},{14,2},{32,64},{... | collective-permute-start | bytes 786440 | tf_op jit(solution)/shard_map/ppermute | solution.py:41
  9.6 15.0 %collective-permute-start.2 = (bf16[2,64,1024]{2,1,0:T(8,128)(2,1)S(1)}, bf16[2,64,1024]{2,1,0:T(8,128)(2,1)S(1)}, u32[]{:S(2)}, u32[]{:S(2)}) collective-permute-start(bf16[2,64,1024]{2,1,0:T(8,128)(2,1)S(1)} %pad_maximum_fusion.1), channel_id=1, source_target_pairs={{0,64},{2,10},{4,68},{6,14},{8,72},{10,2},{12,76},{14,6},{32,96},{... | collective-permute-start | bytes 786440 | tf_op jit(solution)/shard_map/ppermute | solution.py:41
  13.2 11.4 %collective-permute-start.1 = (bf16[2,64,1024]{2,1,0:T(8,128)(2,1)S(1)}, bf16[2,64,1024]{2,1,0:T(8,128)(2,1)S(1)}, u32[]{:S(2)}, u32[]{:S(2)}) collective-permute-start(bf16[2,64,1024]{2,1,0:T(8,128)(2,1)S(1)} %pad_maximum_fusion.1), channel_id=1, source_target_pairs={{0,96},{2,14},{4,100},{6,2},{8,104},{10,6},{12,108},{14,10},{32,0}... | collective-permute-start | bytes 786440 | tf_op jit(solution)/shard_map/ppermute | solution.py:41
  27.1 11.1 %collective-permute-start.7 = (bf16[1024,2048]{1,0:T(8,128)(2,1)}, bf16[1024,2048]{1,0:T(8,128)(2,1)}, u32[]{:S(2)}, u32[]{:S(2)}) collective-permute-start(bf16[1024,2048]{1,0:T(8,128)(2,1)} %get-tuple-element.50), channel_id=1, source_target_pairs={{0,2},{2,0},{1,3},{3,1},{4,6},{6,4},{5,7},{7,5},{8,10},{10,8},{9,1... | collective-permute-start | bytes 12582920 | tf_op jit(solution)/shard_map/ppermute | solution.py:31
  27.7 10.3 %collective-permute-start.8 = (bf16[1024,1024]{1,0:T(8,128)(2,1)S(1)}, bf16[1024,1024]{1,0:T(8,128)(2,1)}, u32[]{:S(2)}, u32[]{:S(2)}) collective-permute-start(bf16[1024,1024]{1,0:T(8,128)(2,1)S(1)} %copy-done.7), channel_id=1, source_target_pairs={{0,2},{2,0},{1,3},{3,1},{4,6},{6,4},{5,7},{7,5},{8,10},{10,8},{9,1... | collective-permute-start | bytes 6291464 | tf_op jit(solution)/shard_map/ppermute | solution.py:31
  27.7 35.1 %collective-permute-start.6 = (bf16[64,8,1024]{2,1,0:T(8,128)(2,1)}, bf16[64,8,1024]{2,1,0:T(8,128)(2,1)}, u32[]{:S(2)}, u32[]{:S(2)}) collective-permute-start(bf16[64,8,1024]{2,1,0:T(8,128)(2,1)} %bitcast.18.refs_0_), channel_id=1, source_target_pairs={{0,4},{2,34},{4,8},{6,38},{8,12},{10,42},{12,0},{14,46},{32,36},{3... | collective-permute-start | bytes 3145736 | tf_op jit(solution)/shard_map/ppermute | solution.py:41
  29.3 33.6 %collective-permute-start.5 = (bf16[64,8,1024]{2,1,0:T(8,128)(2,1)}, bf16[64,8,1024]{2,1,0:T(8,128)(2,1)}, u32[]{:S(2)}, u32[]{:S(2)}) collective-permute-start(bf16[64,8,1024]{2,1,0:T(8,128)(2,1)} %bitcast.18.refs_0_), channel_id=1, source_target_pairs={{0,8},{2,66},{4,12},{6,70},{8,0},{10,74},{12,4},{14,78},{32,40},{3... | collective-permute-start | bytes 3145736 | tf_op jit(solution)/shard_map/ppermute | solution.py:41
  32.0 30.9 %collective-permute-start.4 = (bf16[64,8,1024]{2,1,0:T(8,128)(2,1)}, bf16[64,8,1024]{2,1,0:T(8,128)(2,1)}, u32[]{:S(2)}, u32[]{:S(2)}) collective-permute-start(bf16[64,8,1024]{2,1,0:T(8,128)(2,1)} %bitcast.18.refs_0_), channel_id=1, source_target_pairs={{0,12},{2,98},{4,0},{6,102},{8,4},{10,106},{12,8},{14,110},{32,44}... | collective-permute-start | bytes 3145736 | tf_op jit(solution)/shard_map/ppermute | solution.py:41
  33.4 29.5 %all-to-all-start = ((f32[64,16,128]{2,1,0:T(8,128)}), f32[64,16,128]{2,1,0:T(8,128)S(1)}, u32[]{:S(2)}, u32[]{:S(2)}) async-start(f32[64,16,128]{2,1,0:T(8,128)} %shard_map.101), calls=%async_computation | async-start | bytes 1048576 | tf_op jit(solution)/shard_map/all_to_all | solution.py:354
  38.1 26.3 %collective-permute-start.12 = (bf16[64,8,1024]{2,1,0:T(8,128)(2,1)}, bf16[64,8,1024]{2,1,0:T(8,128)(2,1)}, u32[]{:S(2)}, u32[]{:S(2)}) collective-permute-start(bf16[64,8,1024]{2,1,0:T(8,128)(2,1)} %bitcast.18.refs_0_), channel_id=1, source_target_pairs={{0,2},{2,0},{1,3},{3,1},{4,6},{6,4},{5,7},{7,5},{8,10},{10,8},{9,1... | collective-permute-start | bytes 3145736 | tf_op jit(solution)/shard_map/ppermute | solution.py:31
  62.9 3.8 %collective-permute-start.13 = (bf16[64,8,1024]{2,1,0:T(8,128)(2,1)}, bf16[64,8,1024]{2,1,0:T(8,128)(2,1)S(1)}, u32[]{:S(2)}, u32[]{:S(2)}) collective-permute-start(bf16[64,8,1024]{2,1,0:T(8,128)(2,1)} %collective-permute-done.4.refs_1_), channel_id=1, source_target_pairs={{0,2},{2,0},{1,3},{3,1},{4,6},{6,4},{5,7},{7,5},{8,10},{10,8},{9,1... | collective-permute-start | bytes 3145736 | tf_op jit(solution)/shard_map/ppermute | solution.py:31
  63.0 6.2 %collective-permute-start.14 = (bf16[64,8,1024]{2,1,0:T(8,128)(2,1)}, bf16[64,8,1024]{2,1,0:T(8,128)(2,1)}, u32[]{:S(2)}, u32[]{:S(2)}) collective-permute-start(bf16[64,8,1024]{2,1,0:T(8,128)(2,1)} %collective-permute-done.5.refs_2_), channel_id=1, source_target_pairs={{0,2},{2,0},{1,3},{3,1},{4,6},{6,4},{5,7},{7,5},{8,10},{10,8},{9,1... | collective-permute-start | bytes 3145736 | tf_op jit(solution)/shard_map/ppermute | solution.py:31
  63.5 5.7 %collective-permute-start.15 = (bf16[64,8,1024]{2,1,0:T(8,128)(2,1)}, bf16[64,8,1024]{2,1,0:T(8,128)(2,1)}, u32[]{:S(2)}, u32[]{:S(2)}) collective-permute-start(bf16[64,8,1024]{2,1,0:T(8,128)(2,1)} %collective-permute-done.6.refs_3_), channel_id=1, source_target_pairs={{0,2},{2,0},{1,3},{3,1},{4,6},{6,4},{5,7},{7,5},{8,10},{10,8},{9,1... | collective-permute-start | bytes 3145736 | tf_op jit(solution)/shard_map/ppermute | solution.py:31
  63.6 34.2 %collective-permute-start.9 = (bf16[8,64,1024]{2,1,0:T(8,128)(2,1)}, bf16[8,64,1024]{2,1,0:T(8,128)(2,1)}, u32[]{:S(2)}, u32[]{:S(2)}) collective-permute-start(bf16[8,64,1024]{2,1,0:T(8,128)(2,1)} %copy-done.18), channel_id=1, source_target_pairs={{0,32},{2,6},{4,36},{6,10},{8,40},{10,14},{12,44},{14,2},{32,64},{... | collective-permute-start | bytes 3145736 | tf_op jit(solution)/shard_map/ppermute | solution.py:41
  64.3 33.4 %collective-permute-start.10 = (bf16[8,64,1024]{2,1,0:T(8,128)(2,1)}, bf16[8,64,1024]{2,1,0:T(8,128)(2,1)}, u32[]{:S(2)}, u32[]{:S(2)}) collective-permute-start(bf16[8,64,1024]{2,1,0:T(8,128)(2,1)} %copy-done.17), channel_id=1, source_target_pairs={{0,64},{2,10},{4,68},{6,14},{8,72},{10,2},{12,76},{14,6},{32,96},{... | collective-permute-start | bytes 3145736 | tf_op jit(solution)/shard_map/ppermute | solution.py:41
  67.7 30.1 %collective-permute-start.11 = (bf16[8,64,1024]{2,1,0:T(8,128)(2,1)}, bf16[8,64,1024]{2,1,0:T(8,128)(2,1)}, u32[]{:S(2)}, u32[]{:S(2)}) collective-permute-start(bf16[8,64,1024]{2,1,0:T(8,128)(2,1)} %copy-done.16), channel_id=1, source_target_pairs={{0,96},{2,14},{4,100},{6,2},{8,104},{10,6},{12,108},{14,10},{32,0}... | collective-permute-start | bytes 3145736 | tf_op jit(solution)/shard_map/ppermute | solution.py:41
  73.8 16.5 %copy-start.6 = (bf16[1024,4096]{1,0:T(8,128)(2,1)S(1)}, bf16[1024,4096]{1,0:T(8,128)(2,1)}, u32[]{:S(2)}) copy-start(bf16[1024,4096]{1,0:T(8,128)(2,1)} %tokens.4) | copy-start | bytes 25165828
  87.3 54.6 %collective-permute-start.16 = (f32[1024,512]{1,0:T(8,128)}, f32[1024,512]{1,0:T(8,128)}, u32[]{:S(2)}, u32[]{:S(2)}) collective-permute-start(f32[1024,512]{1,0:T(8,128)} %get-tuple-element.68), channel_id=1, source_target_pairs={{0,1},{1,0},{2,3},{3,2},{4,5},{5,4},{6,7},{7,6},{8,9},{9,8},{10,11... | collective-permute-start | bytes 6291464 | tf_op jit(solution)/shard_map/ppermute | solution.py:31
  102.0 20.3 %collective-permute-start.17 = (bf16[2,64,1024]{2,1,0:T(8,128)(2,1)}, bf16[2,64,1024]{2,1,0:T(8,128)(2,1)S(1)}, u32[]{:S(2)}, u32[]{:S(2)}) collective-permute-start(bf16[2,64,1024]{2,1,0:T(8,128)(2,1)} %get-tuple-element.71), channel_id=1, source_target_pairs={{0,4},{2,34},{4,8},{6,38},{8,12},{10,42},{12,0},{14,46},{32,36},{3... | collective-permute-start | bytes 786440 | tf_op jit(solution)/shard_map/ppermute | solution.py:41
  104.2 18.1 %collective-permute-start.18 = (bf16[2,64,1024]{2,1,0:T(8,128)(2,1)}, bf16[2,64,1024]{2,1,0:T(8,128)(2,1)}, u32[]{:S(2)}, u32[]{:S(2)}) collective-permute-start(bf16[2,64,1024]{2,1,0:T(8,128)(2,1)} %get-tuple-element.72), channel_id=1, source_target_pairs={{0,8},{2,66},{4,12},{6,70},{8,0},{10,74},{12,4},{14,78},{32,40},{3... | collective-permute-start | bytes 786440 | tf_op jit(solution)/shard_map/ppermute | solution.py:41
  106.0 16.3 %collective-permute-start.19 = (bf16[2,64,1024]{2,1,0:T(8,128)(2,1)}, bf16[2,64,1024]{2,1,0:T(8,128)(2,1)}, u32[]{:S(2)}, u32[]{:S(2)}) collective-permute-start(bf16[2,64,1024]{2,1,0:T(8,128)(2,1)} %get-tuple-element.73), channel_id=1, source_target_pairs={{0,12},{2,98},{4,0},{6,102},{8,4},{10,106},{12,8},{14,110},{32,44}... | collective-permute-start | bytes 786440 | tf_op jit(solution)/shard_map/ppermute | solution.py:41
  111.0 28.9 %copy-start.3 = (bf16[4096,1024]{1,0:T(8,128)(2,1)S(1)}, bf16[4096,1024]{1,0:T(8,128)(2,1)}, u32[]{:S(2)}) copy-start(bf16[4096,1024]{1,0:T(8,128)(2,1)} %copy-done.1) | copy-start | bytes 25165828
  123.5 16.3 %collective-permute-start.20 = (bf16[64,1024]{1,0:T(8,128)(2,1)S(1)}, bf16[64,1024]{1,0:T(8,128)(2,1)S(1)}, u32[]{:S(2)}, u32[]{:S(2)}) collective-permute-start(bf16[64,1024]{1,0:T(8,128)(2,1)S(1)} %fusion), channel_id=1, source_target_pairs={{0,16},{16,0},{1,17},{17,1},{2,18},{18,2},{3,19},{19,3},{4,20},{20... | collective-permute-start | bytes 393224 | tf_op jit(solution)/shard_map/ppermute | solution.py:31
  (20 other events, 59.4 us)

commit v3 on v2

v3 whole, which is shorter than its diff:
```python
import functools
import math

import jax
import jax.numpy as jnp
from jax import lax
from jax.experimental import pallas as pl
from jax.experimental.pallas import tpu as pltpu
from jax.sharding import Mesh, PartitionSpec as P

beta_first = 0.9
beta_second = 0.95
learn_rate = 0.001
decay_rate = 0.1
epsilon = 1e-08
bias_first = 1.0 - math.exp(100.0 * math.log(beta_first))
bias_second = 1.0 - math.exp(100.0 * math.log(beta_second))

AXES = ("z", "l", "x", "c", "t")
SIZES = (4, 2, 4, 2, 2)
DP = AXES[:4]
NZ, NL, NX, NC, NT = SIZES
COUNT = NZ * NL * NX * NC
NG = 2
SLOT = 64
TOP = 14.0
CODE = 16
MIB = 1 << 20


def shift(value, axis, step):
    size = SIZES[AXES.index(axis)]
    return lax.ppermute(value, axis, [(i, (i + step) % size) for i in range(size)])


def cross(value, stage, step):
    pairs = []
    for z in range(NZ):
        for x in range(NX):
            for c in range(NC):
                to = ((z + step) % NZ, x) if c == stage else (z, (x + step) % NX)
                pairs.append(((z * NX + x) * NC + c, (to[0] * NX + to[1]) * NC + c))
    return lax.ppermute(value, ("z", "x", "c"), pairs)


def gathered(value, stage):
    return [value] + [cross(value, stage, -k) for k in (1, 2, 3)]


def reduced(terms, stage):
    total = terms[0]
    for k in (1, 2, 3):
        total = total + cross(terms[k], stage, k).astype(jnp.float32)
    return total


def after(value, *others):
    return lax.optimization_barrier((value, *others))[0]


ANY = pl.BlockSpec(memory_space=pl.ANY)
SCALARS = pl.BlockSpec(memory_space=pltpu.SMEM)
AHEAD = 3


def kernel_call(kernel, out_shape, scratch, flops, moved, *args, out_specs=None, in_specs=None):
    return pl.pallas_call(
        kernel,
        in_specs=in_specs or [SCALARS] + [ANY] * (len(args) - 1),
        out_specs=out_specs or [ANY] * len(out_shape),
        out_shape=out_shape,
        scratch_shapes=scratch,
        compiler_params=pltpu.CompilerParams(vmem_limit_bytes=58 * MIB),
        cost_estimate=pl.CostEstimate(flops=flops, bytes_accessed=moved, transcendentals=0),
    )(*args)


def select_kernel(place, tokens, mine, other, held, low, high, in_sem, low_sem, high_sem):
    z, l, x, c = place[0], place[1], place[2], place[3]
    blocks, rows, _ = held.shape
    lanes = NC * SLOT
    below = lax.broadcasted_iota(jnp.int32, (rows, lanes), 1) < SLOT

    def load(k):
        return pltpu.make_async_copy(tokens.at[pl.ds(k * rows, rows)], held.at[k], in_sem.at[k])

    def store(k):
        return (
            pltpu.make_async_copy(low.at[k], mine.at[pl.ds(k * rows, rows)], low_sem.at[k]),
            pltpu.make_async_copy(high.at[k], other.at[pl.ds(k * rows, rows)], high_sem.at[k]),
        )

    def column(k, core, slot):
        first, pair, second = slot // (NL * 4), slot // 4 % NL, slot % 4
        to_z = lax.rem(z + jnp.where(core == 0, first, second), NZ)
        to_x = lax.rem(x + jnp.where(core == 0, second, first), NX)
        at = (to_z * NL + lax.rem(l + pair, NL)) * NX + to_x
        return held[k, :, pl.ds(pl.multiple_of(at * lanes, lanes), lanes)]

    for k in range(blocks):
        load(k).start()

    @pl.loop(0, blocks)
    def _(k):
        load(k).wait()
        for core, out in ((c, low), (1 - c, high)):
            for slot in range(0, COUNT // NC, NC):
                one = pltpu.roll(column(k, core, slot), SLOT * core, 1)
                two = pltpu.roll(column(k, core, slot + 1), SLOT * (1 - core), 1)
                out[k, :, slot * SLOT : (slot + 2) * SLOT] = jnp.where(below, one, two)
        for copy in store(k):
            copy.start()

    for k in range(blocks):
        for copy in store(k):
            copy.wait()


def selected(place, tokens):
    rows, half = tokens.shape
    blocks = 8
    out = jax.ShapeDtypeStruct((rows, half // NC), tokens.dtype)
    part = pltpu.VMEM((blocks, rows // blocks, half // NC), tokens.dtype)
    sems = pltpu.SemaphoreType.DMA((blocks,))
    scratch = [pltpu.VMEM((blocks, rows // blocks, half), tokens.dtype), part, part, sems, sems, sems]
    return kernel_call(select_kernel, [out, out], scratch, 0, 4 * rows * half, place, tokens)


def grad_kernel(mine, theirs, cot, cot_theirs, *refs):
    outs, refs = refs[:4], refs[4:]
    held, held_theirs, cots, own, sends, in_sem, theirs_sem, cot_sem, out_sem = refs
    blocks, _, block = held.shape

    def load(k):
        at = pl.ds(pl.multiple_of(k * block, block), block)
        return (
            pltpu.make_async_copy(mine.at[:, at], held.at[k], in_sem.at[k]),
            pltpu.make_async_copy(theirs.at[:, at], held_theirs.at[k], theirs_sem.at[k]),
        )

    def store(k):
        return pltpu.make_async_copy(own if k == 0 else sends.at[k - 1], outs[k], out_sem.at[k])

    both = [pltpu.make_async_copy(v, cots.at[n], cot_sem.at[n]) for n, v in enumerate((cot, cot_theirs))]
    first, second = load(0)
    both[0].start()
    first.start()
    both[1].start()
    second.start()
    for k in range(1, blocks):
        for copy in load(k):
            copy.start()

    over = (((0,), (0,)), ((), ()))

    @pl.loop(0, blocks)
    def _(k):
        one, two = load(k)
        pl.when(k == 0)(both[0].wait)
        one.wait()
        term = lax.dot_general(held[k], cots[0], over, preferred_element_type=jnp.float32)
        pl.when(k == 0)(both[1].wait)
        two.wait()
        term += lax.dot_general(held_theirs[k], cots[1], over, preferred_element_type=jnp.float32)
        term = term.reshape(own.shape)

        @pl.when(k == 0)
        def _():
            own[...] = term
            store(0).start()

        @pl.when(k > 0)
        def _():
            sends[k - 1] = term.astype(sends.dtype)

        for n in range(1, blocks):
            pl.when(k == n)(store(n).start)

    for k in range(blocks):
        store(k).wait()


def chip_grad(mine, theirs, cotangent, cotangent_theirs):
    rows, half = mine.shape
    width = cotangent.shape[1]
    piece = (half // 4 // SLOT, SLOT, width)
    part = pltpu.VMEM((4, rows, half // 4), mine.dtype)
    sems = pltpu.SemaphoreType.DMA((4,))
    scratch = [
        part,
        part,
        pltpu.VMEM((2, rows, width), mine.dtype),
        pltpu.VMEM(piece, jnp.float32),
        pltpu.VMEM((3, *piece), jnp.bfloat16),
        sems,
        sems,
        pltpu.SemaphoreType.DMA((2,)),
        sems,
    ]
    out_shape = [jax.ShapeDtypeStruct(piece, jnp.bfloat16 if n else jnp.float32) for n in range(4)]
    return kernel_call(
        grad_kernel,
        out_shape,
        scratch,
        0,
        0,
        mine,
        theirs,
        cotangent,
        cotangent_theirs,
        in_specs=[ANY] * 4,
    )


def reorder_kernel(place, target, tokens, *refs):
    pieces, refs = refs[: COUNT // 8], refs[COUNT // 8 :]
    full, keys_send, held, rows_in, moved, even, odd, acc, tokens_sem, rows_sem, full_sem = refs
    t = place[4]
    octets, _, block = held.shape
    lines = rows_in.shape[2]
    width = full.shape[1]
    column = width // NT

    def load(o):
        at = pl.multiple_of(o * lines, lines)
        copies = [
            pltpu.make_async_copy(p.at[pl.ds(at, lines)], rows_in.at[o, n], rows_sem.at[o, n])
            for n, p in enumerate(pieces)
        ]
        at = pl.multiple_of(o * block, block)
        return copies + [pltpu.make_async_copy(tokens.at[:, pl.ds(at, block)], held.at[o], tokens_sem.at[o])]

    def store(o):
        at = pl.ds(pl.multiple_of(o * block, block), block)
        return [
            pltpu.make_async_copy(
                moved.at[h, at], full.at[at, pl.ds(h * column, column)], full_sem.at[o, h]
            )
            for h in range(NT)
        ]

    for o in range(AHEAD):
        for copy in load(o):
            copy.start()
    acc[...] = jnp.zeros_like(acc)
    size, each = block // NG, lines // NG

    def arrive(o):
        @pl.when(o + AHEAD - 1 < octets)
        def _():
            for copy in load(o + AHEAD - 1):
                copy.start()

        for copy in load(o):
            copy.wait()

    def reorder(o, stage):
        for group in range(NG):
            rows = jnp.concatenate(
                [
                    rows_in[o, n, group * each : (group + 1) * each].reshape(-1, width)
                    for n in range(len(pieces))
                ],
                axis=0,
            )
            pick = lax.broadcasted_iota(jnp.int32, (size, rows.shape[0]), 0) == target[o * NG + group]
            pick = jnp.where(pick, 1.0, 0.0).astype(jnp.bfloat16)
            out = jnp.dot(pick, rows, preferred_element_type=jnp.float32).astype(jnp.bfloat16)
            at = pl.ds(pl.multiple_of(o * block + group * size, size), size)
            halves = [out[:, h * column : (h + 1) * column] for h in range(NT)]
            for h in range(NT):
                moved[h, at] = halves[h]
            stage[group * size : (group + 1) * size] = jnp.where(t == 0, halves[1], halves[0])

    def multiply(o, stage):
        acc[...] += jnp.dot(held[o], stage[...], preferred_element_type=jnp.float32)

    def leave(o):
        for copy in store(o):
            copy.start()

    for copy in load(0):
        copy.wait()
    reorder(0, even)
    leave(0)

    @pl.loop(0, octets // 2 - 1)
    def _(i):
        o = 2 * i
        arrive(o + 1)
        reorder(o + 1, odd)
        multiply(o, even)
        leave(o + 1)
        arrive(o + 2)
        reorder(o + 2, even)
        multiply(o + 1, odd)
        leave(o + 2)

    arrive(octets - 1)
    reorder(octets - 1, odd)
    multiply(octets - 2, even)
    leave(octets - 1)
    multiply(octets - 1, odd)
    power = jnp.floor(jnp.log2(jnp.clip(jnp.full((8, 128), jnp.max(jnp.abs(acc[...]))), 1e-30, None)))
    count = acc.shape[0]
    keys_send[:count] = acc[...] * jnp.exp2(TOP - power)[:1, :1]
    keys_send[count:] = jnp.broadcast_to(power[:1, :1], (keys_send.shape[0] - count, column))

    for o in range(octets):
        for copy in store(o):
            copy.wait()


def reorder_and_send(place, target, tokens, pieces):
    rows, half = tokens.shape
    width = pieces[0].shape[-1]
    octets = target.shape[0] // NG
    block = half // octets
    lines, line, _ = pieces[0].shape
    scratch = [
        pltpu.VMEM((octets, rows, block), tokens.dtype),
        pltpu.VMEM((octets, len(pieces), lines // octets, line, width), tokens.dtype),
        pltpu.VMEM((NT, half, width // NT), tokens.dtype),
        pltpu.VMEM((block, width // NT), tokens.dtype),
        pltpu.VMEM((block, width // NT), tokens.dtype),
        pltpu.VMEM((rows, width // NT), jnp.float32),
        pltpu.SemaphoreType.DMA((octets,)),
        pltpu.SemaphoreType.DMA((octets, len(pieces))),
        pltpu.SemaphoreType.DMA((octets, NT)),
    ]
    vmem = pl.BlockSpec(memory_space=pltpu.VMEM)
    return kernel_call(
        reorder_kernel,
        [
            jax.ShapeDtypeStruct((half, width), jnp.bfloat16),
            jax.ShapeDtypeStruct((rows + CODE, width // NT), jnp.float32),
        ],
        scratch,
        2 * rows * half * width,
        rows * half * 2 + half * width * 4,
        place,
        target,
        tokens,
        *pieces,
        in_specs=[SCALARS, vmem] + [ANY] * (1 + len(pieces)),
        out_specs=[ANY, vmem],
    )


def keep_kernel(place, tokens, full, keys, held, part, tokens_sem, part_sem):
    t = place[4]
    blocks, _, block = held.shape
    column = part.shape[2]

    def load(o):
        at = pl.ds(pl.multiple_of(o * block, block), block)
        return (
            pltpu.make_async_copy(
                full.at[at, pl.ds(pl.multiple_of(t * column, column), column)], part.at[o], part_sem.at[o]
            ),
            pltpu.make_async_copy(tokens.at[:, at], held.at[o], tokens_sem.at[o]),
        )

    for o in range(blocks):
        for copy in load(o):
            copy.start()
    keys[...] = jnp.zeros_like(keys)

    @pl.loop(0, blocks)
    def _(o):
        for copy in load(o):
            copy.wait()
        keys[...] += jnp.dot(held[o], part[o], preferred_element_type=jnp.float32)


def keys_kept(place, tokens, full):
    rows, half = tokens.shape
    width = full.shape[1]
    blocks = 4
    sems = pltpu.SemaphoreType.DMA((blocks,))
    return kernel_call(
        keep_kernel,
        jax.ShapeDtypeStruct((rows, width // NT), jnp.float32),
        [
            pltpu.VMEM((blocks, rows, half // blocks), tokens.dtype),
            pltpu.VMEM((blocks, half // blocks, width // NT), tokens.dtype),
            sems,
            sems,
        ],
        0,
        0,
        place,
        tokens,
        full,
        out_specs=pl.BlockSpec(memory_space=pltpu.VMEM),
    )


def back_kernel(first, cotangent, full, *refs):
    back, cot, held, out, cot_sem, in_sem, out_sem = refs[-7:]
    blocks, block, _ = held.shape

    def load(o):
        at = pl.ds(pl.multiple_of((first + o) * block, block), block)
        return pltpu.make_async_copy(full.at[at], held.at[o], in_sem.at[o])

    def store(o):
        at = pl.ds(pl.multiple_of((first + o) * block, block), block)
        return pltpu.make_async_copy(out.at[o], back.at[:, at], out_sem.at[o])

    whole = pltpu.make_async_copy(cotangent, cot, cot_sem)
    whole.start()
    for o in range(blocks):
        load(o).start()
    whole.wait()

    @pl.loop(0, blocks)
    def _(o):
        load(o).wait()
        out[o] = lax.dot_general(
            cot[...], held[o], (((1,), (1,)), ((), ())), preferred_element_type=jnp.float32
        ).astype(out.dtype)
        store(o).start()

    for o in range(blocks):
        store(o).wait()


def back_part(cotangent, full, first, last, held=()):
    rows, width = cotangent.shape
    half = full.shape[0]
    block = 512
    blocks = last - first
    sems = pltpu.SemaphoreType.DMA((blocks,))
    return pl.pallas_call(
        functools.partial(back_kernel, first),
        in_specs=[ANY] * (2 + len(held)),
        out_specs=ANY,
        out_shape=jax.ShapeDtypeStruct((rows, half), jnp.bfloat16),
        scratch_shapes=[
            pltpu.VMEM((rows, width), cotangent.dtype),
            pltpu.VMEM((blocks, block, width), full.dtype),
            pltpu.VMEM((blocks, rows, block), jnp.bfloat16),
            pltpu.SemaphoreType.DMA,
            sems,
            sems,
        ],
        input_output_aliases={2: 0} if held else {},
        compiler_params=pltpu.CompilerParams(vmem_limit_bytes=58 * MIB),
        cost_estimate=pl.CostEstimate(
            flops=2 * rows * block * blocks * width, bytes_accessed=0, transcendentals=0
        ),
    )(cotangent, full, *held)


def decoded(came):
    value = came.astype(jnp.float32)
    return value[:-CODE] * jnp.exp2(value[-CODE : 1 - CODE] - TOP)


def pack_kernel(first, second, out):
    for n, moment in enumerate((first, second)):
        for k in range(8):
            out[:, n * 8 + k, :] = moment[:, k * 128 : (k + 1) * 128]


def packed(first, second):
    rows, width = first.shape
    return pl.pallas_call(
        pack_kernel,
        out_shape=jax.ShapeDtypeStruct((rows, 16, width // 8), jnp.float32),
        compiler_params=pltpu.CompilerParams(vmem_limit_bytes=58 * MIB),
        cost_estimate=pl.CostEstimate(flops=0, bytes_accessed=4 * MIB // 4, transcendentals=0),
    )(first, second)


def update_kernel(scale, source, moments, own, came, full, weight, first, second, held):
    rows = held.shape[0]

    def move(p, carry):
        held[p] = moments[source[p]]
        return carry

    lax.fori_loop(0, rows, move, 0, unroll=8)
    for k in range(8):
        at = slice(k * 128, (k + 1) * 128)
        grad = (own[:, at] + came[:, at].astype(jnp.float32)) * scale
        base = full[:, at].astype(jnp.float32)
        new_first = beta_first * held[:, k, :] + (1.0 - beta_first) * grad
        new_second = beta_second * held[:, 8 + k, :] + (1.0 - beta_second) * grad * grad
        step = new_first / bias_first / (jnp.sqrt(new_second / bias_second) + epsilon)
        weight[:, at] = (base - learn_rate * (step + decay_rate * base)).astype(weight.dtype)
        first[:, at] = new_first
        second[:, at] = new_second


def updated(source, moments, own, came, base, scale):
    rows, width = own.shape
    whole = pl.BlockSpec((rows, width), lambda i, source: (0, 0))
    return pl.pallas_call(
        functools.partial(update_kernel, scale),
        grid_spec=pltpu.PrefetchScalarGridSpec(
            num_scalar_prefetch=1,
            grid=(1,),
            in_specs=[
                pl.BlockSpec(moments.shape, lambda i, source: (0, 0, 0)),
                whole,
                whole,
                whole,
            ],
            out_specs=[whole] * 3,
            scratch_shapes=[pltpu.VMEM(moments.shape, jnp.float32)],
        ),
        out_shape=[jax.ShapeDtypeStruct((rows, width), k) for k in (jnp.bfloat16, jnp.float32, jnp.float32)],
        compiler_params=pltpu.CompilerParams(vmem_limit_bytes=8 * MIB),
        cost_estimate=pl.CostEstimate(flops=0, bytes_accessed=MIB, transcendentals=0),
    )(source, moments, own, came, base)


def targets(landing, place, rows):
    z, l, x, c = place[0], place[1], place[2], place[3]
    steps = jnp.arange(4, dtype=jnp.int32)
    zs, xs = (z + steps) % NZ, (x + steps) % NX
    ls = (l + jnp.arange(NL, dtype=jnp.int32)) % NL

    def owners(core):
        along_z = (zs[None, :, None] * NL + ls) * NX + xs[:, None, None]
        along_x = (zs[:, None, None] * NL + ls) * NX + xs[None, :, None]
        return (jnp.where(core == 0, along_z, along_x) * NC + core).reshape(-1)

    order = jnp.concatenate([owners(c), owners(1 - c)])
    groups = 8 * NG
    each = COUNT // groups
    spots = jnp.take(landing, order, axis=0).reshape(COUNT // (4 * NL), 4 * NL, groups, each)
    spots = spots + jnp.arange(each, dtype=jnp.int32) * rows
    return spots.transpose(2, 0, 3, 1).reshape(groups, 1, each * COUNT)


def shards(tokens, cotangent, old_weight, old_first, old_second, landing):
    z, l, x, c, t = [lax.axis_index(a).astype(jnp.int32) for a in AXES]
    place = jnp.stack([z, l, x, c, t])
    me = ((z * NL + l) * NX + x) * NC + c
    rows, width = old_weight.shape[1:]
    scale = 1.0 / math.sqrt(tokens.shape[0] * COUNT)

    own = old_weight.reshape(rows, width)
    pair = jnp.stack([own, shift(own, "l", 1)])
    moments = packed(old_first.reshape(rows, width), old_second.reshape(rows, width))
    target = targets(landing, place, rows)
    pair, moments, target, place_1 = lax.optimization_barrier((pair, moments, target, place))
    line = jnp.stack(gathered(pair, 0)).reshape(4 * NL, rows, width)
    mine, other = selected(place_1, tokens)
    line, mine, other, cotangent_1, moments = lax.optimization_barrier((line, mine, other, cotangent, moments))
    theirs = shift(other, "c", 1)
    cotangent_theirs = shift(cotangent_1, "c", 1)
    line = line.transpose(1, 0, 2)
    here = gathered(line, 1)
    there = shift(line, "c", 1)
    moments = lax.all_to_all(moments, DP, split_axis=0, concat_axis=0, tiled=True)
    terms = chip_grad(mine, theirs, cotangent, cotangent_theirs)
    here, terms, moments = lax.optimization_barrier((here, terms, moments))
    pieces = here + [there] + [shift(v, "c", 1) for v in here[1:]]

    total = reduced(terms, 0).reshape(NL, 4, rows, width)
    full, keys_send = reorder_and_send(place, target, tokens, pieces)
    keys_came = shift(keys_send.astype(jnp.float16), "t", 1)
    keys_keep = keys_kept(place, tokens, full)
    total, keys_keep = lax.optimization_barrier((total, keys_keep))
    terms = [total[:, 0]] + [total[:, k].astype(jnp.bfloat16) for k in (1, 2, 3)]
    terms, full_1 = lax.optimization_barrier((terms, full))
    total = reduced(terms, 1)
    back = back_part(cotangent, full_1, 0, 4)
    total, back = lax.optimization_barrier((total, back))
    came = shift(total[1].astype(jnp.bfloat16), "l", 1)
    back = back_part(cotangent, full, 4, 8, (back,))

    base = lax.dynamic_slice_in_dim(full, me * rows, rows, 0)
    column = lax.dynamic_slice_in_dim(landing, me, 1, 1)[:, 0]
    lanes = jnp.arange(COUNT, dtype=jnp.int32)
    source = jnp.sum(jnp.where(column[None, :] == lanes[:, None], lanes[None, :], 0), axis=1, dtype=jnp.int32)
    new_weight, new_first, new_second = updated(source, moments, total[0], came, base, scale)
    keys = (keys_keep + decoded(keys_came)).astype(jnp.bfloat16)
    return (keys, back, new_weight[None], new_first[None], new_second[None])


def solution(mesh):
    fine = Mesh(mesh.devices.reshape(SIZES), AXES)
    in_specs = (
        P(DP, "t"),
        P(DP, None),
        P("t", DP, None),
        P("t", DP, None),
        P("t", DP, None),
        P(),
    )
    out_specs = (
        P(DP, "t"),
        P(DP, "t"),
        P("t", DP, None),
        P("t", DP, None),
        P("t", DP, None),
    )
    return jax.shard_map(shards, mesh=fine, in_specs=in_specs, out_specs=out_specs, check_vma=False)
```

time: 147 us -> 128 us (0.87); the launches traced: 145 us -> 128 us
  local copies, waits for them, and re-layouts: 26.7 us -> 7.26 us
  Pallas kernels: 54.4 us -> 68.9 us
  waiting for transfers between devices: 22.2 us -> 16.1 us
  other arithmetic: 8.2 us -> 4.93 us
  starting transfers between devices: 32.4 us -> 29.4 us
    unnamed x45 -> x15, local copies, waits for them, and re-layouts: 22.3 us -> 1.56 us
    pallas_call x5 -> x6, Pallas kernels: 51.3 us -> 64.7 us  [the longest x4 47.2 us: kernel_call(): pl.pallas_call(kernel, in_specs=in_specs or [SCALARS] + [ANY] * (len(args...]
    ppermute x9, waiting for transfers between devices: 16.1 us -> 3.55 us  [shift(): lax.ppermute(value, axis, [(i, (i + step) % size) for i in range(size)])]
    ppermute x12, starting transfers between devices: 22 us -> 16.7 us  [cross(): return lax.ppermute(value, ('z', 'x', 'c'), pairs)]
    all_to_all x1, waiting for transfers between devices: 6.1 us -> 10.8 us  [shards(): lax.all_to_all(moments, DP, split_axis=0, concat_axis=0, tiled=True)]
    add x2, other arithmetic: 4.46 us -> 2.05 us  [reduced(): total = total + cross(terms[k], stage, k).astype(jnp.float32)]
    ppermute x12, waiting for transfers between devices: 0.03 us -> 1.72 us  [cross(): return lax.ppermute(value, ('z', 'x', 'c'), pairs)]
    ppermute x9, starting transfers between devices: 5.76 us -> 7.39 us  [shift(): lax.ppermute(value, axis, [(i, (i + step) % size) for i in range(size)])]
  transfers between devices with their start and end apart: 22 -> 22, of which waited for: 2 -> 4; matrix products, arithmetic and copies ran while one was open for 6% -> 4% of each run, Pallas kernels for 38% -> 54%
where the time goes in v3:
time: 128 us
  Pallas kernels  68.9 us (54%)
  starting transfers between devices  29.4 us (23%)
  waiting for transfers between devices  16.1 us (13%)
  local copies, waits for them, and re-layouts  7.26 us (6%)
  other arithmetic  4.93 us (4%)
    pallas_call x4, Pallas kernels, kernel_call(): pl.pallas_call(kernel, in_specs=in_specs or [SCALARS] + [ANY] * (len(args...  47.2 us
    pallas_call x2, Pallas kernels, back_part(): pl.pallas_call(functools.partial(back_kernel, first), in_specs=[ANY] * (2...  17.5 us
    ppermute x12, starting transfers between devices, cross(): return lax.ppermute(value, ('z', 'x', 'c'), pairs)  16.7 us
    all_to_all x1, waiting for transfers between devices, shards(): lax.all_to_all(moments, DP, split_axis=0, concat_axis=0, tiled=True)  10.8 us
    ppermute x9, starting transfers between devices, shift(): lax.ppermute(value, axis, [(i, (i + step) % size) for i in range(size)])  7.39 us
    all_to_all x1, starting transfers between devices, shards(): lax.all_to_all(moments, DP, split_axis=0, concat_axis=0, tiled=True)  5.39 us
    ppermute x9, waiting for transfers between devices, shift(): lax.ppermute(value, axis, [(i, (i + step) % size) for i in range(size)])  3.55 us
  transfers between devices with their start and end apart: 22, of which 4 were waited for; matrix products, arithmetic and copies ran while one was open for 4% of the time, Pallas kernels for 54%

profile of v3, /device:TPU:0, one launch (start us, length us, event | category | flops | bytes accessed | tf_op | source)
XLA Modules:
  0.0 127.6 jit_solution(3849091060753159277)
XLA Ops:
  0.7 1.7 %collective-permute-start = (bf16[64,1024]{1,0:T(8,128)(2,1)}, bf16[64,1024]{1,0:T(8,128)(2,1)S(1)}, u32[]{:S(2)}, u32[]{:S(2)}) collective-permute-start(bf16[64,1024]{1,0:T(8,128)(2,1)} %bitcast.50), channel_id=1, source_target_pairs={{0,16},{16,0},{1,17},{17,1},{2,18},{18,2},{3,19},{19,3},{4,20},{20... | collective-permute-start | bytes 393224 | tf_op jit(solution)/shard_map/ppermute | solution.py:33
  4.6 2.2 %shard_map.101 = f32[64,16,128]{2,1,0:T(8,128)} custom-call(f32[64,1024]{1,0:T(8,128)} %bitcast.45, f32[64,1024]{1,0:T(8,128)} %bitcast.46), custom_call_target="tpu_custom_call" | custom-call | bytes 1048576 | tf_op jit(solution)/shard_map/pallas_call | solution.py:469
  7.4 2.0 %collective-permute-start.3 = (bf16[2,64,1024]{2,1,0:T(8,128)(2,1)S(1)}, bf16[2,64,1024]{2,1,0:T(8,128)(2,1)S(1)}, u32[]{:S(2)}, u32[]{:S(2)}) collective-permute-start(bf16[2,64,1024]{2,1,0:T(8,128)(2,1)S(1)} %pad_maximum_fusion.1), channel_id=1, source_target_pairs={{0,32},{2,6},{4,36},{6,10},{8,40},{10,14},{12,44},{14,2},{32,64},{... | collective-permute-start | bytes 786440 | tf_op jit(solution)/shard_map/ppermute | solution.py:43
  9.4 3.6 %collective-permute-start.2 = (bf16[2,64,1024]{2,1,0:T(8,128)(2,1)S(1)}, bf16[2,64,1024]{2,1,0:T(8,128)(2,1)S(1)}, u32[]{:S(2)}, u32[]{:S(2)}) collective-permute-start(bf16[2,64,1024]{2,1,0:T(8,128)(2,1)S(1)} %pad_maximum_fusion.1), channel_id=1, source_target_pairs={{0,64},{2,10},{4,68},{6,14},{8,72},{10,2},{12,76},{14,6},{32,96},{... | collective-permute-start | bytes 786440 | tf_op jit(solution)/shard_map/ppermute | solution.py:43
  14.0 8.3 %shard_map.102 = (bf16[1024,2048]{1,0:T(8,128)(2,1)}, bf16[1024,2048]{1,0:T(8,128)(2,1)}) custom-call(s32[5]{0:T(128)} %stack.46.place, bf16[1024,4096]{1,0:T(8,128)(2,1)} %tokens.5), custom_call_target="tpu_custom_call" | custom-call | bytes 16777216 | tf_op jit(solution)/shard_map/pallas_call | solution.py:67
  22.5 1.5 %copy.32 = bf16[8,64,1024]{2,0,1:T(8,128)(2,1)} copy(bf16[8,64,1024]{2,1,0:T(8,128)(2,1)S(1)} %bitcast.42) | data formatting | bytes 2097152 | tf_op jit(solution)/shard_map/reshape | solution.py:551
  24.6 2.8 %collective-permute-start.4 = (bf16[64,8,1024]{2,1,0:T(8,128)(2,1)}, bf16[64,8,1024]{2,1,0:T(8,128)(2,1)}, u32[]{:S(2)}, u32[]{:S(2)}) collective-permute-start(bf16[64,8,1024]{2,1,0:T(8,128)(2,1)} %bitcast.18.refs_0_), channel_id=1, source_target_pairs={{0,12},{2,98},{4,0},{6,102},{8,4},{10,106},{12,8},{14,110},{32,44}... | collective-permute-start | bytes 3145736 | tf_op jit(solution)/shard_map/ppermute | solution.py:43
  29.0 5.4 %all-to-all-start = ((f32[64,16,128]{2,1,0:T(8,128)}), f32[64,16,128]{2,1,0:T(8,128)S(1)}, u32[]{:S(2)}, u32[]{:S(2)}) async-start(f32[64,16,128]{2,1,0:T(8,128)} %shard_map.101), calls=%async_computation | async-start | bytes 1048576 | tf_op jit(solution)/shard_map/all_to_all | solution.py:559
  34.6 15.7 %shard_map.103 = (f32[8,64,1024]{2,1,0:T(8,128)}, bf16[8,64,1024]{2,1,0:T(8,128)(2,1)}, bf16[8,64,1024]{2,1,0:T(8,128)(2,1)}, bf16[8,64,1024]{2,1,0:T(8,128)(2,1)}) custom-call(bf16[1024,2048]{1,0:T(8,128)(2,1)} %get-tuple-element.49.mine, bf16[1024,2048]{1,0:T(8,128)(2,1)} %collective-permute-done.7.theirs, bf16[1024,1024]{1,0:T(8,128)(2,1)} %cotangent.3, ...), custom_call_target="tpu_custom_call" | custom-call | tf_op jit(solution)/shard_map/pallas_call | solution.py:67
  50.3 10.8 %all-to-all-done.moments = f32[64,16,128]{2,1,0:T(8,128)S(1)} async-done(((f32[64,16,128]{2,1,0:T(8,128)}), f32[64,16,128]{2,1,0:T(8,128)S(1)}, u32[]{:S(2)}, u32[]{:S(2)}) %all-to-all-start) | async-done | bytes 524320 | tf_op jit(solution)/shard_map/all_to_all | solution.py:559
  61.8 2.4 %collective-permute-start.11 = (bf16[8,64,1024]{2,1,0:T(8,128)(2,1)}, bf16[8,64,1024]{2,1,0:T(8,128)(2,1)S(1)}, u32[]{:S(2)}, u32[]{:S(2)}) collective-permute-start(bf16[8,64,1024]{2,1,0:T(8,128)(2,1)} %get-tuple-element.60), channel_id=1, source_target_pairs={{0,96},{2,14},{4,100},{6,2},{8,104},{10,6},{12,108},{14,10},{32,0}... | collective-permute-start | bytes 3145736 | tf_op jit(solution)/shard_map/ppermute | solution.py:43
  64.3 1.2 collective-permute-start.9
  67.2 14.0 %shard_map.104 = (bf16[4096,1024]{1,0:T(8,128)(2,1)}, f32[1040,512]{1,0:T(8,128)}) custom-call(s32[5]{0:T(128)} %stack.46.place, s32[16,1,256]{2,1,0:T(1,128)} %copy.29.target, bf16[1024,4096]{1,0:T(8,128)(2,1)} %tokens.5, bf16[64,8,1024]{2,1,0:T(8,128)(2,1)} %bitcast.18.refs_0_, bf16[64,8,1024]{2,1,0:T(8,128)(2,1)} %collective-permute-done.4.refs_1_, ...), custom_call_target="tpu_custom_call" | custom-call | flops 8589934592 | bytes 25165824 | tf_op jit(solution)/shard_map/pallas_call | solution.py:67
  81.2 9.1 %shard_map.105 = f32[1024,512]{1,0:T(8,128)} custom-call(s32[5]{0:T(128)} %stack.46.place, bf16[1024,4096]{1,0:T(8,128)(2,1)} %tokens.5, bf16[4096,1024]{1,0:T(8,128)(2,1)} %get-tuple-element.74.full), custom_call_target="tpu_custom_call" | custom-call | tf_op jit(solution)/shard_map/pallas_call | solution.py:67
  90.4 1.7 %collective-permute-done.9 = bf16[8,64,1024]{2,1,0:T(8,128)(2,1)} collective-permute-done((bf16[8,64,1024]{2,1,0:T(8,128)(2,1)}, bf16[8,64,1024]{2,1,0:T(8,128)(2,1)}, u32[]{:S(2)}, u32[]{:S(2)}) %collective-permute-start.9) | collective-permute-done | bytes 1048608 | tf_op jit(solution)/shard_map/ppermute | solution.py:43
  92.1 1.9 %convert_add_fusion = f32[8,64,1024]{2,1,0:T(8,128)S(1)} fusion(bf16[8,64,1024]{2,1,0:T(8,128)(2,1)S(1)} %collective-permute-done.11, bf16[8,64,1024]{2,1,0:T(8,128)(2,1)S(1)} %collective-permute-done.10, f32[8,64,1024]{2,1,0:T(8,128)S(1)} %copy-done.5, bf16[8,64,1024]{2,1,0:T(8,128)(2,1)} %collective-permute-done.9), kind=kLoop, calls=%fused_computation.4 | loop fusion | flops 3145728 | bytes 7340032 | tf_op jit(solution)/shard_map/add | solution.py:53
  94.2 1.4 %copy-done.4 = f32[1040,512]{1,0:T(8,128)S(1)} copy-done((f32[1040,512]{1,0:T(8,128)S(1)}, f32[1040,512]{1,0:T(8,128)}, u32[]{:S(2)}) %copy-start.4) | copy-done | bytes 2129944
  95.9 3.3 %collective-permute-start.16 = (f16[1040,512]{1,0:T(8,128)(2,1)S(1)}, f16[1040,512]{1,0:T(8,128)(2,1)S(1)}, u32[]{:S(2)}, u32[]{:S(2)}) collective-permute-start(f16[1040,512]{1,0:T(8,128)(2,1)S(1)} %convert_element_type.46), channel_id=1, source_target_pairs={{0,1},{1,0},{2,3},{3,2},{4,5},{5,4},{6,7},{7,6},{8,9},{9,8},{10,11... | collective-permute-start | bytes 3194888 | tf_op jit(solution)/shard_map/ppermute | solution.py:33
  99.9 1.3 %collective-permute-start.17 = (bf16[2,64,1024]{2,1,0:T(8,128)(2,1)S(1)}, bf16[2,64,1024]{2,1,0:T(8,128)(2,1)S(1)}, u32[]{:S(2)}, u32[]{:S(2)}) collective-permute-start(bf16[2,64,1024]{2,1,0:T(8,128)(2,1)S(1)} %get-tuple-element.71), channel_id=1, source_target_pairs={{0,4},{2,34},{4,8},{6,38},{8,12},{10,42},{12,0},{14,46},{32,36},{3... | collective-permute-start | bytes 786440 | tf_op jit(solution)/shard_map/ppermute | solution.py:43
  102.1 8.8 %shard_map.106.refs_0_ = bf16[1024,4096]{1,0:T(8,128)(2,1)} custom-call(bf16[1024,1024]{1,0:T(8,128)(2,1)} %cotangent.3, bf16[4096,1024]{1,0:T(8,128)(2,1)} %get-tuple-element.74.full), custom_call_target="tpu_custom_call" | custom-call | flops 4294967296 | tf_op jit(solution)/shard_map/pallas_call | solution.py:435
  112.1 8.7 %shard_map.107 = bf16[1024,4096]{1,0:T(8,128)(2,1)} custom-call(bf16[1024,1024]{1,0:T(8,128)(2,1)} %cotangent.3, bf16[4096,1024]{1,0:T(8,128)(2,1)} %get-tuple-element.74.full, bf16[1024,4096]{1,0:T(8,128)(2,1)} %shard_map.106.refs_0_), custom_call_target="tpu_custom_call", output_to_operand_aliasing={{}: (2, {})} | custom-call | flops 4294967296 | tf_op jit(solution)/shard_map/pallas_call | solution.py:435
  120.9 2.7 %collective-permute-done.20.came = bf16[64,1024]{1,0:T(8,128)(2,1)S(1)} collective-permute-done((bf16[64,1024]{1,0:T(8,128)(2,1)S(1)}, bf16[64,1024]{1,0:T(8,128)(2,1)S(1)}, u32[]{:S(2)}, u32[]{:S(2)}) %collective-permute-start.20) | collective-permute-done | bytes 131104 | tf_op jit(solution)/shard_map/ppermute | solution.py:33
  123.7 2.0 %shard_map.108 = (bf16[64,1024]{1,0:T(8,128)(2,1)}, f32[64,1024]{1,0:T(8,128)}, f32[64,1024]{1,0:T(8,128)}) custom-call(s32[64]{0:T(128)S(1)} %select_reduce_fusion.source, f32[64,16,128]{2,1,0:T(8,128)S(1)} %all-to-all-done.moments, f32[64,1024]{1,0:T(8,128)S(1)} %slice_bitcast_fusion.4.own, bf16[64,1024]{1,0:T(8,128)(2,1)S(1)} %collective-permute-done.20.came, ...), custom_call_target="tpu_custom_call" | custom-call | bytes 1048576 | tf_op jit(solution)/shard_map/pallas_call | solution.py:500
  126.0 1.5 %fusion.1 = bf16[1024,512]{1,0:T(8,128)(2,1)} fusion(f32[1024,512]{1,0:T(8,128)S(1)} %copy-done.3, f32[1040,512]{1,0:T(8,128)S(1)} %convert_element_type.47, f32[512]{0:T(512)S(1)} %bitcast.53), kind=kLoop, calls=%fused_computation.3 | loop fusion | flops 1572864 | bytes 5244928 | tf_op jit(solution)/shard_map/convert_element_type | solution.py:582
  (82 shorter events, 12.3 us)
Async XLA Ops:
  0.6 6.8 %copy-start.6 = (bf16[1,64,1024]{2,1,0:T(8,128)(2,1)S(1)}, bf16[1,64,1024]{2,1,0:T(8,128)(2,1)}, u32[]{:S(2)}) copy-start(bf16[1,64,1024]{2,1,0:T(8,128)(2,1)} %param.8) | copy-start | bytes 393220
  0.7 6.8 %collective-permute-start = (bf16[64,1024]{1,0:T(8,128)(2,1)}, bf16[64,1024]{1,0:T(8,128)(2,1)S(1)}, u32[]{:S(2)}, u32[]{:S(2)}) collective-permute-start(bf16[64,1024]{1,0:T(8,128)(2,1)} %bitcast.50), channel_id=1, source_target_pairs={{0,16},{16,0},{1,17},{17,1},{2,18},{18,2},{3,19},{19,3},{4,20},{20... | collective-permute-start | bytes 393224 | tf_op jit(solution)/shard_map/ppermute | solution.py:33
  7.4 14.9 %collective-permute-start.3 = (bf16[2,64,1024]{2,1,0:T(8,128)(2,1)S(1)}, bf16[2,64,1024]{2,1,0:T(8,128)(2,1)S(1)}, u32[]{:S(2)}, u32[]{:S(2)}) collective-permute-start(bf16[2,64,1024]{2,1,0:T(8,128)(2,1)S(1)} %pad_maximum_fusion.1), channel_id=1, source_target_pairs={{0,32},{2,6},{4,36},{6,10},{8,40},{10,14},{12,44},{14,2},{32,64},{... | collective-permute-start | bytes 786440 | tf_op jit(solution)/shard_map/ppermute | solution.py:43
  9.4 12.9 %collective-permute-start.2 = (bf16[2,64,1024]{2,1,0:T(8,128)(2,1)S(1)}, bf16[2,64,1024]{2,1,0:T(8,128)(2,1)S(1)}, u32[]{:S(2)}, u32[]{:S(2)}) collective-permute-start(bf16[2,64,1024]{2,1,0:T(8,128)(2,1)S(1)} %pad_maximum_fusion.1), channel_id=1, source_target_pairs={{0,64},{2,10},{4,68},{6,14},{8,72},{10,2},{12,76},{14,6},{32,96},{... | collective-permute-start | bytes 786440 | tf_op jit(solution)/shard_map/ppermute | solution.py:43
  13.0 9.4 %collective-permute-start.1 = (bf16[2,64,1024]{2,1,0:T(8,128)(2,1)S(1)}, bf16[2,64,1024]{2,1,0:T(8,128)(2,1)S(1)}, u32[]{:S(2)}, u32[]{:S(2)}) collective-permute-start(bf16[2,64,1024]{2,1,0:T(8,128)(2,1)S(1)} %pad_maximum_fusion.1), channel_id=1, source_target_pairs={{0,96},{2,14},{4,100},{6,2},{8,104},{10,6},{12,108},{14,10},{32,0}... | collective-permute-start | bytes 786440 | tf_op jit(solution)/shard_map/ppermute | solution.py:43
  24.1 10.5 %collective-permute-start.7 = (bf16[1024,2048]{1,0:T(8,128)(2,1)}, bf16[1024,2048]{1,0:T(8,128)(2,1)}, u32[]{:S(2)}, u32[]{:S(2)}) collective-permute-start(bf16[1024,2048]{1,0:T(8,128)(2,1)} %get-tuple-element.50), channel_id=1, source_target_pairs={{0,2},{2,0},{1,3},{3,1},{4,6},{6,4},{5,7},{7,5},{8,10},{10,8},{9,1... | collective-permute-start | bytes 12582920 | tf_op jit(solution)/shard_map/ppermute | solution.py:33
  24.1 10.3 %collective-permute-start.8 = (bf16[1024,1024]{1,0:T(8,128)(2,1)S(1)}, bf16[1024,1024]{1,0:T(8,128)(2,1)}, u32[]{:S(2)}, u32[]{:S(2)}) collective-permute-start(bf16[1024,1024]{1,0:T(8,128)(2,1)S(1)} %copy-done.2), channel_id=1, source_target_pairs={{0,2},{2,0},{1,3},{3,1},{4,6},{6,4},{5,7},{7,5},{8,10},{10,8},{9,1... | collective-permute-start | bytes 6291464 | tf_op jit(solution)/shard_map/ppermute | solution.py:33
  24.6 36.6 %collective-permute-start.4 = (bf16[64,8,1024]{2,1,0:T(8,128)(2,1)}, bf16[64,8,1024]{2,1,0:T(8,128)(2,1)}, u32[]{:S(2)}, u32[]{:S(2)}) collective-permute-start(bf16[64,8,1024]{2,1,0:T(8,128)(2,1)} %bitcast.18.refs_0_), channel_id=1, source_target_pairs={{0,12},{2,98},{4,0},{6,102},{8,4},{10,106},{12,8},{14,110},{32,44}... | collective-permute-start | bytes 3145736 | tf_op jit(solution)/shard_map/ppermute | solution.py:43
  27.4 33.8 %collective-permute-start.5 = (bf16[64,8,1024]{2,1,0:T(8,128)(2,1)}, bf16[64,8,1024]{2,1,0:T(8,128)(2,1)}, u32[]{:S(2)}, u32[]{:S(2)}) collective-permute-start(bf16[64,8,1024]{2,1,0:T(8,128)(2,1)} %bitcast.18.refs_0_), channel_id=1, source_target_pairs={{0,8},{2,66},{4,12},{6,70},{8,0},{10,74},{12,4},{14,78},{32,40},{3... | collective-permute-start | bytes 3145736 | tf_op jit(solution)/shard_map/ppermute | solution.py:43
  28.2 33.0 %collective-permute-start.6 = (bf16[64,8,1024]{2,1,0:T(8,128)(2,1)}, bf16[64,8,1024]{2,1,0:T(8,128)(2,1)}, u32[]{:S(2)}, u32[]{:S(2)}) collective-permute-start(bf16[64,8,1024]{2,1,0:T(8,128)(2,1)} %bitcast.18.refs_0_), channel_id=1, source_target_pairs={{0,4},{2,34},{4,8},{6,38},{8,12},{10,42},{12,0},{14,46},{32,36},{3... | collective-permute-start | bytes 3145736 | tf_op jit(solution)/shard_map/ppermute | solution.py:43
  29.0 32.1 %all-to-all-start = ((f32[64,16,128]{2,1,0:T(8,128)}), f32[64,16,128]{2,1,0:T(8,128)S(1)}, u32[]{:S(2)}, u32[]{:S(2)}) async-start(f32[64,16,128]{2,1,0:T(8,128)} %shard_map.101), calls=%async_computation | async-start | bytes 1048576 | tf_op jit(solution)/shard_map/all_to_all | solution.py:559
  34.4 29.9 %collective-permute-start.12 = (bf16[64,8,1024]{2,1,0:T(8,128)(2,1)}, bf16[64,8,1024]{2,1,0:T(8,128)(2,1)}, u32[]{:S(2)}, u32[]{:S(2)}) collective-permute-start(bf16[64,8,1024]{2,1,0:T(8,128)(2,1)} %bitcast.18.refs_0_), channel_id=1, source_target_pairs={{0,2},{2,0},{1,3},{3,1},{4,6},{6,4},{5,7},{7,5},{8,10},{10,8},{9,1... | collective-permute-start | bytes 3145736 | tf_op jit(solution)/shard_map/ppermute | solution.py:33
  61.2 3.2 %collective-permute-start.13 = (bf16[64,8,1024]{2,1,0:T(8,128)(2,1)}, bf16[64,8,1024]{2,1,0:T(8,128)(2,1)}, u32[]{:S(2)}, u32[]{:S(2)}) collective-permute-start(bf16[64,8,1024]{2,1,0:T(8,128)(2,1)} %collective-permute-done.4.refs_1_), channel_id=1, source_target_pairs={{0,2},{2,0},{1,3},{3,1},{4,6},{6,4},{5,7},{7,5},{8,10},{10,8},{9,1... | collective-permute-start | bytes 3145736 | tf_op jit(solution)/shard_map/ppermute | solution.py:33
  61.3 5.2 %collective-permute-start.14 = (bf16[64,8,1024]{2,1,0:T(8,128)(2,1)}, bf16[64,8,1024]{2,1,0:T(8,128)(2,1)}, u32[]{:S(2)}, u32[]{:S(2)}) collective-permute-start(bf16[64,8,1024]{2,1,0:T(8,128)(2,1)} %collective-permute-done.5.refs_2_), channel_id=1, source_target_pairs={{0,2},{2,0},{1,3},{3,1},{4,6},{6,4},{5,7},{7,5},{8,10},{10,8},{9,1... | collective-permute-start | bytes 3145736 | tf_op jit(solution)/shard_map/ppermute | solution.py:33
  61.8 5.5 %collective-permute-start.15 = (bf16[64,8,1024]{2,1,0:T(8,128)(2,1)}, bf16[64,8,1024]{2,1,0:T(8,128)(2,1)}, u32[]{:S(2)}, u32[]{:S(2)}) collective-permute-start(bf16[64,8,1024]{2,1,0:T(8,128)(2,1)} %collective-permute-done.6.refs_3_), channel_id=1, source_target_pairs={{0,2},{2,0},{1,3},{3,1},{4,6},{6,4},{5,7},{7,5},{8,10},{10,8},{9,1... | collective-permute-start | bytes 3145736 | tf_op jit(solution)/shard_map/ppermute | solution.py:33
  61.8 28.5 %collective-permute-start.11 = (bf16[8,64,1024]{2,1,0:T(8,128)(2,1)}, bf16[8,64,1024]{2,1,0:T(8,128)(2,1)S(1)}, u32[]{:S(2)}, u32[]{:S(2)}) collective-permute-start(bf16[8,64,1024]{2,1,0:T(8,128)(2,1)} %get-tuple-element.60), channel_id=1, source_target_pairs={{0,96},{2,14},{4,100},{6,2},{8,104},{10,6},{12,108},{14,10},{32,0}... | collective-permute-start | bytes 3145736 | tf_op jit(solution)/shard_map/ppermute | solution.py:43
  64.3 26.1 %collective-permute-start.10 = (bf16[8,64,1024]{2,1,0:T(8,128)(2,1)}, bf16[8,64,1024]{2,1,0:T(8,128)(2,1)S(1)}, u32[]{:S(2)}, u32[]{:S(2)}) collective-permute-start(bf16[8,64,1024]{2,1,0:T(8,128)(2,1)} %get-tuple-element.59), channel_id=1, source_target_pairs={{0,64},{2,10},{4,68},{6,14},{8,72},{10,2},{12,76},{14,6},{32,96},{... | collective-permute-start | bytes 3145736 | tf_op jit(solution)/shard_map/ppermute | solution.py:43
  64.3 27.8 %collective-permute-start.9 = (bf16[8,64,1024]{2,1,0:T(8,128)(2,1)}, bf16[8,64,1024]{2,1,0:T(8,128)(2,1)}, u32[]{:S(2)}, u32[]{:S(2)}) collective-permute-start(bf16[8,64,1024]{2,1,0:T(8,128)(2,1)} %get-tuple-element.58), channel_id=1, source_target_pairs={{0,32},{2,6},{4,36},{6,10},{8,40},{10,14},{12,44},{14,2},{32,64},{... | collective-permute-start | bytes 3145736 | tf_op jit(solution)/shard_map/ppermute | solution.py:43
  81.2 10.9 %copy-start.5 = (f32[8,64,1024]{2,1,0:T(8,128)S(1)}, f32[8,64,1024]{2,1,0:T(8,128)}, u32[]{:S(2)}) copy-start(f32[8,64,1024]{2,1,0:T(8,128)} %get-tuple-element.57) | copy-start | bytes 6291460
  95.9 29.8 %collective-permute-start.16 = (f16[1040,512]{1,0:T(8,128)(2,1)S(1)}, f16[1040,512]{1,0:T(8,128)(2,1)S(1)}, u32[]{:S(2)}, u32[]{:S(2)}) collective-permute-start(f16[1040,512]{1,0:T(8,128)(2,1)S(1)} %convert_element_type.46), channel_id=1, source_target_pairs={{0,1},{1,0},{2,3},{3,2},{4,5},{5,4},{6,7},{7,6},{8,9},{9,8},{10,11... | collective-permute-start | bytes 3194888 | tf_op jit(solution)/shard_map/ppermute | solution.py:33
  99.2 11.7 %collective-permute-start.19 = (bf16[2,64,1024]{2,1,0:T(8,128)(2,1)S(1)}, bf16[2,64,1024]{2,1,0:T(8,128)(2,1)S(1)}, u32[]{:S(2)}, u32[]{:S(2)}) collective-permute-start(bf16[2,64,1024]{2,1,0:T(8,128)(2,1)S(1)} %get-tuple-element.73), channel_id=1, source_target_pairs={{0,12},{2,98},{4,0},{6,102},{8,4},{10,106},{12,8},{14,110},{32,44}... | collective-permute-start | bytes 786440 | tf_op jit(solution)/shard_map/ppermute | solution.py:43
  99.2 11.7 %collective-permute-start.18 = (bf16[2,64,1024]{2,1,0:T(8,128)(2,1)S(1)}, bf16[2,64,1024]{2,1,0:T(8,128)(2,1)S(1)}, u32[]{:S(2)}, u32[]{:S(2)}) collective-permute-start(bf16[2,64,1024]{2,1,0:T(8,128)(2,1)S(1)} %get-tuple-element.72), channel_id=1, source_target_pairs={{0,8},{2,66},{4,12},{6,70},{8,0},{10,74},{12,4},{14,78},{32,40},{3... | collective-permute-start | bytes 786440 | tf_op jit(solution)/shard_map/ppermute | solution.py:43
  99.9 11.0 %collective-permute-start.17 = (bf16[2,64,1024]{2,1,0:T(8,128)(2,1)S(1)}, bf16[2,64,1024]{2,1,0:T(8,128)(2,1)S(1)}, u32[]{:S(2)}, u32[]{:S(2)}) collective-permute-start(bf16[2,64,1024]{2,1,0:T(8,128)(2,1)S(1)} %get-tuple-element.71), channel_id=1, source_target_pairs={{0,4},{2,34},{4,8},{6,38},{8,12},{10,42},{12,0},{14,46},{32,36},{3... | collective-permute-start | bytes 786440 | tf_op jit(solution)/shard_map/ppermute | solution.py:43
  111.1 12.6 %collective-permute-start.20 = (bf16[64,1024]{1,0:T(8,128)(2,1)S(1)}, bf16[64,1024]{1,0:T(8,128)(2,1)S(1)}, u32[]{:S(2)}, u32[]{:S(2)}) collective-permute-start(bf16[64,1024]{1,0:T(8,128)(2,1)S(1)} %fusion.2), channel_id=1, source_target_pairs={{0,16},{16,0},{1,17},{17,1},{2,18},{18,2},{3,19},{19,3},{4,20},{20... | collective-permute-start | bytes 393224 | tf_op jit(solution)/shard_map/ppermute | solution.py:33
  (5 other events, 12.4 us)

commit v4 on v3

--- a/solution.py
+++ b/solution.py
@@ -3,6 +3,7 @@
 
 import jax
 import jax.numpy as jnp
+import numpy as np
 from jax import lax
 from jax.experimental import pallas as pl
 from jax.experimental.pallas import tpu as pltpu
@@ -47,120 +48,138 @@
     return [value] + [cross(value, stage, -k) for k in (1, 2, 3)]
 
 
-def reduced(terms, stage):
-    total = terms[0]
-    for k in (1, 2, 3):
-        total = total + cross(terms[k], stage, k).astype(jnp.float32)
-    return total
-
-
-def after(value, *others):
-    return lax.optimization_barrier((value, *others))[0]
+def delivered(terms, stage):
+    return [terms[0]] + [cross(terms[k], stage, k) for k in (1, 2, 3)]
+
+
+def summed(terms):
+    return sum(v.astype(jnp.float32) for v in terms[1:]) + terms[0]
 
 
 ANY = pl.BlockSpec(memory_space=pl.ANY)
 SCALARS = pl.BlockSpec(memory_space=pltpu.SMEM)
-AHEAD = 3
-
-
-def kernel_call(kernel, out_shape, scratch, flops, moved, *args, out_specs=None, in_specs=None):
+AHEAD = 2
+PARTS = 1
+
+
+def kernel_call(kernel, out_shape, scratch, flops, moved, *args, out_specs=None, in_specs=None, vmem=58):
     return pl.pallas_call(
         kernel,
         in_specs=in_specs or [SCALARS] + [ANY] * (len(args) - 1),
         out_specs=out_specs or [ANY] * len(out_shape),
         out_shape=out_shape,
         scratch_shapes=scratch,
-        compiler_params=pltpu.CompilerParams(vmem_limit_bytes=58 * MIB),
+        compiler_params=pltpu.CompilerParams(vmem_limit_bytes=vmem * MIB),
         cost_estimate=pl.CostEstimate(flops=flops, bytes_accessed=moved, transcendentals=0),
     )(*args)
 
 
-def select_kernel(place, tokens, mine, other, held, low, high, in_sem, low_sem, high_sem):
-    z, l, x, c = place[0], place[1], place[2], place[3]
-    blocks, rows, _ = held.shape
+def select_kernel(start, own, place, tokens, *refs):
+    beside, (out, held, made, in_sem, beside_sem, out_sem) = refs[:-6], refs[-6:]
+    z, x = place[0], place[2]
+    core = place[3] if own else 1 - place[3]
+    blocks, rows, half = held.shape
     lanes = NC * SLOT
     below = lax.broadcasted_iota(jnp.int32, (rows, lanes), 1) < SLOT
 
     def load(k):
-        return pltpu.make_async_copy(tokens.at[pl.ds(k * rows, rows)], held.at[k], in_sem.at[k])
+        at = pl.ds(pl.multiple_of(start + k * rows, rows), rows)
+        copies = [pltpu.make_async_copy(tokens.at[at], held.at[k], in_sem.at[k])]
+        for v in beside:
+            into = made.at[k, :, pl.ds(half // NC, v.shape[1])]
+            copies.append(pltpu.make_async_copy(v.at[at], into, beside_sem.at[k]))
+        return copies
 
     def store(k):
-        return (
-            pltpu.make_async_copy(low.at[k], mine.at[pl.ds(k * rows, rows)], low_sem.at[k]),
-            pltpu.make_async_copy(high.at[k], other.at[pl.ds(k * rows, rows)], high_sem.at[k]),
-        )
-
-    def column(k, core, slot):
+        return pltpu.make_async_copy(made.at[k], out.at[pl.ds(k * rows, rows)], out_sem.at[k])
+
+    def column(k, slot):
         first, pair, second = slot // (NL * 4), slot // 4 % NL, slot % 4
         to_z = lax.rem(z + jnp.where(core == 0, first, second), NZ)
         to_x = lax.rem(x + jnp.where(core == 0, second, first), NX)
-        at = (to_z * NL + lax.rem(l + pair, NL)) * NX + to_x
+        at = (to_z * NL + lax.rem(place[1] + pair, NL)) * NX + to_x
         return held[k, :, pl.ds(pl.multiple_of(at * lanes, lanes), lanes)]
 
     for k in range(blocks):
-        load(k).start()
+        for copy in load(k):
+            copy.start()
 
     @pl.loop(0, blocks)
     def _(k):
-        load(k).wait()
-        for core, out in ((c, low), (1 - c, high)):
-            for slot in range(0, COUNT // NC, NC):
-                one = pltpu.roll(column(k, core, slot), SLOT * core, 1)
-                two = pltpu.roll(column(k, core, slot + 1), SLOT * (1 - core), 1)
-                out[k, :, slot * SLOT : (slot + 2) * SLOT] = jnp.where(below, one, two)
-        for copy in store(k):
-            copy.start()
+        for copy in load(k):
+            copy.wait()
+        for slot in range(0, COUNT // NC, NC):
+            one = pltpu.roll(column(k, slot), SLOT * core, 1)
+            two = pltpu.roll(column(k, slot + 1), SLOT * (1 - core), 1)
+            made[k, :, slot * SLOT : (slot + 2) * SLOT] = jnp.where(below, one, two)
+        store(k).start()
 
     for k in range(blocks):
-        for copy in store(k):
-            copy.wait()
-
-
-def selected(place, tokens):
+        store(k).wait()
+
+
+def selected(place, tokens, own, part, parts, *beside):
     rows, half = tokens.shape
-    blocks = 8
-    out = jax.ShapeDtypeStruct((rows, half // NC), tokens.dtype)
-    part = pltpu.VMEM((blocks, rows // blocks, half // NC), tokens.dtype)
-    sems = pltpu.SemaphoreType.DMA((blocks,))
-    scratch = [pltpu.VMEM((blocks, rows // blocks, half), tokens.dtype), part, part, sems, sems, sems]
-    return kernel_call(select_kernel, [out, out], scratch, 0, 4 * rows * half, place, tokens)
-
-
-def grad_kernel(mine, theirs, cot, cot_theirs, *refs):
+    rows //= parts
+    blocks = 8 // parts
+    size = half // NC + sum(v.shape[1] for v in beside)
+    scratch = [pltpu.VMEM((blocks, rows // blocks, n), tokens.dtype) for n in (half, size)]
+    scratch += [pltpu.SemaphoreType.DMA((blocks,))] * 3
+    kernel = functools.partial(select_kernel, part * rows, own)
+    out = jax.ShapeDtypeStruct((rows, size), tokens.dtype)
+    return kernel_call(kernel, out, scratch, 0, 2 * rows * half, place, tokens, *beside, out_specs=ANY)
+
+
+def grad_kernel(mine, cot, *refs):
+    theirs, refs = refs[:PARTS], refs[PARTS:]
     outs, refs = refs[:4], refs[4:]
     held, held_theirs, cots, own, sends, in_sem, theirs_sem, cot_sem, out_sem = refs
     blocks, _, block = held.shape
+    rows = theirs[0].shape[0]
+    parts = [pl.ds(p * rows, rows) for p in range(PARTS)]
 
     def load(k):
         at = pl.ds(pl.multiple_of(k * block, block), block)
-        return (
-            pltpu.make_async_copy(mine.at[:, at], held.at[k], in_sem.at[k]),
-            pltpu.make_async_copy(theirs.at[:, at], held_theirs.at[k], theirs_sem.at[k]),
-        )
+        return [pltpu.make_async_copy(mine.at[:, at], held.at[k], in_sem.at[k])], [
+            pltpu.make_async_copy(v.at[:, at], held_theirs.at[k, part], theirs_sem.at[k, p])
+            for p, (v, part) in enumerate(zip(theirs, parts))
+        ]
 
     def store(k):
         return pltpu.make_async_copy(own if k == 0 else sends.at[k - 1], outs[k], out_sem.at[k])
 
-    both = [pltpu.make_async_copy(v, cots.at[n], cot_sem.at[n]) for n, v in enumerate((cot, cot_theirs))]
-    first, second = load(0)
-    both[0].start()
-    first.start()
-    both[1].start()
-    second.start()
-    for k in range(1, blocks):
-        for copy in load(k):
+    beside = pl.ds(blocks * block, cot.shape[1])
+    cot_copies = [pltpu.make_async_copy(cot, cots.at[0], cot_sem.at[0])], [
+        pltpu.make_async_copy(v.at[:, beside], cots.at[1, part], cot_sem.at[1 + p])
+        for p, (v, part) in enumerate(zip(theirs, parts))
+    ]
+
+    def start(copies):
+        for copy in copies:
             copy.start()
 
+    def wait(copies):
+        for copy in copies:
+            copy.wait()
+
+    for n, copies in enumerate(load(0)):
+        start(cot_copies[n])
+        start(copies)
     over = (((0,), (0,)), ((), ()))
 
     @pl.loop(0, blocks)
     def _(k):
+        @pl.when(k + 1 < blocks)
+        def _():
+            for copies in load(k + 1):
+                start(copies)
+
         one, two = load(k)
-        pl.when(k == 0)(both[0].wait)
-        one.wait()
+        pl.when(k == 0)(lambda: wait(cot_copies[0]))
+        wait(one)
         term = lax.dot_general(held[k], cots[0], over, preferred_element_type=jnp.float32)
-        pl.when(k == 0)(both[1].wait)
-        two.wait()
+        pl.when(k == 0)(lambda: wait(cot_copies[1]))
+        wait(two)
         term += lax.dot_general(held_theirs[k], cots[1], over, preferred_element_type=jnp.float32)
         term = term.reshape(own.shape)
 
@@ -180,7 +199,7 @@
         store(k).wait()
 
 
-def chip_grad(mine, theirs, cotangent, cotangent_theirs):
+def chip_grad(mine, theirs, cotangent):
     rows, half = mine.shape
     width = cotangent.shape[1]
     piece = (half // 4 // SLOT, SLOT, width)
@@ -193,8 +212,8 @@
         pltpu.VMEM(piece, jnp.float32),
         pltpu.VMEM((3, *piece), jnp.bfloat16),
         sems,
-        sems,
-        pltpu.SemaphoreType.DMA((2,)),
+        pltpu.SemaphoreType.DMA((4, PARTS)),
+        pltpu.SemaphoreType.DMA((1 + PARTS,)),
         sems,
     ]
     out_shape = [jax.ShapeDtypeStruct(piece, jnp.bfloat16 if n else jnp.float32) for n in range(4)]
@@ -205,16 +224,15 @@
         0,
         0,
         mine,
-        theirs,
         cotangent,
-        cotangent_theirs,
-        in_specs=[ANY] * 4,
+        *theirs,
+        in_specs=[ANY] * (2 + PARTS),
     )
 
 
 def reorder_kernel(place, target, tokens, *refs):
     pieces, refs = refs[: COUNT // 8], refs[COUNT // 8 :]
-    full, keys_send, held, rows_in, moved, even, odd, acc, tokens_sem, rows_sem, full_sem = refs
+    full, keys_send, keys_keep, base, held, rows_in, moved, even, odd, acc, tokens_sem, rows_sem, full_sem, base_sem = refs
     t = place[4]
     octets, _, block = held.shape
     lines = rows_in.shape[2]
@@ -243,6 +261,7 @@
         for copy in load(o):
             copy.start()
     acc[...] = jnp.zeros_like(acc)
+    keys_keep[...] = jnp.zeros_like(keys_keep)
     size, each = block // NG, lines // NG
 
     def arrive(o):
@@ -270,10 +289,14 @@
             halves = [out[:, h * column : (h + 1) * column] for h in range(NT)]
             for h in range(NT):
                 moved[h, at] = halves[h]
-            stage[group * size : (group + 1) * size] = jnp.where(t == 0, halves[1], halves[0])
+            at = slice(group * size, (group + 1) * size)
+            stage[at, :column] = jnp.where(t == 0, halves[0], halves[1])
+            stage[at, column:] = jnp.where(t == 0, halves[1], halves[0])
 
     def multiply(o, stage):
-        acc[...] += jnp.dot(held[o], stage[...], preferred_element_type=jnp.float32)
+        term = jnp.dot(held[o], stage[...], preferred_element_type=jnp.float32)
+        keys_keep[...] += term[:, :column]
+        acc[...] += term[:, column:]
 
     def leave(o):
         for copy in store(o):
@@ -300,18 +323,31 @@
     reorder(octets - 1, odd)
     multiply(octets - 2, even)
     leave(octets - 1)
+    me = ((place[0] * NL + place[1]) * NX + place[2]) * NC + place[3]
+    own = [
+        pltpu.make_async_copy(
+            moved.at[h, pl.ds(pl.multiple_of(me * SLOT, SLOT), SLOT)],
+            base.at[:, pl.ds(h * column, column)],
+            base_sem.at[h],
+        )
+        for h in range(NT)
+    ]
+    for copy in own:
+        copy.start()
     multiply(octets - 1, odd)
     power = jnp.floor(jnp.log2(jnp.clip(jnp.full((8, 128), jnp.max(jnp.abs(acc[...]))), 1e-30, None)))
     count = acc.shape[0]
     keys_send[:count] = acc[...] * jnp.exp2(TOP - power)[:1, :1]
     keys_send[count:] = jnp.broadcast_to(power[:1, :1], (keys_send.shape[0] - count, column))
 
+    for copy in own:
+        copy.wait()
     for o in range(octets):
         for copy in store(o):
             copy.wait()
 
 
-def reorder_and_send(place, target, tokens, pieces):
+def reorder_and_keys(place, target, tokens, pieces):
     rows, half = tokens.shape
     width = pieces[0].shape[-1]
     octets = target.shape[0] // NG
@@ -321,12 +357,13 @@
         pltpu.VMEM((octets, rows, block), tokens.dtype),
         pltpu.VMEM((octets, len(pieces), lines // octets, line, width), tokens.dtype),
         pltpu.VMEM((NT, half, width // NT), tokens.dtype),
-        pltpu.VMEM((block, width // NT), tokens.dtype),
-        pltpu.VMEM((block, width // NT), tokens.dtype),
+        pltpu.VMEM((block, width), tokens.dtype),
+        pltpu.VMEM((block, width), tokens.dtype),
         pltpu.VMEM((rows, width // NT), jnp.float32),
         pltpu.SemaphoreType.DMA((octets,)),
         pltpu.SemaphoreType.DMA((octets, len(pieces))),
         pltpu.SemaphoreType.DMA((octets, NT)),
+        pltpu.SemaphoreType.DMA((NT,)),
     ]
     vmem = pl.BlockSpec(memory_space=pltpu.VMEM)
     return kernel_call(
@@ -334,65 +371,19 @@
         [
             jax.ShapeDtypeStruct((half, width), jnp.bfloat16),
             jax.ShapeDtypeStruct((rows + CODE, width // NT), jnp.float32),
+            jax.ShapeDtypeStruct((rows, width // NT), jnp.float32),
+            jax.ShapeDtypeStruct((SLOT, width), jnp.bfloat16),
         ],
         scratch,
-        2 * rows * half * width,
+        3 * rows * half * width,
         rows * half * 2 + half * width * 4,
         place,
         target,
         tokens,
         *pieces,
         in_specs=[SCALARS, vmem] + [ANY] * (1 + len(pieces)),
-        out_specs=[ANY, vmem],
-    )
-
-
-def keep_kernel(place, tokens, full, keys, held, part, tokens_sem, part_sem):
-    t = place[4]
-    blocks, _, block = held.shape
-    column = part.shape[2]
-
-    def load(o):
-        at = pl.ds(pl.multiple_of(o * block, block), block)
-        return (
-            pltpu.make_async_copy(
-                full.at[at, pl.ds(pl.multiple_of(t * column, column), column)], part.at[o], part_sem.at[o]
-            ),
-            pltpu.make_async_copy(tokens.at[:, at], held.at[o], tokens_sem.at[o]),
-        )
-
-    for o in range(blocks):
-        for copy in load(o):
-            copy.start()
-    keys[...] = jnp.zeros_like(keys)
-
-    @pl.loop(0, blocks)
-    def _(o):
-        for copy in load(o):
-            copy.wait()
-        keys[...] += jnp.dot(held[o], part[o], preferred_element_type=jnp.float32)
-
-
-def keys_kept(place, tokens, full):
-    rows, half = tokens.shape
-    width = full.shape[1]
-    blocks = 4
-    sems = pltpu.SemaphoreType.DMA((blocks,))
-    return kernel_call(
-        keep_kernel,
-        jax.ShapeDtypeStruct((rows, width // NT), jnp.float32),
-        [
-            pltpu.VMEM((blocks, rows, half // blocks), tokens.dtype),
-            pltpu.VMEM((blocks, half // blocks, width // NT), tokens.dtype),
-            sems,
-            sems,
-        ],
-        0,
-        0,
-        place,
-        tokens,
-        full,
-        out_specs=pl.BlockSpec(memory_space=pltpu.VMEM),
+        out_specs=[ANY, vmem, vmem, ANY],
+        vmem=50,
     )
 
 
@@ -410,12 +401,15 @@
 
     whole = pltpu.make_async_copy(cotangent, cot, cot_sem)
     whole.start()
-    for o in range(blocks):
-        load(o).start()
+    load(0).start()
     whole.wait()
 
     @pl.loop(0, blocks)
     def _(o):
+        @pl.when(o + 1 < blocks)
+        def _():
+            load(o + 1).start()
+
         load(o).wait()
         out[o] = lax.dot_general(
             cot[...], held[o], (((1,), (1,)), ((), ())), preferred_element_type=jnp.float32
@@ -454,8 +448,8 @@
 
 
 def decoded(came):
-    value = came.astype(jnp.float32)
-    return value[:-CODE] * jnp.exp2(value[-CODE : 1 - CODE] - TOP)
+    power = came[-CODE : 1 - CODE].astype(jnp.float32)
+    return came[:-CODE].astype(jnp.float32) * jnp.exp2(power - TOP)
 
 
 def pack_kernel(first, second, out):
@@ -517,18 +511,24 @@
     )(source, moments, own, came, base)
 
 
-def targets(landing, place, rows):
-    z, l, x, c = place[0], place[1], place[2], place[3]
-    steps = jnp.arange(4, dtype=jnp.int32)
-    zs, xs = (z + steps) % NZ, (x + steps) % NX
-    ls = (l + jnp.arange(NL, dtype=jnp.int32)) % NL
-
-    def owners(core):
-        along_z = (zs[None, :, None] * NL + ls) * NX + xs[:, None, None]
-        along_x = (zs[:, None, None] * NL + ls) * NX + xs[None, :, None]
-        return (jnp.where(core == 0, along_z, along_x) * NC + core).reshape(-1)
-
-    order = jnp.concatenate([owners(c), owners(1 - c)])
+def gather_orders():
+    orders = []
+    for me in range(COUNT):
+        z, l, x, c = me // (NL * NX * NC), me // (NX * NC) % NL, me // NC % NX, me % NC
+        order = []
+        for core in (c, 1 - c):
+            for second in range(4):
+                for first in range(4):
+                    dz, dx = (first, second) if core == 0 else (second, first)
+                    for pair in range(NL):
+                        to = (((z + dz) % NZ) * NL + (l + pair) % NL) * NX + (x + dx) % NX
+                        order.append(to * NC + core)
+        orders.append(order)
+    return np.array(orders, np.int32)
+
+
+def targets(landing, me, rows):
+    order = lax.dynamic_slice_in_dim(jnp.asarray(gather_orders()), me, 1, 0)[0]
     groups = 8 * NG
     each = COUNT // groups
     spots = jnp.take(landing, order, axis=0).reshape(COUNT // (4 * NL), 4 * NL, groups, each)
@@ -546,35 +546,37 @@
     own = old_weight.reshape(rows, width)
     pair = jnp.stack([own, shift(own, "l", 1)])
     moments = packed(old_first.reshape(rows, width), old_second.reshape(rows, width))
-    target = targets(landing, place, rows)
+    target = targets(landing, me, rows)
     pair, moments, target, place_1 = lax.optimization_barrier((pair, moments, target, place))
     line = jnp.stack(gathered(pair, 0)).reshape(4 * NL, rows, width)
-    mine, other = selected(place_1, tokens)
-    line, mine, other, cotangent_1, moments = lax.optimization_barrier((line, mine, other, cotangent, moments))
+    other = selected(place_1, tokens, False, 0, PARTS, cotangent)
+    line, other, place_2 = lax.optimization_barrier((line, other, place_1))
     theirs = shift(other, "c", 1)
-    cotangent_theirs = shift(cotangent_1, "c", 1)
     line = line.transpose(1, 0, 2)
     here = gathered(line, 1)
     there = shift(line, "c", 1)
+    mine = selected(place_2, tokens, True, 0, 1)
+    terms = chip_grad(mine, (theirs,), cotangent)
+    here, there, terms, moments = lax.optimization_barrier((here, there, terms, moments))
     moments = lax.all_to_all(moments, DP, split_axis=0, concat_axis=0, tiled=True)
-    terms = chip_grad(mine, theirs, cotangent, cotangent_theirs)
-    here, terms, moments = lax.optimization_barrier((here, terms, moments))
     pieces = here + [there] + [shift(v, "c", 1) for v in here[1:]]
-
-    total = reduced(terms, 0).reshape(NL, 4, rows, width)
-    full, keys_send = reorder_and_send(place, target, tokens, pieces)
+    pieces, terms = lax.optimization_barrier((pieces, terms))
+
+    terms = delivered(terms, 0)
+    full, keys_send, keys_keep, base = reorder_and_keys(place, target, tokens, pieces)
     keys_came = shift(keys_send.astype(jnp.float16), "t", 1)
-    keys_keep = keys_kept(place, tokens, full)
-    total, keys_keep = lax.optimization_barrier((total, keys_keep))
+    terms, keys_keep, moments = lax.optimization_barrier((terms, keys_keep, moments))
+    total = summed(terms).reshape(NL, 4, rows, width)
     terms = [total[:, 0]] + [total[:, k].astype(jnp.bfloat16) for k in (1, 2, 3)]
     terms, full_1 = lax.optimization_barrier((terms, full))
-    total = reduced(terms, 1)
+    terms = delivered(terms, 1)
     back = back_part(cotangent, full_1, 0, 4)
-    total, back = lax.optimization_barrier((total, back))
+    terms, back = lax.optimization_barrier((terms, back))
+    total = summed(terms)
     came = shift(total[1].astype(jnp.bfloat16), "l", 1)
     back = back_part(cotangent, full, 4, 8, (back,))
-
-    base = lax.dynamic_slice_in_dim(full, me * rows, rows, 0)
+    came, keys_came, back = lax.optimization_barrier((came, keys_came, back))
+
     column = lax.dynamic_slice_in_dim(landing, me, 1, 1)[:, 0]
     lanes = jnp.arange(COUNT, dtype=jnp.int32)
     source = jnp.sum(jnp.where(column[None, :] == lanes[:, None], lanes[None, :], 0), axis=1, dtype=jnp.int32)

time: 128 us -> 125 us (0.977)
  waiting for transfers between devices: 16.1 us -> 6.18 us
  other arithmetic: 4.93 us -> 10.1 us
  starting transfers between devices: 29.4 us -> 33.3 us
  local copies, waits for them, and re-layouts: 7.26 us -> 3.64 us
    all_to_all x1, waiting for transfers between devices: 10.8 us -> 0.01 us  [shards(): lax.all_to_all(moments, DP, split_axis=0, concat_axis=0, tiled=True)]
    ppermute x12, starting transfers between devices: 16.7 us -> 21.7 us  [cross(): return lax.ppermute(value, ('z', 'x', 'c'), pairs)]
    ppermute x12, waiting for transfers between devices: 1.72 us -> 5.98 us  [cross(): return lax.ppermute(value, ('z', 'x', 'c'), pairs)]
    ppermute x9 -> x8, waiting for transfers between devices: 3.55 us -> 0.2 us  [shift(): lax.ppermute(value, axis, [(i, (i + step) % size) for i in range(size)])]
    convert_element_type x1, other arithmetic: 0.26 us -> 2.99 us  [shards(): keys_came = shift(keys_send.astype(jnp.float16), 't', 1)]
    pallas_call x4, Pallas kernels: 47.2 us -> 48.6 us  [kernel_call(): pl.pallas_call(kernel, in_specs=in_specs or [SCALARS] + [ANY] * (len(args...]
    unnamed x15 -> x14, local copies, waits for them, and re-layouts: 1.56 us -> 0.23 us
    add x4 -> x2, other arithmetic: 2.2 us -> 2.74 us  [summed(): return sum((v.astype(jnp.float32) for v in terms[1:])) + terms[0]]
  transfers between devices with their start and end apart: 22 -> 21, of which waited for: 4 -> 4; matrix products, arithmetic and copies ran while one was open for 4% -> 8% of each run, Pallas kernels for 54% -> 55%
where the time goes in v4:
time: 125 us; the launch traced here: 124 us
  Pallas kernels  69.7 us (56%)
  starting transfers between devices  33.3 us (27%)
  other arithmetic  10.1 us (8%)
  waiting for transfers between devices  6.18 us (5%)
  local copies, waits for them, and re-layouts  3.64 us (3%)
    pallas_call x4, Pallas kernels, kernel_call(): pl.pallas_call(kernel, in_specs=in_specs or [SCALARS] + [ANY] * (len(args...  48.6 us
    ppermute x12, starting transfers between devices, cross(): return lax.ppermute(value, ('z', 'x', 'c'), pairs)  21.7 us
    pallas_call x2, Pallas kernels, back_part(): pl.pallas_call(functools.partial(back_kernel, first), in_specs=[ANY] * (2...  16.9 us
    ppermute x8, starting transfers between devices, shift(): lax.ppermute(value, axis, [(i, (i + step) % size) for i in range(size)])  6.92 us
    ppermute x12, waiting for transfers between devices, cross(): return lax.ppermute(value, ('z', 'x', 'c'), pairs)  5.98 us
    all_to_all x1, starting transfers between devices, shards(): lax.all_to_all(moments, DP, split_axis=0, concat_axis=0, tiled=True)  4.64 us
    convert_element_type x1, other arithmetic, shards(): keys_came = shift(keys_send.astype(jnp.float16), 't', 1)  2.99 us
    add x2, other arithmetic, summed(): return sum((v.astype(jnp.float32) for v in terms[1:])) + terms[0]  2.74 us
  transfers between devices with their start and end apart: 21, of which 4 were waited for; matrix products, arithmetic and copies ran while one was open for 8% of the time, Pallas kernels for 55%

profile of v4, /device:TPU:0, one launch (start us, length us, event | category | flops | bytes accessed | tf_op | source)
XLA Modules:
  0.0 123.8 jit_solution(4209759864376147821)
XLA Ops:
  0.7 1.7 %collective-permute-start = (bf16[64,1024]{1,0:T(8,128)(2,1)}, bf16[64,1024]{1,0:T(8,128)(2,1)S(1)}, u32[]{:S(2)}, u32[]{:S(2)}) collective-permute-start(bf16[64,1024]{1,0:T(8,128)(2,1)} %bitcast.56), channel_id=1, source_target_pairs={{0,16},{16,0},{1,17},{17,1},{2,18},{18,2},{3,19},{19,3},{4,20},{20... | collective-permute-start | bytes 393224 | tf_op jit(solution)/shard_map/ppermute | solution.py:34
  5.0 2.2 %shard_map.110 = f32[64,16,128]{2,1,0:T(8,128)} custom-call(f32[64,1024]{1,0:T(8,128)} %bitcast.51, f32[64,1024]{1,0:T(8,128)} %bitcast.52), custom_call_target="tpu_custom_call" | custom-call | bytes 1048576 | tf_op jit(solution)/shard_map/pallas_call | solution.py:463
  7.8 2.0 %collective-permute-start.3 = (bf16[2,64,1024]{2,1,0:T(8,128)(2,1)S(1)}, bf16[2,64,1024]{2,1,0:T(8,128)(2,1)S(1)}, u32[]{:S(2)}, u32[]{:S(2)}) collective-permute-start(bf16[2,64,1024]{2,1,0:T(8,128)(2,1)S(1)} %pad_maximum_fusion.1), channel_id=1, source_target_pairs={{0,32},{2,6},{4,36},{6,10},{8,40},{10,14},{12,44},{14,2},{32,64},{... | collective-permute-start | bytes 786440 | tf_op jit(solution)/shard_map/ppermute | solution.py:44
  9.8 3.6 %collective-permute-start.2 = (bf16[2,64,1024]{2,1,0:T(8,128)(2,1)S(1)}, bf16[2,64,1024]{2,1,0:T(8,128)(2,1)S(1)}, u32[]{:S(2)}, u32[]{:S(2)}) collective-permute-start(bf16[2,64,1024]{2,1,0:T(8,128)(2,1)S(1)} %pad_maximum_fusion.1), channel_id=1, source_target_pairs={{0,64},{2,10},{4,68},{6,14},{8,72},{10,2},{12,76},{14,6},{32,96},{... | collective-permute-start | bytes 786440 | tf_op jit(solution)/shard_map/ppermute | solution.py:44
  14.4 7.5 %shard_map.111 = bf16[1024,3072]{1,0:T(8,128)(2,1)} custom-call(s32[5]{0:T(128)} %stack.46.place, bf16[1024,4096]{1,0:T(8,128)(2,1)} %tokens.5, bf16[1024,1024]{1,0:T(8,128)(2,1)} %cotangent.3), custom_call_target="tpu_custom_call" | custom-call | bytes 8388608 | tf_op jit(solution)/shard_map/pallas_call | solution.py:66
  22.7 2.8 %collective-permute-start.4 = (bf16[64,8,1024]{2,1,0:T(8,128)(2,1)S(1)}, bf16[64,8,1024]{2,1,0:T(8,128)(2,1)S(1)}, u32[]{:S(2)}, u32[]{:S(2)}) collective-permute-start(bf16[64,8,1024]{2,1,0:T(8,128)(2,1)S(1)} %bitcast.41), channel_id=1, source_target_pairs={{0,12},{2,98},{4,0},{6,102},{8,4},{10,106},{12,8},{14,110},{32,44}... | collective-permute-start | bytes 3145736 | tf_op jit(solution)/shard_map/ppermute | solution.py:44
  27.3 6.4 %shard_map.112.mine = bf16[1024,2048]{1,0:T(8,128)(2,1)} custom-call(s32[5]{0:T(128)} %stack.46.place, bf16[1024,4096]{1,0:T(8,128)(2,1)} %tokens.5), custom_call_target="tpu_custom_call" | custom-call | bytes 8388608 | tf_op jit(solution)/shard_map/pallas_call | solution.py:66
  33.7 14.4 %shard_map.113 = (f32[8,64,1024]{2,1,0:T(8,128)}, bf16[8,64,1024]{2,1,0:T(8,128)(2,1)}, bf16[8,64,1024]{2,1,0:T(8,128)(2,1)}, bf16[8,64,1024]{2,1,0:T(8,128)(2,1)}) custom-call(bf16[1024,2048]{1,0:T(8,128)(2,1)} %shard_map.112.mine, bf16[1024,1024]{1,0:T(8,128)(2,1)} %cotangent.3, bf16[1024,3072]{1,0:T(8,128)(2,1)} %collective-permute-done.8.refs_0_), custom_call_target="tpu_custom_call" | custom-call | tf_op jit(solution)/shard_map/pallas_call | solution.py:66
  49.2 4.1 %collective-permute-done.6.refs_3_ = bf16[64,8,1024]{2,1,0:T(8,128)(2,1)} collective-permute-done((bf16[64,8,1024]{2,1,0:T(8,128)(2,1)S(1)}, bf16[64,8,1024]{2,1,0:T(8,128)(2,1)}, u32[]{:S(2)}, u32[]{:S(2)}) %collective-permute-start.6) | collective-permute-done | bytes 1048608 | tf_op jit(solution)/shard_map/ppermute | solution.py:44
  54.4 4.6 %all-to-all-start = ((f32[64,16,128]{2,1,0:T(8,128)}), f32[64,16,128]{2,1,0:T(8,128)S(1)}, u32[]{:S(2)}, u32[]{:S(2)}) async-start(f32[64,16,128]{2,1,0:T(8,128)} %shard_map.110), calls=%async_computation | async-start | bytes 1048576 | tf_op jit(solution)/shard_map/all_to_all | solution.py:561
  59.2 1.5 %collective-permute-start.12 = (bf16[8,64,1024]{2,1,0:T(8,128)(2,1)}, bf16[8,64,1024]{2,1,0:T(8,128)(2,1)}, u32[]{:S(2)}, u32[]{:S(2)}) collective-permute-start(bf16[8,64,1024]{2,1,0:T(8,128)(2,1)} %get-tuple-element.84), channel_id=1, source_target_pairs={{0,32},{2,6},{4,36},{6,10},{8,40},{10,14},{12,44},{14,2},{32,64},{... | collective-permute-start | bytes 3145736 | tf_op jit(solution)/shard_map/ppermute | solution.py:44
  60.7 2.9 %collective-permute-start.13 = (bf16[8,64,1024]{2,1,0:T(8,128)(2,1)}, bf16[8,64,1024]{2,1,0:T(8,128)(2,1)}, u32[]{:S(2)}, u32[]{:S(2)}) collective-permute-start(bf16[8,64,1024]{2,1,0:T(8,128)(2,1)} %get-tuple-element.85), channel_id=1, source_target_pairs={{0,64},{2,10},{4,68},{6,14},{8,72},{10,2},{12,76},{14,6},{32,96},{... | collective-permute-start | bytes 3145736 | tf_op jit(solution)/shard_map/ppermute | solution.py:44
  63.6 1.4 %collective-permute-start.14 = (bf16[8,64,1024]{2,1,0:T(8,128)(2,1)}, bf16[8,64,1024]{2,1,0:T(8,128)(2,1)}, u32[]{:S(2)}, u32[]{:S(2)}) collective-permute-start(bf16[8,64,1024]{2,1,0:T(8,128)(2,1)} %get-tuple-element.86), channel_id=1, source_target_pairs={{0,96},{2,14},{4,100},{6,2},{8,104},{10,6},{12,108},{14,10},{32,0}... | collective-permute-start | bytes 3145736 | tf_op jit(solution)/shard_map/ppermute | solution.py:44
  64.9 20.4 %shard_map.114 = (bf16[4096,1024]{1,0:T(8,128)(2,1)}, f32[1040,512]{1,0:T(8,128)}, f32[1024,512]{1,0:T(8,128)}, bf16[64,1024]{1,0:T(8,128)(2,1)S(1)}) custom-call(s32[5]{0:T(128)S(1)} %copy-done.2, s32[16,1,256]{2,1,0:T(1,128)S(1)} %copy.24.target, bf16[1024,4096]{1,0:T(8,128)(2,1)} %tokens.5, bf16[64,8,1024]{2,1,0:T(8,128)(2,1)S(1)} %bitcast.45, ...), custom_call_target="tpu_custom_call" | custom-call | flops 12884901888 | bytes 25165824 | tf_op jit(solution)/shard_map/pallas_call | solution.py:66
  85.3 3.0 %convert_element_type.56 = f16[1040,512]{1,0:T(8,128)(2,1)} convert(f32[1040,512]{1,0:T(8,128)} %get-tuple-element.113) | non-fusion elementwise | flops 532480 | bytes 3194880 | tf_op jit(solution)/shard_map/convert_element_type | solution.py:567
  88.3 2.9 %collective-permute-start.19 = (f16[1040,512]{1,0:T(8,128)(2,1)}, f16[1040,512]{1,0:T(8,128)(2,1)}, u32[]{:S(2)}, u32[]{:S(2)}) collective-permute-start(f16[1040,512]{1,0:T(8,128)(2,1)} %convert_element_type.56), channel_id=1, source_target_pairs={{0,1},{1,0},{2,3},{3,2},{4,5},{5,4},{6,7},{7,6},{8,9},{9,8},{10,11... | collective-permute-start | bytes 3194888 | tf_op jit(solution)/shard_map/ppermute | solution.py:34
  92.1 2.6 %add_add_fusion = f32[8,64,1024]{2,1,0:T(8,128)S(1)} fusion(f32[8,64,1024]{2,1,0:T(8,128)S(1)} %copy-done.3, bf16[8,64,1024]{2,1,0:T(8,128)(2,1)} %collective-permute-done.14, bf16[8,64,1024]{2,1,0:T(8,128)(2,1)} %collective-permute-done.13, bf16[8,64,1024]{2,1,0:T(8,128)(2,1)} %collective-permute-done.12), kind=kLoop, calls=%fused_computation.2 | loop fusion | flops 3145728 | bytes 7340032 | tf_op jit(solution)/shard_map/add | solution.py:56
  95.8 2.6 %collective-permute-start.16 = (bf16[2,64,1024]{2,1,0:T(8,128)(2,1)S(1)}, bf16[2,64,1024]{2,1,0:T(8,128)(2,1)S(1)}, u32[]{:S(2)}, u32[]{:S(2)}) collective-permute-start(bf16[2,64,1024]{2,1,0:T(8,128)(2,1)S(1)} %get-tuple-element.106), channel_id=1, source_target_pairs={{0,8},{2,66},{4,12},{6,70},{8,0},{10,74},{12,4},{14,78},{32,40},{3... | collective-permute-start | bytes 786440 | tf_op jit(solution)/shard_map/ppermute | solution.py:44
  98.4 1.4 %collective-permute-start.17 = (bf16[2,64,1024]{2,1,0:T(8,128)(2,1)S(1)}, bf16[2,64,1024]{2,1,0:T(8,128)(2,1)S(1)}, u32[]{:S(2)}, u32[]{:S(2)}) collective-permute-start(bf16[2,64,1024]{2,1,0:T(8,128)(2,1)S(1)} %get-tuple-element.107), channel_id=1, source_target_pairs={{0,12},{2,98},{4,0},{6,102},{8,4},{10,106},{12,8},{14,110},{32,44}... | collective-permute-start | bytes 786440 | tf_op jit(solution)/shard_map/ppermute | solution.py:44
  99.8 8.4 %shard_map.115.refs_0_ = bf16[1024,4096]{1,0:T(8,128)(2,1)} custom-call(bf16[1024,1024]{1,0:T(8,128)(2,1)} %cotangent.3, bf16[4096,1024]{1,0:T(8,128)(2,1)} %get-tuple-element.108.full), custom_call_target="tpu_custom_call" | custom-call | flops 4294967296 | tf_op jit(solution)/shard_map/pallas_call | solution.py:429
  108.4 1.6 %collective-permute-start.18 = (bf16[64,1024]{1,0:T(8,128)(2,1)S(1)}, bf16[64,1024]{1,0:T(8,128)(2,1)S(1)}, u32[]{:S(2)}, u32[]{:S(2)}) collective-permute-start(bf16[64,1024]{1,0:T(8,128)(2,1)S(1)} %fusion), channel_id=1, source_target_pairs={{0,16},{16,0},{1,17},{17,1},{2,18},{18,2},{3,19},{19,3},{4,20},{20... | collective-permute-start | bytes 393224 | tf_op jit(solution)/shard_map/ppermute | solution.py:34
  110.0 8.4 %shard_map.116 = bf16[1024,4096]{1,0:T(8,128)(2,1)} custom-call(bf16[1024,1024]{1,0:T(8,128)(2,1)} %cotangent.3, bf16[4096,1024]{1,0:T(8,128)(2,1)} %get-tuple-element.108.full, bf16[1024,4096]{1,0:T(8,128)(2,1)} %shard_map.115.refs_0_), custom_call_target="tpu_custom_call", output_to_operand_aliasing={{}: (2, {})} | custom-call | flops 4294967296 | tf_op jit(solution)/shard_map/pallas_call | solution.py:429
  119.3 2.5 %add_convert_fusion = bf16[1024,512]{1,0:T(8,128)(2,1)} fusion(f32[1024,512]{1,0:T(8,128)S(1)} %copy-done.4, f32[512]{0:T(512)S(1)} %bitcast.58, f16[1040,512]{1,0:T(8,128)(2,1)} %collective-permute-done.19), kind=kLoop, calls=%fused_computation.1 | loop fusion | flops 2097152 | bytes 4196352 | tf_op jit(solution)/shard_map/convert_element_type | solution.py:584
  121.8 2.0 %shard_map.117 = (bf16[64,1024]{1,0:T(8,128)(2,1)}, f32[64,1024]{1,0:T(8,128)}, f32[64,1024]{1,0:T(8,128)}) custom-call(s32[64]{0:T(128)S(1)} %select_reduce_fusion.source, f32[64,16,128]{2,1,0:T(8,128)S(1)} %all-to-all-done.moments, f32[64,1024]{1,0:T(8,128)S(1)} %slice_bitcast_fusion.1.own, bf16[64,1024]{1,0:T(8,128)(2,1)S(1)} %collective-permute-done.18.came, ...), custom_call_target="tpu_custom_call" | custom-call | bytes 1048576 | tf_op jit(solution)/shard_map/pallas_call | solution.py:494
  (67 shorter events, 12.0 us)
Async XLA Ops:
  0.6 7.1 %copy-start.5 = (bf16[1,64,1024]{2,1,0:T(8,128)(2,1)S(1)}, bf16[1,64,1024]{2,1,0:T(8,128)(2,1)}, u32[]{:S(2)}) copy-start(bf16[1,64,1024]{2,1,0:T(8,128)(2,1)} %param.9) | copy-start | bytes 393220
  0.7 7.1 %collective-permute-start = (bf16[64,1024]{1,0:T(8,128)(2,1)}, bf16[64,1024]{1,0:T(8,128)(2,1)S(1)}, u32[]{:S(2)}, u32[]{:S(2)}) collective-permute-start(bf16[64,1024]{1,0:T(8,128)(2,1)} %bitcast.56), channel_id=1, source_target_pairs={{0,16},{16,0},{1,17},{17,1},{2,18},{18,2},{3,19},{19,3},{4,20},{20... | collective-permute-start | bytes 393224 | tf_op jit(solution)/shard_map/ppermute | solution.py:34
  7.8 14.1 %collective-permute-start.3 = (bf16[2,64,1024]{2,1,0:T(8,128)(2,1)S(1)}, bf16[2,64,1024]{2,1,0:T(8,128)(2,1)S(1)}, u32[]{:S(2)}, u32[]{:S(2)}) collective-permute-start(bf16[2,64,1024]{2,1,0:T(8,128)(2,1)S(1)} %pad_maximum_fusion.1), channel_id=1, source_target_pairs={{0,32},{2,6},{4,36},{6,10},{8,40},{10,14},{12,44},{14,2},{32,64},{... | collective-permute-start | bytes 786440 | tf_op jit(solution)/shard_map/ppermute | solution.py:44
  9.8 12.1 %collective-permute-start.2 = (bf16[2,64,1024]{2,1,0:T(8,128)(2,1)S(1)}, bf16[2,64,1024]{2,1,0:T(8,128)(2,1)S(1)}, u32[]{:S(2)}, u32[]{:S(2)}) collective-permute-start(bf16[2,64,1024]{2,1,0:T(8,128)(2,1)S(1)} %pad_maximum_fusion.1), channel_id=1, source_target_pairs={{0,64},{2,10},{4,68},{6,14},{8,72},{10,2},{12,76},{14,6},{32,96},{... | collective-permute-start | bytes 786440 | tf_op jit(solution)/shard_map/ppermute | solution.py:44
  13.4 8.5 %collective-permute-start.1 = (bf16[2,64,1024]{2,1,0:T(8,128)(2,1)S(1)}, bf16[2,64,1024]{2,1,0:T(8,128)(2,1)S(1)}, u32[]{:S(2)}, u32[]{:S(2)}) collective-permute-start(bf16[2,64,1024]{2,1,0:T(8,128)(2,1)S(1)} %pad_maximum_fusion.1), channel_id=1, source_target_pairs={{0,96},{2,14},{4,100},{6,2},{8,104},{10,6},{12,108},{14,10},{32,0}... | collective-permute-start | bytes 786440 | tf_op jit(solution)/shard_map/ppermute | solution.py:44
  22.7 11.0 %collective-permute-start.8 = (bf16[1024,3072]{1,0:T(8,128)(2,1)}, bf16[1024,3072]{1,0:T(8,128)(2,1)}, u32[]{:S(2)}, u32[]{:S(2)}) collective-permute-start(bf16[1024,3072]{1,0:T(8,128)(2,1)} %shard_map.111), channel_id=1, source_target_pairs={{0,2},{2,0},{1,3},{3,1},{4,6},{6,4},{5,7},{7,5},{8,10},{10,8},{9,1... | collective-permute-start | bytes 18874376 | tf_op jit(solution)/shard_map/ppermute | solution.py:34
  22.7 26.4 %collective-permute-start.4 = (bf16[64,8,1024]{2,1,0:T(8,128)(2,1)S(1)}, bf16[64,8,1024]{2,1,0:T(8,128)(2,1)S(1)}, u32[]{:S(2)}, u32[]{:S(2)}) collective-permute-start(bf16[64,8,1024]{2,1,0:T(8,128)(2,1)S(1)} %bitcast.41), channel_id=1, source_target_pairs={{0,12},{2,98},{4,0},{6,102},{8,4},{10,106},{12,8},{14,110},{32,44}... | collective-permute-start | bytes 3145736 | tf_op jit(solution)/shard_map/ppermute | solution.py:44
  25.6 23.6 %collective-permute-start.5 = (bf16[64,8,1024]{2,1,0:T(8,128)(2,1)S(1)}, bf16[64,8,1024]{2,1,0:T(8,128)(2,1)}, u32[]{:S(2)}, u32[]{:S(2)}) collective-permute-start(bf16[64,8,1024]{2,1,0:T(8,128)(2,1)S(1)} %bitcast.42), channel_id=1, source_target_pairs={{0,8},{2,66},{4,12},{6,70},{8,0},{10,74},{12,4},{14,78},{32,40},{3... | collective-permute-start | bytes 3145736 | tf_op jit(solution)/shard_map/ppermute | solution.py:44
  26.4 26.8 %collective-permute-start.6 = (bf16[64,8,1024]{2,1,0:T(8,128)(2,1)S(1)}, bf16[64,8,1024]{2,1,0:T(8,128)(2,1)}, u32[]{:S(2)}, u32[]{:S(2)}) collective-permute-start(bf16[64,8,1024]{2,1,0:T(8,128)(2,1)S(1)} %bitcast.43), channel_id=1, source_target_pairs={{0,4},{2,34},{4,8},{6,38},{8,12},{10,42},{12,0},{14,46},{32,36},{3... | collective-permute-start | bytes 3145736 | tf_op jit(solution)/shard_map/ppermute | solution.py:44
  27.3 26.0 %collective-permute-start.7 = (bf16[64,8,1024]{2,1,0:T(8,128)(2,1)S(1)}, bf16[64,8,1024]{2,1,0:T(8,128)(2,1)S(1)}, u32[]{:S(2)}, u32[]{:S(2)}) collective-permute-start(bf16[64,8,1024]{2,1,0:T(8,128)(2,1)S(1)} %bitcast.44), channel_id=1, source_target_pairs={{0,2},{2,0},{1,3},{3,1},{4,6},{6,4},{5,7},{7,5},{8,10},{10,8},{9,1... | collective-permute-start | bytes 3145736 | tf_op jit(solution)/shard_map/ppermute | solution.py:34
  33.7 31.3 %copy-start.2 = (s32[5]{0:T(128)S(1)}, s32[5]{0:T(128)}, u32[]{:S(2)}) copy-start(s32[5]{0:T(128)} %stack.46.place) | copy-start | bytes 64
  53.2 5.8 %collective-permute-start.9 = (bf16[64,8,1024]{2,1,0:T(8,128)(2,1)S(1)}, bf16[64,8,1024]{2,1,0:T(8,128)(2,1)}, u32[]{:S(2)}, u32[]{:S(2)}) collective-permute-start(bf16[64,8,1024]{2,1,0:T(8,128)(2,1)S(1)} %collective-permute-done.4.refs_1_), channel_id=1, source_target_pairs={{0,2},{2,0},{1,3},{3,1},{4,6},{6,4},{5,7},{7,5},{8,10},{10,8},{9,1... | collective-permute-start | bytes 3145736 | tf_op jit(solution)/shard_map/ppermute | solution.py:34
  53.2 5.8 %collective-permute-start.10 = (bf16[64,8,1024]{2,1,0:T(8,128)(2,1)}, bf16[64,8,1024]{2,1,0:T(8,128)(2,1)}, u32[]{:S(2)}, u32[]{:S(2)}) collective-permute-start(bf16[64,8,1024]{2,1,0:T(8,128)(2,1)} %collective-permute-done.5.refs_2_), channel_id=1, source_target_pairs={{0,2},{2,0},{1,3},{3,1},{4,6},{6,4},{5,7},{7,5},{8,10},{10,8},{9,1... | collective-permute-start | bytes 3145736 | tf_op jit(solution)/shard_map/ppermute | solution.py:34
  53.7 5.5 %collective-permute-start.11 = (bf16[64,8,1024]{2,1,0:T(8,128)(2,1)}, bf16[64,8,1024]{2,1,0:T(8,128)(2,1)}, u32[]{:S(2)}, u32[]{:S(2)}) collective-permute-start(bf16[64,8,1024]{2,1,0:T(8,128)(2,1)} %collective-permute-done.6.refs_3_), channel_id=1, source_target_pairs={{0,2},{2,0},{1,3},{3,1},{4,6},{6,4},{5,7},{7,5},{8,10},{10,8},{9,1... | collective-permute-start | bytes 3145736 | tf_op jit(solution)/shard_map/ppermute | solution.py:34
  54.4 36.8 %all-to-all-start = ((f32[64,16,128]{2,1,0:T(8,128)}), f32[64,16,128]{2,1,0:T(8,128)S(1)}, u32[]{:S(2)}, u32[]{:S(2)}) async-start(f32[64,16,128]{2,1,0:T(8,128)} %shard_map.110), calls=%async_computation | async-start | bytes 1048576 | tf_op jit(solution)/shard_map/all_to_all | solution.py:561
  59.2 32.0 %collective-permute-start.12 = (bf16[8,64,1024]{2,1,0:T(8,128)(2,1)}, bf16[8,64,1024]{2,1,0:T(8,128)(2,1)}, u32[]{:S(2)}, u32[]{:S(2)}) collective-permute-start(bf16[8,64,1024]{2,1,0:T(8,128)(2,1)} %get-tuple-element.84), channel_id=1, source_target_pairs={{0,32},{2,6},{4,36},{6,10},{8,40},{10,14},{12,44},{14,2},{32,64},{... | collective-permute-start | bytes 3145736 | tf_op jit(solution)/shard_map/ppermute | solution.py:44
  60.7 31.4 %collective-permute-start.13 = (bf16[8,64,1024]{2,1,0:T(8,128)(2,1)}, bf16[8,64,1024]{2,1,0:T(8,128)(2,1)}, u32[]{:S(2)}, u32[]{:S(2)}) collective-permute-start(bf16[8,64,1024]{2,1,0:T(8,128)(2,1)} %get-tuple-element.85), channel_id=1, source_target_pairs={{0,64},{2,10},{4,68},{6,14},{8,72},{10,2},{12,76},{14,6},{32,96},{... | collective-permute-start | bytes 3145736 | tf_op jit(solution)/shard_map/ppermute | solution.py:44
  63.6 28.5 %collective-permute-start.14 = (bf16[8,64,1024]{2,1,0:T(8,128)(2,1)}, bf16[8,64,1024]{2,1,0:T(8,128)(2,1)}, u32[]{:S(2)}, u32[]{:S(2)}) collective-permute-start(bf16[8,64,1024]{2,1,0:T(8,128)(2,1)} %get-tuple-element.86), channel_id=1, source_target_pairs={{0,96},{2,14},{4,100},{6,2},{8,104},{10,6},{12,108},{14,10},{32,0}... | collective-permute-start | bytes 3145736 | tf_op jit(solution)/shard_map/ppermute | solution.py:44
  88.3 30.2 %collective-permute-start.19 = (f16[1040,512]{1,0:T(8,128)(2,1)}, f16[1040,512]{1,0:T(8,128)(2,1)}, u32[]{:S(2)}, u32[]{:S(2)}) collective-permute-start(f16[1040,512]{1,0:T(8,128)(2,1)} %convert_element_type.56), channel_id=1, source_target_pairs={{0,1},{1,0},{2,3},{3,2},{4,5},{5,4},{6,7},{7,6},{8,9},{9,8},{10,11... | collective-permute-start | bytes 3194888 | tf_op jit(solution)/shard_map/ppermute | solution.py:34
  94.8 13.4 %collective-permute-start.15 = (bf16[2,64,1024]{2,1,0:T(8,128)(2,1)S(1)}, bf16[2,64,1024]{2,1,0:T(8,128)(2,1)S(1)}, u32[]{:S(2)}, u32[]{:S(2)}) collective-permute-start(bf16[2,64,1024]{2,1,0:T(8,128)(2,1)S(1)} %get-tuple-element.105), channel_id=1, source_target_pairs={{0,4},{2,34},{4,8},{6,38},{8,12},{10,42},{12,0},{14,46},{32,36},{3... | collective-permute-start | bytes 786440 | tf_op jit(solution)/shard_map/ppermute | solution.py:44
  95.8 12.4 %collective-permute-start.16 = (bf16[2,64,1024]{2,1,0:T(8,128)(2,1)S(1)}, bf16[2,64,1024]{2,1,0:T(8,128)(2,1)S(1)}, u32[]{:S(2)}, u32[]{:S(2)}) collective-permute-start(bf16[2,64,1024]{2,1,0:T(8,128)(2,1)S(1)} %get-tuple-element.106), channel_id=1, source_target_pairs={{0,8},{2,66},{4,12},{6,70},{8,0},{10,74},{12,4},{14,78},{32,40},{3... | collective-permute-start | bytes 786440 | tf_op jit(solution)/shard_map/ppermute | solution.py:44
  98.4 9.8 %collective-permute-start.17 = (bf16[2,64,1024]{2,1,0:T(8,128)(2,1)S(1)}, bf16[2,64,1024]{2,1,0:T(8,128)(2,1)S(1)}, u32[]{:S(2)}, u32[]{:S(2)}) collective-permute-start(bf16[2,64,1024]{2,1,0:T(8,128)(2,1)S(1)} %get-tuple-element.107), channel_id=1, source_target_pairs={{0,12},{2,98},{4,0},{6,102},{8,4},{10,106},{12,8},{14,110},{32,44}... | collective-permute-start | bytes 786440 | tf_op jit(solution)/shard_map/ppermute | solution.py:44
  108.4 10.8 %copy-start.4 = (f32[1024,512]{1,0:T(8,128)S(1)}, f32[1024,512]{1,0:T(8,128)}, u32[]{:S(2)}) copy-start(f32[1024,512]{1,0:T(8,128)} %get-tuple-element.98) | copy-start | bytes 6291460
  108.4 10.1 %collective-permute-start.18 = (bf16[64,1024]{1,0:T(8,128)(2,1)S(1)}, bf16[64,1024]{1,0:T(8,128)(2,1)S(1)}, u32[]{:S(2)}, u32[]{:S(2)}) collective-permute-start(bf16[64,1024]{1,0:T(8,128)(2,1)S(1)} %fusion), channel_id=1, source_target_pairs={{0,16},{16,0},{1,17},{17,1},{2,18},{18,2},{3,19},{19,3},{4,20},{20... | collective-permute-start | bytes 393224 | tf_op jit(solution)/shard_map/ppermute | solution.py:34
  (4 other events, 15.5 us)

commit v5 on v4

--- a/solution.py
+++ b/solution.py
@@ -58,7 +58,7 @@
 
 ANY = pl.BlockSpec(memory_space=pl.ANY)
 SCALARS = pl.BlockSpec(memory_space=pltpu.SMEM)
-AHEAD = 2
+AHEAD = 3
 PARTS = 1
 
 
@@ -440,7 +440,7 @@
             sems,
         ],
         input_output_aliases={2: 0} if held else {},
-        compiler_params=pltpu.CompilerParams(vmem_limit_bytes=58 * MIB),
+        compiler_params=pltpu.CompilerParams(vmem_limit_bytes=40 * MIB),
         cost_estimate=pl.CostEstimate(
             flops=2 * rows * block * blocks * width, bytes_accessed=0, transcendentals=0
         ),

time: 125 us -> 122 us (0.976)
  Pallas kernels: 69.7 us -> 64.7 us
  waiting for transfers between devices: 6.18 us -> 7.91 us
    pallas_call x2, Pallas kernels: 16.9 us -> 13.3 us  [back_part(): pl.pallas_call(functools.partial(back_kernel, first), in_specs=[ANY] * (2...]
    pallas_call x4, Pallas kernels: 48.6 us -> 47.3 us  [kernel_call(): pl.pallas_call(kernel, in_specs=in_specs or [SCALARS] + [ANY] * (len(args...]
    ppermute x12, waiting for transfers between devices: 5.98 us -> 7.25 us  [cross(): return lax.ppermute(value, ('z', 'x', 'c'), pairs)]
  transfers between devices with their start and end apart: 21 -> 21, of which waited for: 4 -> 5; matrix products, arithmetic and copies ran while one was open for 8% -> 8% of each run, Pallas kernels for 55% -> 52%
where the time goes in v5:
time: 122 us
  Pallas kernels  64.7 us (53%)
  starting transfers between devices  33.4 us (27%)
  other arithmetic  10.9 us (9%)
  waiting for transfers between devices  7.91 us (6%)
  local copies, waits for them, and re-layouts  3.66 us (3%)
    pallas_call x4, Pallas kernels, kernel_call(): pl.pallas_call(kernel, in_specs=in_specs or [SCALARS] + [ANY] * (len(args...  47.3 us
    ppermute x12, starting transfers between devices, cross(): return lax.ppermute(value, ('z', 'x', 'c'), pairs)  21.8 us
    pallas_call x2, Pallas kernels, back_part(): pl.pallas_call(functools.partial(back_kernel, first), in_specs=[ANY] * (2...  13.3 us
    ppermute x12, waiting for transfers between devices, cross(): return lax.ppermute(value, ('z', 'x', 'c'), pairs)  7.25 us
    ppermute x8, starting transfers between devices, shift(): lax.ppermute(value, axis, [(i, (i + step) % size) for i in range(size)])  7 us
    all_to_all x1, starting transfers between devices, shards(): lax.all_to_all(moments, DP, split_axis=0, concat_axis=0, tiled=True)  4.65 us
    add x2, other arithmetic, summed(): return sum((v.astype(jnp.float32) for v in terms[1:])) + terms[0]  3.54 us
    convert_element_type x1, other arithmetic, shards(): keys_came = shift(keys_send.astype(jnp.float16), 't', 1)  3.01 us
  transfers between devices with their start and end apart: 21, of which 5 were waited for; matrix products, arithmetic and copies ran while one was open for 8% of the time, Pallas kernels for 52%

profile of v5, /device:TPU:0, one launch (start us, length us, event | category | flops | bytes accessed | tf_op | source)
XLA Modules:
  0.0 121.5 jit_solution(4795193523638988184)
XLA Ops:
  0.7 1.7 %collective-permute-start = (bf16[64,1024]{1,0:T(8,128)(2,1)}, bf16[64,1024]{1,0:T(8,128)(2,1)S(1)}, u32[]{:S(2)}, u32[]{:S(2)}) collective-permute-start(bf16[64,1024]{1,0:T(8,128)(2,1)} %bitcast.56), channel_id=1, source_target_pairs={{0,16},{16,0},{1,17},{17,1},{2,18},{18,2},{3,19},{19,3},{4,20},{20... | collective-permute-start | bytes 393224 | tf_op jit(solution)/shard_map/ppermute | solution.py:34
  5.0 2.2 %shard_map.110 = f32[64,16,128]{2,1,0:T(8,128)} custom-call(f32[64,1024]{1,0:T(8,128)} %bitcast.51, f32[64,1024]{1,0:T(8,128)} %bitcast.52), custom_call_target="tpu_custom_call" | custom-call | bytes 1048576 | tf_op jit(solution)/shard_map/pallas_call | solution.py:463
  7.8 2.0 %collective-permute-start.3 = (bf16[2,64,1024]{2,1,0:T(8,128)(2,1)S(1)}, bf16[2,64,1024]{2,1,0:T(8,128)(2,1)S(1)}, u32[]{:S(2)}, u32[]{:S(2)}) collective-permute-start(bf16[2,64,1024]{2,1,0:T(8,128)(2,1)S(1)} %pad_maximum_fusion.1), channel_id=1, source_target_pairs={{0,32},{2,6},{4,36},{6,10},{8,40},{10,14},{12,44},{14,2},{32,64},{... | collective-permute-start | bytes 786440 | tf_op jit(solution)/shard_map/ppermute | solution.py:44
  9.8 3.6 %collective-permute-start.2 = (bf16[2,64,1024]{2,1,0:T(8,128)(2,1)S(1)}, bf16[2,64,1024]{2,1,0:T(8,128)(2,1)S(1)}, u32[]{:S(2)}, u32[]{:S(2)}) collective-permute-start(bf16[2,64,1024]{2,1,0:T(8,128)(2,1)S(1)} %pad_maximum_fusion.1), channel_id=1, source_target_pairs={{0,64},{2,10},{4,68},{6,14},{8,72},{10,2},{12,76},{14,6},{32,96},{... | collective-permute-start | bytes 786440 | tf_op jit(solution)/shard_map/ppermute | solution.py:44
  14.4 7.5 %shard_map.111 = bf16[1024,3072]{1,0:T(8,128)(2,1)} custom-call(s32[5]{0:T(128)} %stack.46.place, bf16[1024,4096]{1,0:T(8,128)(2,1)} %tokens.5, bf16[1024,1024]{1,0:T(8,128)(2,1)} %cotangent.3), custom_call_target="tpu_custom_call" | custom-call | bytes 8388608 | tf_op jit(solution)/shard_map/pallas_call | solution.py:66
  22.7 2.8 %collective-permute-start.4 = (bf16[64,8,1024]{2,1,0:T(8,128)(2,1)S(1)}, bf16[64,8,1024]{2,1,0:T(8,128)(2,1)}, u32[]{:S(2)}, u32[]{:S(2)}) collective-permute-start(bf16[64,8,1024]{2,1,0:T(8,128)(2,1)S(1)} %bitcast.41), channel_id=1, source_target_pairs={{0,12},{2,98},{4,0},{6,102},{8,4},{10,106},{12,8},{14,110},{32,44}... | collective-permute-start | bytes 3145736 | tf_op jit(solution)/shard_map/ppermute | solution.py:44
  27.2 6.4 %shard_map.112.mine = bf16[1024,2048]{1,0:T(8,128)(2,1)} custom-call(s32[5]{0:T(128)} %stack.46.place, bf16[1024,4096]{1,0:T(8,128)(2,1)} %tokens.5), custom_call_target="tpu_custom_call" | custom-call | bytes 8388608 | tf_op jit(solution)/shard_map/pallas_call | solution.py:66
  33.7 14.4 %shard_map.113 = (f32[8,64,1024]{2,1,0:T(8,128)}, bf16[8,64,1024]{2,1,0:T(8,128)(2,1)}, bf16[8,64,1024]{2,1,0:T(8,128)(2,1)}, bf16[8,64,1024]{2,1,0:T(8,128)(2,1)}) custom-call(bf16[1024,2048]{1,0:T(8,128)(2,1)} %shard_map.112.mine, bf16[1024,1024]{1,0:T(8,128)(2,1)} %cotangent.3, bf16[1024,3072]{1,0:T(8,128)(2,1)} %collective-permute-done.8.refs_0_), custom_call_target="tpu_custom_call" | custom-call | tf_op jit(solution)/shard_map/pallas_call | solution.py:66
  49.1 3.9 %collective-permute-done.6.refs_3_ = bf16[64,8,1024]{2,1,0:T(8,128)(2,1)S(1)} collective-permute-done((bf16[64,8,1024]{2,1,0:T(8,128)(2,1)S(1)}, bf16[64,8,1024]{2,1,0:T(8,128)(2,1)S(1)}, u32[]{:S(2)}, u32[]{:S(2)}) %collective-permute-start.6) | collective-permute-done | bytes 1048608 | tf_op jit(solution)/shard_map/ppermute | solution.py:44
  54.4 4.6 %all-to-all-start = ((f32[64,16,128]{2,1,0:T(8,128)}), f32[64,16,128]{2,1,0:T(8,128)S(1)}, u32[]{:S(2)}, u32[]{:S(2)}) async-start(f32[64,16,128]{2,1,0:T(8,128)} %shard_map.110), calls=%async_computation | async-start | bytes 1048576 | tf_op jit(solution)/shard_map/all_to_all | solution.py:561
  59.2 1.5 %collective-permute-start.12 = (bf16[8,64,1024]{2,1,0:T(8,128)(2,1)}, bf16[8,64,1024]{2,1,0:T(8,128)(2,1)}, u32[]{:S(2)}, u32[]{:S(2)}) collective-permute-start(bf16[8,64,1024]{2,1,0:T(8,128)(2,1)} %get-tuple-element.84), channel_id=1, source_target_pairs={{0,32},{2,6},{4,36},{6,10},{8,40},{10,14},{12,44},{14,2},{32,64},{... | collective-permute-start | bytes 3145736 | tf_op jit(solution)/shard_map/ppermute | solution.py:44
  60.7 2.9 %collective-permute-start.13 = (bf16[8,64,1024]{2,1,0:T(8,128)(2,1)}, bf16[8,64,1024]{2,1,0:T(8,128)(2,1)}, u32[]{:S(2)}, u32[]{:S(2)}) collective-permute-start(bf16[8,64,1024]{2,1,0:T(8,128)(2,1)} %get-tuple-element.85), channel_id=1, source_target_pairs={{0,64},{2,10},{4,68},{6,14},{8,72},{10,2},{12,76},{14,6},{32,96},{... | collective-permute-start | bytes 3145736 | tf_op jit(solution)/shard_map/ppermute | solution.py:44
  64.9 18.9 %shard_map.114 = (bf16[4096,1024]{1,0:T(8,128)(2,1)}, f32[1040,512]{1,0:T(8,128)}, f32[1024,512]{1,0:T(8,128)}, bf16[64,1024]{1,0:T(8,128)(2,1)S(1)}) custom-call(s32[5]{0:T(128)S(1)} %copy-done.4, s32[16,1,256]{2,1,0:T(1,128)S(1)} %copy.24.target, bf16[1024,4096]{1,0:T(8,128)(2,1)} %tokens.5, bf16[64,8,1024]{2,1,0:T(8,128)(2,1)S(1)} %bitcast.45, ...), custom_call_target="tpu_custom_call" | custom-call | flops 12884901888 | bytes 25165824 | tf_op jit(solution)/shard_map/pallas_call | solution.py:66
  83.9 3.0 %convert_element_type.56 = f16[1040,512]{1,0:T(8,128)(2,1)} convert(f32[1040,512]{1,0:T(8,128)} %get-tuple-element.113) | non-fusion elementwise | flops 532480 | bytes 3194880 | tf_op jit(solution)/shard_map/convert_element_type | solution.py:567
  86.9 2.9 %collective-permute-start.19 = (f16[1040,512]{1,0:T(8,128)(2,1)}, f16[1040,512]{1,0:T(8,128)(2,1)}, u32[]{:S(2)}, u32[]{:S(2)}) collective-permute-start(f16[1040,512]{1,0:T(8,128)(2,1)} %convert_element_type.56), channel_id=1, source_target_pairs={{0,1},{1,0},{2,3},{3,2},{4,5},{5,4},{6,7},{7,6},{8,9},{9,8},{10,11... | collective-permute-start | bytes 3194888 | tf_op jit(solution)/shard_map/ppermute | solution.py:34
  89.8 2.3 %collective-permute-done.13 = bf16[8,64,1024]{2,1,0:T(8,128)(2,1)} collective-permute-done((bf16[8,64,1024]{2,1,0:T(8,128)(2,1)}, bf16[8,64,1024]{2,1,0:T(8,128)(2,1)}, u32[]{:S(2)}, u32[]{:S(2)}) %collective-permute-start.13) | collective-permute-done | bytes 1048608 | tf_op jit(solution)/shard_map/ppermute | solution.py:44
  92.1 3.4 %add_add_fusion = f32[8,64,1024]{2,1,0:T(8,128)S(1)} fusion(f32[8,64,1024]{2,1,0:T(8,128)} %get-tuple-element.102, bf16[8,64,1024]{2,1,0:T(8,128)(2,1)} %collective-permute-done.14, bf16[8,64,1024]{2,1,0:T(8,128)(2,1)} %collective-permute-done.13, bf16[8,64,1024]{2,1,0:T(8,128)(2,1)} %collective-permute-done.12), kind=kLoop, calls=%fused_computation.2 | loop fusion | flops 3145728 | bytes 7340032 | tf_op jit(solution)/shard_map/add | solution.py:56
  96.6 2.6 %collective-permute-start.16 = (bf16[2,64,1024]{2,1,0:T(8,128)(2,1)S(1)}, bf16[2,64,1024]{2,1,0:T(8,128)(2,1)S(1)}, u32[]{:S(2)}, u32[]{:S(2)}) collective-permute-start(bf16[2,64,1024]{2,1,0:T(8,128)(2,1)S(1)} %get-tuple-element.106), channel_id=1, source_target_pairs={{0,8},{2,66},{4,12},{6,70},{8,0},{10,74},{12,4},{14,78},{32,40},{3... | collective-permute-start | bytes 786440 | tf_op jit(solution)/shard_map/ppermute | solution.py:44
  99.2 1.4 %collective-permute-start.17 = (bf16[2,64,1024]{2,1,0:T(8,128)(2,1)S(1)}, bf16[2,64,1024]{2,1,0:T(8,128)(2,1)S(1)}, u32[]{:S(2)}, u32[]{:S(2)}) collective-permute-start(bf16[2,64,1024]{2,1,0:T(8,128)(2,1)S(1)} %get-tuple-element.107), channel_id=1, source_target_pairs={{0,12},{2,98},{4,0},{6,102},{8,4},{10,106},{12,8},{14,110},{32,44}... | collective-permute-start | bytes 786440 | tf_op jit(solution)/shard_map/ppermute | solution.py:44
  100.6 6.6 %shard_map.115.refs_0_ = bf16[1024,4096]{1,0:T(8,128)(2,1)} custom-call(bf16[1024,1024]{1,0:T(8,128)(2,1)S(1)} %copy-done.3, bf16[4096,1024]{1,0:T(8,128)(2,1)S(1)} %copy-done.2), custom_call_target="tpu_custom_call" | custom-call | flops 4294967296 | tf_op jit(solution)/shard_map/pallas_call | solution.py:429
  107.4 1.6 %collective-permute-start.18 = (bf16[64,1024]{1,0:T(8,128)(2,1)S(1)}, bf16[64,1024]{1,0:T(8,128)(2,1)S(1)}, u32[]{:S(2)}, u32[]{:S(2)}) collective-permute-start(bf16[64,1024]{1,0:T(8,128)(2,1)S(1)} %fusion), channel_id=1, source_target_pairs={{0,16},{16,0},{1,17},{17,1},{2,18},{18,2},{3,19},{19,3},{4,20},{20... | collective-permute-start | bytes 393224 | tf_op jit(solution)/shard_map/ppermute | solution.py:34
  109.0 6.6 %shard_map.116 = bf16[1024,4096]{1,0:T(8,128)(2,1)} custom-call(bf16[1024,1024]{1,0:T(8,128)(2,1)S(1)} %copy-done.3, bf16[4096,1024]{1,0:T(8,128)(2,1)S(1)} %copy-done.2, bf16[1024,4096]{1,0:T(8,128)(2,1)} %shard_map.115.refs_0_), custom_call_target="tpu_custom_call", output_to_operand_aliasing={{}: (2, {})} | custom-call | flops 4294967296 | tf_op jit(solution)/shard_map/pallas_call | solution.py:429
  116.9 2.5 %add_convert_fusion = bf16[1024,512]{1,0:T(8,128)(2,1)} fusion(f32[1024,512]{1,0:T(8,128)S(1)} %copy-done.5, f32[512]{0:T(512)S(1)} %bitcast.58, f16[1040,512]{1,0:T(8,128)(2,1)} %collective-permute-done.19), kind=kLoop, calls=%fused_computation.1 | loop fusion | flops 2097152 | bytes 4196352 | tf_op jit(solution)/shard_map/convert_element_type | solution.py:584
  119.5 2.0 %shard_map.117 = (bf16[64,1024]{1,0:T(8,128)(2,1)}, f32[64,1024]{1,0:T(8,128)}, f32[64,1024]{1,0:T(8,128)}) custom-call(s32[64]{0:T(128)S(1)} %select_reduce_fusion.source, f32[64,16,128]{2,1,0:T(8,128)S(1)} %all-to-all-done.moments, f32[64,1024]{1,0:T(8,128)S(1)} %slice_bitcast_fusion.1.own, bf16[64,1024]{1,0:T(8,128)(2,1)S(1)} %collective-permute-done.18.came, ...), custom_call_target="tpu_custom_call" | custom-call | bytes 1048576 | tf_op jit(solution)/shard_map/pallas_call | solution.py:494
  (71 shorter events, 13.0 us)
Async XLA Ops:
  0.7 7.1 %collective-permute-start = (bf16[64,1024]{1,0:T(8,128)(2,1)}, bf16[64,1024]{1,0:T(8,128)(2,1)S(1)}, u32[]{:S(2)}, u32[]{:S(2)}) collective-permute-start(bf16[64,1024]{1,0:T(8,128)(2,1)} %bitcast.56), channel_id=1, source_target_pairs={{0,16},{16,0},{1,17},{17,1},{2,18},{18,2},{3,19},{19,3},{4,20},{20... | collective-permute-start | bytes 393224 | tf_op jit(solution)/shard_map/ppermute | solution.py:34
  7.8 14.1 %collective-permute-start.3 = (bf16[2,64,1024]{2,1,0:T(8,128)(2,1)S(1)}, bf16[2,64,1024]{2,1,0:T(8,128)(2,1)S(1)}, u32[]{:S(2)}, u32[]{:S(2)}) collective-permute-start(bf16[2,64,1024]{2,1,0:T(8,128)(2,1)S(1)} %pad_maximum_fusion.1), channel_id=1, source_target_pairs={{0,32},{2,6},{4,36},{6,10},{8,40},{10,14},{12,44},{14,2},{32,64},{... | collective-permute-start | bytes 786440 | tf_op jit(solution)/shard_map/ppermute | solution.py:44
  9.8 12.1 %collective-permute-start.2 = (bf16[2,64,1024]{2,1,0:T(8,128)(2,1)S(1)}, bf16[2,64,1024]{2,1,0:T(8,128)(2,1)S(1)}, u32[]{:S(2)}, u32[]{:S(2)}) collective-permute-start(bf16[2,64,1024]{2,1,0:T(8,128)(2,1)S(1)} %pad_maximum_fusion.1), channel_id=1, source_target_pairs={{0,64},{2,10},{4,68},{6,14},{8,72},{10,2},{12,76},{14,6},{32,96},{... | collective-permute-start | bytes 786440 | tf_op jit(solution)/shard_map/ppermute | solution.py:44
  13.4 8.5 %collective-permute-start.1 = (bf16[2,64,1024]{2,1,0:T(8,128)(2,1)S(1)}, bf16[2,64,1024]{2,1,0:T(8,128)(2,1)S(1)}, u32[]{:S(2)}, u32[]{:S(2)}) collective-permute-start(bf16[2,64,1024]{2,1,0:T(8,128)(2,1)S(1)} %pad_maximum_fusion.1), channel_id=1, source_target_pairs={{0,96},{2,14},{4,100},{6,2},{8,104},{10,6},{12,108},{14,10},{32,0}... | collective-permute-start | bytes 786440 | tf_op jit(solution)/shard_map/ppermute | solution.py:44
  22.6 11.1 %collective-permute-start.8 = (bf16[1024,3072]{1,0:T(8,128)(2,1)}, bf16[1024,3072]{1,0:T(8,128)(2,1)}, u32[]{:S(2)}, u32[]{:S(2)}) collective-permute-start(bf16[1024,3072]{1,0:T(8,128)(2,1)} %shard_map.111), channel_id=1, source_target_pairs={{0,2},{2,0},{1,3},{3,1},{4,6},{6,4},{5,7},{7,5},{8,10},{10,8},{9,1... | collective-permute-start | bytes 18874376 | tf_op jit(solution)/shard_map/ppermute | solution.py:34
  22.7 26.4 %collective-permute-start.4 = (bf16[64,8,1024]{2,1,0:T(8,128)(2,1)S(1)}, bf16[64,8,1024]{2,1,0:T(8,128)(2,1)}, u32[]{:S(2)}, u32[]{:S(2)}) collective-permute-start(bf16[64,8,1024]{2,1,0:T(8,128)(2,1)S(1)} %bitcast.41), channel_id=1, source_target_pairs={{0,12},{2,98},{4,0},{6,102},{8,4},{10,106},{12,8},{14,110},{32,44}... | collective-permute-start | bytes 3145736 | tf_op jit(solution)/shard_map/ppermute | solution.py:44
  25.5 23.6 %collective-permute-start.5 = (bf16[64,8,1024]{2,1,0:T(8,128)(2,1)S(1)}, bf16[64,8,1024]{2,1,0:T(8,128)(2,1)}, u32[]{:S(2)}, u32[]{:S(2)}) collective-permute-start(bf16[64,8,1024]{2,1,0:T(8,128)(2,1)S(1)} %bitcast.42), channel_id=1, source_target_pairs={{0,8},{2,66},{4,12},{6,70},{8,0},{10,74},{12,4},{14,78},{32,40},{3... | collective-permute-start | bytes 3145736 | tf_op jit(solution)/shard_map/ppermute | solution.py:44
  26.3 26.7 %collective-permute-start.6 = (bf16[64,8,1024]{2,1,0:T(8,128)(2,1)S(1)}, bf16[64,8,1024]{2,1,0:T(8,128)(2,1)S(1)}, u32[]{:S(2)}, u32[]{:S(2)}) collective-permute-start(bf16[64,8,1024]{2,1,0:T(8,128)(2,1)S(1)} %bitcast.43), channel_id=1, source_target_pairs={{0,4},{2,34},{4,8},{6,38},{8,12},{10,42},{12,0},{14,46},{32,36},{3... | collective-permute-start | bytes 3145736 | tf_op jit(solution)/shard_map/ppermute | solution.py:44
  27.2 25.9 %collective-permute-start.7 = (bf16[64,8,1024]{2,1,0:T(8,128)(2,1)S(1)}, bf16[64,8,1024]{2,1,0:T(8,128)(2,1)S(1)}, u32[]{:S(2)}, u32[]{:S(2)}) collective-permute-start(bf16[64,8,1024]{2,1,0:T(8,128)(2,1)S(1)} %bitcast.44), channel_id=1, source_target_pairs={{0,2},{2,0},{1,3},{3,1},{4,6},{6,4},{5,7},{7,5},{8,10},{10,8},{9,1... | collective-permute-start | bytes 3145736 | tf_op jit(solution)/shard_map/ppermute | solution.py:34
  33.6 31.3 %copy-start.4 = (s32[5]{0:T(128)S(1)}, s32[5]{0:T(128)}, u32[]{:S(2)}) copy-start(s32[5]{0:T(128)} %stack.46.place) | copy-start | bytes 64
  53.1 11.9 %copy-start.7 = (bf16[64,8,1024]{2,1,0:T(8,128)(2,1)}, bf16[64,8,1024]{2,1,0:T(8,128)(2,1)S(1)}, u32[]{:S(2)}) copy-start(bf16[64,8,1024]{2,1,0:T(8,128)(2,1)S(1)} %collective-permute-done.6.refs_3_) | copy-start | bytes 3145732
  53.1 5.9 %collective-permute-start.9 = (bf16[64,8,1024]{2,1,0:T(8,128)(2,1)}, bf16[64,8,1024]{2,1,0:T(8,128)(2,1)}, u32[]{:S(2)}, u32[]{:S(2)}) collective-permute-start(bf16[64,8,1024]{2,1,0:T(8,128)(2,1)} %collective-permute-done.4.refs_1_), channel_id=1, source_target_pairs={{0,2},{2,0},{1,3},{3,1},{4,6},{6,4},{5,7},{7,5},{8,10},{10,8},{9,1... | collective-permute-start | bytes 3145736 | tf_op jit(solution)/shard_map/ppermute | solution.py:34
  53.2 6.0 %collective-permute-start.10 = (bf16[64,8,1024]{2,1,0:T(8,128)(2,1)}, bf16[64,8,1024]{2,1,0:T(8,128)(2,1)}, u32[]{:S(2)}, u32[]{:S(2)}) collective-permute-start(bf16[64,8,1024]{2,1,0:T(8,128)(2,1)} %collective-permute-done.5.refs_2_), channel_id=1, source_target_pairs={{0,2},{2,0},{1,3},{3,1},{4,6},{6,4},{5,7},{7,5},{8,10},{10,8},{9,1... | collective-permute-start | bytes 3145736 | tf_op jit(solution)/shard_map/ppermute | solution.py:34
  53.7 5.5 %collective-permute-start.11 = (bf16[64,8,1024]{2,1,0:T(8,128)(2,1)S(1)}, bf16[64,8,1024]{2,1,0:T(8,128)(2,1)}, u32[]{:S(2)}, u32[]{:S(2)}) collective-permute-start(bf16[64,8,1024]{2,1,0:T(8,128)(2,1)S(1)} %collective-permute-done.6.refs_3_), channel_id=1, source_target_pairs={{0,2},{2,0},{1,3},{3,1},{4,6},{6,4},{5,7},{7,5},{8,10},{10,8},{9,1... | collective-permute-start | bytes 3145736 | tf_op jit(solution)/shard_map/ppermute | solution.py:34
  54.4 35.4 %all-to-all-start = ((f32[64,16,128]{2,1,0:T(8,128)}), f32[64,16,128]{2,1,0:T(8,128)S(1)}, u32[]{:S(2)}, u32[]{:S(2)}) async-start(f32[64,16,128]{2,1,0:T(8,128)} %shard_map.110), calls=%async_computation | async-start | bytes 1048576 | tf_op jit(solution)/shard_map/all_to_all | solution.py:561
  59.2 30.6 %collective-permute-start.12 = (bf16[8,64,1024]{2,1,0:T(8,128)(2,1)}, bf16[8,64,1024]{2,1,0:T(8,128)(2,1)}, u32[]{:S(2)}, u32[]{:S(2)}) collective-permute-start(bf16[8,64,1024]{2,1,0:T(8,128)(2,1)} %get-tuple-element.84), channel_id=1, source_target_pairs={{0,32},{2,6},{4,36},{6,10},{8,40},{10,14},{12,44},{14,2},{32,64},{... | collective-permute-start | bytes 3145736 | tf_op jit(solution)/shard_map/ppermute | solution.py:44
  60.7 31.4 %collective-permute-start.13 = (bf16[8,64,1024]{2,1,0:T(8,128)(2,1)}, bf16[8,64,1024]{2,1,0:T(8,128)(2,1)}, u32[]{:S(2)}, u32[]{:S(2)}) collective-permute-start(bf16[8,64,1024]{2,1,0:T(8,128)(2,1)} %get-tuple-element.85), channel_id=1, source_target_pairs={{0,64},{2,10},{4,68},{6,14},{8,72},{10,2},{12,76},{14,6},{32,96},{... | collective-permute-start | bytes 3145736 | tf_op jit(solution)/shard_map/ppermute | solution.py:44
  63.6 28.5 %collective-permute-start.14 = (bf16[8,64,1024]{2,1,0:T(8,128)(2,1)}, bf16[8,64,1024]{2,1,0:T(8,128)(2,1)}, u32[]{:S(2)}, u32[]{:S(2)}) collective-permute-start(bf16[8,64,1024]{2,1,0:T(8,128)(2,1)} %get-tuple-element.86), channel_id=1, source_target_pairs={{0,96},{2,14},{4,100},{6,2},{8,104},{10,6},{12,108},{14,10},{32,0}... | collective-permute-start | bytes 3145736 | tf_op jit(solution)/shard_map/ppermute | solution.py:44
  83.9 16.7 %copy-start.3 = (bf16[1024,1024]{1,0:T(8,128)(2,1)S(1)}, bf16[1024,1024]{1,0:T(8,128)(2,1)}, u32[]{:S(2)}) copy-start(bf16[1024,1024]{1,0:T(8,128)(2,1)} %cotangent.3) | copy-start | bytes 6291460
  86.9 28.8 %collective-permute-start.19 = (f16[1040,512]{1,0:T(8,128)(2,1)}, f16[1040,512]{1,0:T(8,128)(2,1)}, u32[]{:S(2)}, u32[]{:S(2)}) collective-permute-start(f16[1040,512]{1,0:T(8,128)(2,1)} %convert_element_type.56), channel_id=1, source_target_pairs={{0,1},{1,0},{2,3},{3,2},{4,5},{5,4},{6,7},{7,6},{8,9},{9,8},{10,11... | collective-permute-start | bytes 3194888 | tf_op jit(solution)/shard_map/ppermute | solution.py:34
  95.6 11.6 %collective-permute-start.15 = (bf16[2,64,1024]{2,1,0:T(8,128)(2,1)S(1)}, bf16[2,64,1024]{2,1,0:T(8,128)(2,1)S(1)}, u32[]{:S(2)}, u32[]{:S(2)}) collective-permute-start(bf16[2,64,1024]{2,1,0:T(8,128)(2,1)S(1)} %get-tuple-element.105), channel_id=1, source_target_pairs={{0,4},{2,34},{4,8},{6,38},{8,12},{10,42},{12,0},{14,46},{32,36},{3... | collective-permute-start | bytes 786440 | tf_op jit(solution)/shard_map/ppermute | solution.py:44
  96.6 10.6 %collective-permute-start.16 = (bf16[2,64,1024]{2,1,0:T(8,128)(2,1)S(1)}, bf16[2,64,1024]{2,1,0:T(8,128)(2,1)S(1)}, u32[]{:S(2)}, u32[]{:S(2)}) collective-permute-start(bf16[2,64,1024]{2,1,0:T(8,128)(2,1)S(1)} %get-tuple-element.106), channel_id=1, source_target_pairs={{0,8},{2,66},{4,12},{6,70},{8,0},{10,74},{12,4},{14,78},{32,40},{3... | collective-permute-start | bytes 786440 | tf_op jit(solution)/shard_map/ppermute | solution.py:44
  99.2 8.0 %collective-permute-start.17 = (bf16[2,64,1024]{2,1,0:T(8,128)(2,1)S(1)}, bf16[2,64,1024]{2,1,0:T(8,128)(2,1)S(1)}, u32[]{:S(2)}, u32[]{:S(2)}) collective-permute-start(bf16[2,64,1024]{2,1,0:T(8,128)(2,1)S(1)} %get-tuple-element.107), channel_id=1, source_target_pairs={{0,12},{2,98},{4,0},{6,102},{8,4},{10,106},{12,8},{14,110},{32,44}... | collective-permute-start | bytes 786440 | tf_op jit(solution)/shard_map/ppermute | solution.py:44
  107.4 8.8 %collective-permute-start.18 = (bf16[64,1024]{1,0:T(8,128)(2,1)S(1)}, bf16[64,1024]{1,0:T(8,128)(2,1)S(1)}, u32[]{:S(2)}, u32[]{:S(2)}) collective-permute-start(bf16[64,1024]{1,0:T(8,128)(2,1)S(1)} %fusion), channel_id=1, source_target_pairs={{0,16},{16,0},{1,17},{17,1},{2,18},{18,2},{3,19},{19,3},{4,20},{20... | collective-permute-start | bytes 393224 | tf_op jit(solution)/shard_map/ppermute | solution.py:34
  (6 other events, 34.0 us)

commit v6 on v5

--- a/solution.py
+++ b/solution.py
@@ -58,7 +58,7 @@
 
 ANY = pl.BlockSpec(memory_space=pl.ANY)
 SCALARS = pl.BlockSpec(memory_space=pltpu.SMEM)
-AHEAD = 3
+AHEAD = 4
 PARTS = 1
 
 
@@ -440,7 +440,7 @@
             sems,
         ],
         input_output_aliases={2: 0} if held else {},
-        compiler_params=pltpu.CompilerParams(vmem_limit_bytes=40 * MIB),
+        compiler_params=pltpu.CompilerParams(vmem_limit_bytes=28 * MIB),
         cost_estimate=pl.CostEstimate(
             flops=2 * rows * block * blocks * width, bytes_accessed=0, transcendentals=0
         ),

time: 122 us -> 122 us (level)
  no operation moved by 1% of the time
where the time goes in v6:
time: 122 us; the launch traced here: 121 us
  Pallas kernels  64.5 us (53%)
  starting transfers between devices  33.4 us (27%)
  other arithmetic  10.8 us (9%)
  waiting for transfers between devices  7.95 us (7%)
  local copies, waits for them, and re-layouts  3.66 us (3%)
    pallas_call x4, Pallas kernels, kernel_call(): pl.pallas_call(kernel, in_specs=in_specs or [SCALARS] + [ANY] * (len(args...  47.1 us
    ppermute x12, starting transfers between devices, cross(): return lax.ppermute(value, ('z', 'x', 'c'), pairs)  21.8 us
    pallas_call x2, Pallas kernels, back_part(): pl.pallas_call(functools.partial(back_kernel, first), in_specs=[ANY] * (2...  13.3 us
    ppermute x12, waiting for transfers between devices, cross(): return lax.ppermute(value, ('z', 'x', 'c'), pairs)  7.44 us
    ppermute x8, starting transfers between devices, shift(): lax.ppermute(value, axis, [(i, (i + step) % size) for i in range(size)])  6.99 us
    all_to_all x1, starting transfers between devices, shards(): lax.all_to_all(moments, DP, split_axis=0, concat_axis=0, tiled=True)  4.65 us
    add x2, other arithmetic, summed(): return sum((v.astype(jnp.float32) for v in terms[1:])) + terms[0]  3.5 us
    convert_element_type x1, other arithmetic, shards(): keys_came = shift(keys_send.astype(jnp.float16), 't', 1)  3.01 us
  transfers between devices with their start and end apart: 21, of which 5 were waited for; matrix products, arithmetic and copies ran while one was open for 8% of the time, Pallas kernels for 52%

profile of v6, /device:TPU:0, one launch (start us, length us, event | category | flops | bytes accessed | tf_op | source)
XLA Modules:
  0.0 121.3 jit_solution(15871299022547928064)
XLA Ops:
  0.7 1.7 %collective-permute-start = (bf16[64,1024]{1,0:T(8,128)(2,1)}, bf16[64,1024]{1,0:T(8,128)(2,1)S(1)}, u32[]{:S(2)}, u32[]{:S(2)}) collective-permute-start(bf16[64,1024]{1,0:T(8,128)(2,1)} %bitcast.56), channel_id=1, source_target_pairs={{0,16},{16,0},{1,17},{17,1},{2,18},{18,2},{3,19},{19,3},{4,20},{20... | collective-permute-start | bytes 393224 | tf_op jit(solution)/shard_map/ppermute | solution.py:34
  5.0 2.2 %shard_map.110 = f32[64,16,128]{2,1,0:T(8,128)} custom-call(f32[64,1024]{1,0:T(8,128)} %bitcast.51, f32[64,1024]{1,0:T(8,128)} %bitcast.52), custom_call_target="tpu_custom_call" | custom-call | bytes 1048576 | tf_op jit(solution)/shard_map/pallas_call | solution.py:463
  7.8 2.0 %collective-permute-start.3 = (bf16[2,64,1024]{2,1,0:T(8,128)(2,1)S(1)}, bf16[2,64,1024]{2,1,0:T(8,128)(2,1)S(1)}, u32[]{:S(2)}, u32[]{:S(2)}) collective-permute-start(bf16[2,64,1024]{2,1,0:T(8,128)(2,1)S(1)} %pad_maximum_fusion.1), channel_id=1, source_target_pairs={{0,32},{2,6},{4,36},{6,10},{8,40},{10,14},{12,44},{14,2},{32,64},{... | collective-permute-start | bytes 786440 | tf_op jit(solution)/shard_map/ppermute | solution.py:44
  9.8 3.6 %collective-permute-start.2 = (bf16[2,64,1024]{2,1,0:T(8,128)(2,1)S(1)}, bf16[2,64,1024]{2,1,0:T(8,128)(2,1)S(1)}, u32[]{:S(2)}, u32[]{:S(2)}) collective-permute-start(bf16[2,64,1024]{2,1,0:T(8,128)(2,1)S(1)} %pad_maximum_fusion.1), channel_id=1, source_target_pairs={{0,64},{2,10},{4,68},{6,14},{8,72},{10,2},{12,76},{14,6},{32,96},{... | collective-permute-start | bytes 786440 | tf_op jit(solution)/shard_map/ppermute | solution.py:44
  14.4 7.5 %shard_map.111 = bf16[1024,3072]{1,0:T(8,128)(2,1)} custom-call(s32[5]{0:T(128)} %stack.46.place, bf16[1024,4096]{1,0:T(8,128)(2,1)} %tokens.5, bf16[1024,1024]{1,0:T(8,128)(2,1)} %cotangent.3), custom_call_target="tpu_custom_call" | custom-call | bytes 8388608 | tf_op jit(solution)/shard_map/pallas_call | solution.py:66
  22.7 2.8 %collective-permute-start.4 = (bf16[64,8,1024]{2,1,0:T(8,128)(2,1)S(1)}, bf16[64,8,1024]{2,1,0:T(8,128)(2,1)}, u32[]{:S(2)}, u32[]{:S(2)}) collective-permute-start(bf16[64,8,1024]{2,1,0:T(8,128)(2,1)S(1)} %bitcast.41), channel_id=1, source_target_pairs={{0,12},{2,98},{4,0},{6,102},{8,4},{10,106},{12,8},{14,110},{32,44}... | collective-permute-start | bytes 3145736 | tf_op jit(solution)/shard_map/ppermute | solution.py:44
  27.2 6.4 %shard_map.112.mine = bf16[1024,2048]{1,0:T(8,128)(2,1)} custom-call(s32[5]{0:T(128)} %stack.46.place, bf16[1024,4096]{1,0:T(8,128)(2,1)} %tokens.5), custom_call_target="tpu_custom_call" | custom-call | bytes 8388608 | tf_op jit(solution)/shard_map/pallas_call | solution.py:66
  33.7 14.4 %shard_map.113 = (f32[8,64,1024]{2,1,0:T(8,128)}, bf16[8,64,1024]{2,1,0:T(8,128)(2,1)}, bf16[8,64,1024]{2,1,0:T(8,128)(2,1)}, bf16[8,64,1024]{2,1,0:T(8,128)(2,1)}) custom-call(bf16[1024,2048]{1,0:T(8,128)(2,1)} %shard_map.112.mine, bf16[1024,1024]{1,0:T(8,128)(2,1)} %cotangent.3, bf16[1024,3072]{1,0:T(8,128)(2,1)} %collective-permute-done.8.refs_0_), custom_call_target="tpu_custom_call" | custom-call | tf_op jit(solution)/shard_map/pallas_call | solution.py:66
  49.1 3.9 %collective-permute-done.6.refs_3_ = bf16[64,8,1024]{2,1,0:T(8,128)(2,1)S(1)} collective-permute-done((bf16[64,8,1024]{2,1,0:T(8,128)(2,1)S(1)}, bf16[64,8,1024]{2,1,0:T(8,128)(2,1)S(1)}, u32[]{:S(2)}, u32[]{:S(2)}) %collective-permute-start.6) | collective-permute-done | bytes 1048608 | tf_op jit(solution)/shard_map/ppermute | solution.py:44
  54.4 4.6 %all-to-all-start = ((f32[64,16,128]{2,1,0:T(8,128)}), f32[64,16,128]{2,1,0:T(8,128)S(1)}, u32[]{:S(2)}, u32[]{:S(2)}) async-start(f32[64,16,128]{2,1,0:T(8,128)} %shard_map.110), calls=%async_computation | async-start | bytes 1048576 | tf_op jit(solution)/shard_map/all_to_all | solution.py:561
  59.2 1.5 %collective-permute-start.12 = (bf16[8,64,1024]{2,1,0:T(8,128)(2,1)}, bf16[8,64,1024]{2,1,0:T(8,128)(2,1)}, u32[]{:S(2)}, u32[]{:S(2)}) collective-permute-start(bf16[8,64,1024]{2,1,0:T(8,128)(2,1)} %get-tuple-element.84), channel_id=1, source_target_pairs={{0,32},{2,6},{4,36},{6,10},{8,40},{10,14},{12,44},{14,2},{32,64},{... | collective-permute-start | bytes 3145736 | tf_op jit(solution)/shard_map/ppermute | solution.py:44
  60.7 2.9 %collective-permute-start.13 = (bf16[8,64,1024]{2,1,0:T(8,128)(2,1)}, bf16[8,64,1024]{2,1,0:T(8,128)(2,1)}, u32[]{:S(2)}, u32[]{:S(2)}) collective-permute-start(bf16[8,64,1024]{2,1,0:T(8,128)(2,1)} %get-tuple-element.85), channel_id=1, source_target_pairs={{0,64},{2,10},{4,68},{6,14},{8,72},{10,2},{12,76},{14,6},{32,96},{... | collective-permute-start | bytes 3145736 | tf_op jit(solution)/shard_map/ppermute | solution.py:44
  64.9 18.7 %shard_map.114 = (bf16[4096,1024]{1,0:T(8,128)(2,1)}, f32[1040,512]{1,0:T(8,128)}, f32[1024,512]{1,0:T(8,128)}, bf16[64,1024]{1,0:T(8,128)(2,1)S(1)}) custom-call(s32[5]{0:T(128)S(1)} %copy-done.4, s32[16,1,256]{2,1,0:T(1,128)S(1)} %copy.24.target, bf16[1024,4096]{1,0:T(8,128)(2,1)} %tokens.5, bf16[64,8,1024]{2,1,0:T(8,128)(2,1)S(1)} %bitcast.45, ...), custom_call_target="tpu_custom_call" | custom-call | flops 12884901888 | bytes 25165824 | tf_op jit(solution)/shard_map/pallas_call | solution.py:66
  83.7 3.0 %convert_element_type.56 = f16[1040,512]{1,0:T(8,128)(2,1)} convert(f32[1040,512]{1,0:T(8,128)} %get-tuple-element.113) | non-fusion elementwise | flops 532480 | bytes 3194880 | tf_op jit(solution)/shard_map/convert_element_type | solution.py:567
  86.7 2.9 %collective-permute-start.19 = (f16[1040,512]{1,0:T(8,128)(2,1)}, f16[1040,512]{1,0:T(8,128)(2,1)}, u32[]{:S(2)}, u32[]{:S(2)}) collective-permute-start(f16[1040,512]{1,0:T(8,128)(2,1)} %convert_element_type.56), channel_id=1, source_target_pairs={{0,1},{1,0},{2,3},{3,2},{4,5},{5,4},{6,7},{7,6},{8,9},{9,8},{10,11... | collective-permute-start | bytes 3194888 | tf_op jit(solution)/shard_map/ppermute | solution.py:34
  89.6 2.5 %collective-permute-done.13 = bf16[8,64,1024]{2,1,0:T(8,128)(2,1)} collective-permute-done((bf16[8,64,1024]{2,1,0:T(8,128)(2,1)}, bf16[8,64,1024]{2,1,0:T(8,128)(2,1)}, u32[]{:S(2)}, u32[]{:S(2)}) %collective-permute-start.13) | collective-permute-done | bytes 1048608 | tf_op jit(solution)/shard_map/ppermute | solution.py:44
  92.1 3.4 %add_add_fusion = f32[8,64,1024]{2,1,0:T(8,128)S(1)} fusion(f32[8,64,1024]{2,1,0:T(8,128)} %get-tuple-element.102, bf16[8,64,1024]{2,1,0:T(8,128)(2,1)} %collective-permute-done.14, bf16[8,64,1024]{2,1,0:T(8,128)(2,1)} %collective-permute-done.13, bf16[8,64,1024]{2,1,0:T(8,128)(2,1)} %collective-permute-done.12), kind=kLoop, calls=%fused_computation.2 | loop fusion | flops 3145728 | bytes 7340032 | tf_op jit(solution)/shard_map/add | solution.py:56
  96.6 2.6 %collective-permute-start.16 = (bf16[2,64,1024]{2,1,0:T(8,128)(2,1)S(1)}, bf16[2,64,1024]{2,1,0:T(8,128)(2,1)S(1)}, u32[]{:S(2)}, u32[]{:S(2)}) collective-permute-start(bf16[2,64,1024]{2,1,0:T(8,128)(2,1)S(1)} %get-tuple-element.106), channel_id=1, source_target_pairs={{0,8},{2,66},{4,12},{6,70},{8,0},{10,74},{12,4},{14,78},{32,40},{3... | collective-permute-start | bytes 786440 | tf_op jit(solution)/shard_map/ppermute | solution.py:44
  99.2 1.4 %collective-permute-start.17 = (bf16[2,64,1024]{2,1,0:T(8,128)(2,1)S(1)}, bf16[2,64,1024]{2,1,0:T(8,128)(2,1)S(1)}, u32[]{:S(2)}, u32[]{:S(2)}) collective-permute-start(bf16[2,64,1024]{2,1,0:T(8,128)(2,1)S(1)} %get-tuple-element.107), channel_id=1, source_target_pairs={{0,12},{2,98},{4,0},{6,102},{8,4},{10,106},{12,8},{14,110},{32,44}... | collective-permute-start | bytes 786440 | tf_op jit(solution)/shard_map/ppermute | solution.py:44
  100.5 6.6 %shard_map.115.refs_0_ = bf16[1024,4096]{1,0:T(8,128)(2,1)} custom-call(bf16[1024,1024]{1,0:T(8,128)(2,1)S(1)} %copy-done.3, bf16[4096,1024]{1,0:T(8,128)(2,1)S(1)} %copy-done.2), custom_call_target="tpu_custom_call" | custom-call | flops 4294967296 | tf_op jit(solution)/shard_map/pallas_call | solution.py:429
  107.4 1.6 %collective-permute-start.18 = (bf16[64,1024]{1,0:T(8,128)(2,1)S(1)}, bf16[64,1024]{1,0:T(8,128)(2,1)S(1)}, u32[]{:S(2)}, u32[]{:S(2)}) collective-permute-start(bf16[64,1024]{1,0:T(8,128)(2,1)S(1)} %fusion), channel_id=1, source_target_pairs={{0,16},{16,0},{1,17},{17,1},{2,18},{18,2},{3,19},{19,3},{4,20},{20... | collective-permute-start | bytes 393224 | tf_op jit(solution)/shard_map/ppermute | solution.py:34
  109.0 6.6 %shard_map.116 = bf16[1024,4096]{1,0:T(8,128)(2,1)} custom-call(bf16[1024,1024]{1,0:T(8,128)(2,1)S(1)} %copy-done.3, bf16[4096,1024]{1,0:T(8,128)(2,1)S(1)} %copy-done.2, bf16[1024,4096]{1,0:T(8,128)(2,1)} %shard_map.115.refs_0_), custom_call_target="tpu_custom_call", output_to_operand_aliasing={{}: (2, {})} | custom-call | flops 4294967296 | tf_op jit(solution)/shard_map/pallas_call | solution.py:429
  116.8 2.5 %add_convert_fusion = bf16[1024,512]{1,0:T(8,128)(2,1)} fusion(f32[1024,512]{1,0:T(8,128)S(1)} %copy-done.5, f32[512]{0:T(512)S(1)} %bitcast.58, f16[1040,512]{1,0:T(8,128)(2,1)} %collective-permute-done.19), kind=kLoop, calls=%fused_computation.1 | loop fusion | flops 2097152 | bytes 4196352 | tf_op jit(solution)/shard_map/convert_element_type | solution.py:584
  119.3 2.0 %shard_map.117 = (bf16[64,1024]{1,0:T(8,128)(2,1)}, f32[64,1024]{1,0:T(8,128)}, f32[64,1024]{1,0:T(8,128)}) custom-call(s32[64]{0:T(128)S(1)} %select_reduce_fusion.source, f32[64,16,128]{2,1,0:T(8,128)S(1)} %all-to-all-done.moments, f32[64,1024]{1,0:T(8,128)S(1)} %slice_bitcast_fusion.1.own, bf16[64,1024]{1,0:T(8,128)(2,1)S(1)} %collective-permute-done.18.came, ...), custom_call_target="tpu_custom_call" | custom-call | bytes 1048576 | tf_op jit(solution)/shard_map/pallas_call | solution.py:494
  (71 shorter events, 12.9 us)
Async XLA Ops:
  0.7 7.1 %collective-permute-start = (bf16[64,1024]{1,0:T(8,128)(2,1)}, bf16[64,1024]{1,0:T(8,128)(2,1)S(1)}, u32[]{:S(2)}, u32[]{:S(2)}) collective-permute-start(bf16[64,1024]{1,0:T(8,128)(2,1)} %bitcast.56), channel_id=1, source_target_pairs={{0,16},{16,0},{1,17},{17,1},{2,18},{18,2},{3,19},{19,3},{4,20},{20... | collective-permute-start | bytes 393224 | tf_op jit(solution)/shard_map/ppermute | solution.py:34
  7.8 14.1 %collective-permute-start.3 = (bf16[2,64,1024]{2,1,0:T(8,128)(2,1)S(1)}, bf16[2,64,1024]{2,1,0:T(8,128)(2,1)S(1)}, u32[]{:S(2)}, u32[]{:S(2)}) collective-permute-start(bf16[2,64,1024]{2,1,0:T(8,128)(2,1)S(1)} %pad_maximum_fusion.1), channel_id=1, source_target_pairs={{0,32},{2,6},{4,36},{6,10},{8,40},{10,14},{12,44},{14,2},{32,64},{... | collective-permute-start | bytes 786440 | tf_op jit(solution)/shard_map/ppermute | solution.py:44
  9.8 12.1 %collective-permute-start.2 = (bf16[2,64,1024]{2,1,0:T(8,128)(2,1)S(1)}, bf16[2,64,1024]{2,1,0:T(8,128)(2,1)S(1)}, u32[]{:S(2)}, u32[]{:S(2)}) collective-permute-start(bf16[2,64,1024]{2,1,0:T(8,128)(2,1)S(1)} %pad_maximum_fusion.1), channel_id=1, source_target_pairs={{0,64},{2,10},{4,68},{6,14},{8,72},{10,2},{12,76},{14,6},{32,96},{... | collective-permute-start | bytes 786440 | tf_op jit(solution)/shard_map/ppermute | solution.py:44
  13.4 8.5 %collective-permute-start.1 = (bf16[2,64,1024]{2,1,0:T(8,128)(2,1)S(1)}, bf16[2,64,1024]{2,1,0:T(8,128)(2,1)S(1)}, u32[]{:S(2)}, u32[]{:S(2)}) collective-permute-start(bf16[2,64,1024]{2,1,0:T(8,128)(2,1)S(1)} %pad_maximum_fusion.1), channel_id=1, source_target_pairs={{0,96},{2,14},{4,100},{6,2},{8,104},{10,6},{12,108},{14,10},{32,0}... | collective-permute-start | bytes 786440 | tf_op jit(solution)/shard_map/ppermute | solution.py:44
  22.6 11.1 %collective-permute-start.8 = (bf16[1024,3072]{1,0:T(8,128)(2,1)}, bf16[1024,3072]{1,0:T(8,128)(2,1)}, u32[]{:S(2)}, u32[]{:S(2)}) collective-permute-start(bf16[1024,3072]{1,0:T(8,128)(2,1)} %shard_map.111), channel_id=1, source_target_pairs={{0,2},{2,0},{1,3},{3,1},{4,6},{6,4},{5,7},{7,5},{8,10},{10,8},{9,1... | collective-permute-start | bytes 18874376 | tf_op jit(solution)/shard_map/ppermute | solution.py:34
  22.7 26.4 %collective-permute-start.4 = (bf16[64,8,1024]{2,1,0:T(8,128)(2,1)S(1)}, bf16[64,8,1024]{2,1,0:T(8,128)(2,1)}, u32[]{:S(2)}, u32[]{:S(2)}) collective-permute-start(bf16[64,8,1024]{2,1,0:T(8,128)(2,1)S(1)} %bitcast.41), channel_id=1, source_target_pairs={{0,12},{2,98},{4,0},{6,102},{8,4},{10,106},{12,8},{14,110},{32,44}... | collective-permute-start | bytes 3145736 | tf_op jit(solution)/shard_map/ppermute | solution.py:44
  25.5 23.6 %collective-permute-start.5 = (bf16[64,8,1024]{2,1,0:T(8,128)(2,1)S(1)}, bf16[64,8,1024]{2,1,0:T(8,128)(2,1)}, u32[]{:S(2)}, u32[]{:S(2)}) collective-permute-start(bf16[64,8,1024]{2,1,0:T(8,128)(2,1)S(1)} %bitcast.42), channel_id=1, source_target_pairs={{0,8},{2,66},{4,12},{6,70},{8,0},{10,74},{12,4},{14,78},{32,40},{3... | collective-permute-start | bytes 3145736 | tf_op jit(solution)/shard_map/ppermute | solution.py:44
  26.3 26.7 %collective-permute-start.6 = (bf16[64,8,1024]{2,1,0:T(8,128)(2,1)S(1)}, bf16[64,8,1024]{2,1,0:T(8,128)(2,1)S(1)}, u32[]{:S(2)}, u32[]{:S(2)}) collective-permute-start(bf16[64,8,1024]{2,1,0:T(8,128)(2,1)S(1)} %bitcast.43), channel_id=1, source_target_pairs={{0,4},{2,34},{4,8},{6,38},{8,12},{10,42},{12,0},{14,46},{32,36},{3... | collective-permute-start | bytes 3145736 | tf_op jit(solution)/shard_map/ppermute | solution.py:44
  27.2 25.9 %collective-permute-start.7 = (bf16[64,8,1024]{2,1,0:T(8,128)(2,1)S(1)}, bf16[64,8,1024]{2,1,0:T(8,128)(2,1)S(1)}, u32[]{:S(2)}, u32[]{:S(2)}) collective-permute-start(bf16[64,8,1024]{2,1,0:T(8,128)(2,1)S(1)} %bitcast.44), channel_id=1, source_target_pairs={{0,2},{2,0},{1,3},{3,1},{4,6},{6,4},{5,7},{7,5},{8,10},{10,8},{9,1... | collective-permute-start | bytes 3145736 | tf_op jit(solution)/shard_map/ppermute | solution.py:34
  33.6 31.3 %copy-start.4 = (s32[5]{0:T(128)S(1)}, s32[5]{0:T(128)}, u32[]{:S(2)}) copy-start(s32[5]{0:T(128)} %stack.46.place) | copy-start | bytes 64
  53.1 11.9 %copy-start.7 = (bf16[64,8,1024]{2,1,0:T(8,128)(2,1)}, bf16[64,8,1024]{2,1,0:T(8,128)(2,1)S(1)}, u32[]{:S(2)}) copy-start(bf16[64,8,1024]{2,1,0:T(8,128)(2,1)S(1)} %collective-permute-done.6.refs_3_) | copy-start | bytes 3145732
  53.1 5.9 %collective-permute-start.9 = (bf16[64,8,1024]{2,1,0:T(8,128)(2,1)}, bf16[64,8,1024]{2,1,0:T(8,128)(2,1)}, u32[]{:S(2)}, u32[]{:S(2)}) collective-permute-start(bf16[64,8,1024]{2,1,0:T(8,128)(2,1)} %collective-permute-done.4.refs_1_), channel_id=1, source_target_pairs={{0,2},{2,0},{1,3},{3,1},{4,6},{6,4},{5,7},{7,5},{8,10},{10,8},{9,1... | collective-permute-start | bytes 3145736 | tf_op jit(solution)/shard_map/ppermute | solution.py:34
  53.2 6.0 %collective-permute-start.10 = (bf16[64,8,1024]{2,1,0:T(8,128)(2,1)}, bf16[64,8,1024]{2,1,0:T(8,128)(2,1)}, u32[]{:S(2)}, u32[]{:S(2)}) collective-permute-start(bf16[64,8,1024]{2,1,0:T(8,128)(2,1)} %collective-permute-done.5.refs_2_), channel_id=1, source_target_pairs={{0,2},{2,0},{1,3},{3,1},{4,6},{6,4},{5,7},{7,5},{8,10},{10,8},{9,1... | collective-permute-start | bytes 3145736 | tf_op jit(solution)/shard_map/ppermute | solution.py:34
  53.7 5.5 %collective-permute-start.11 = (bf16[64,8,1024]{2,1,0:T(8,128)(2,1)S(1)}, bf16[64,8,1024]{2,1,0:T(8,128)(2,1)}, u32[]{:S(2)}, u32[]{:S(2)}) collective-permute-start(bf16[64,8,1024]{2,1,0:T(8,128)(2,1)S(1)} %collective-permute-done.6.refs_3_), channel_id=1, source_target_pairs={{0,2},{2,0},{1,3},{3,1},{4,6},{6,4},{5,7},{7,5},{8,10},{10,8},{9,1... | collective-permute-start | bytes 3145736 | tf_op jit(solution)/shard_map/ppermute | solution.py:34
  54.4 35.2 %all-to-all-start = ((f32[64,16,128]{2,1,0:T(8,128)}), f32[64,16,128]{2,1,0:T(8,128)S(1)}, u32[]{:S(2)}, u32[]{:S(2)}) async-start(f32[64,16,128]{2,1,0:T(8,128)} %shard_map.110), calls=%async_computation | async-start | bytes 1048576 | tf_op jit(solution)/shard_map/all_to_all | solution.py:561
  59.2 30.4 %collective-permute-start.12 = (bf16[8,64,1024]{2,1,0:T(8,128)(2,1)}, bf16[8,64,1024]{2,1,0:T(8,128)(2,1)}, u32[]{:S(2)}, u32[]{:S(2)}) collective-permute-start(bf16[8,64,1024]{2,1,0:T(8,128)(2,1)} %get-tuple-element.84), channel_id=1, source_target_pairs={{0,32},{2,6},{4,36},{6,10},{8,40},{10,14},{12,44},{14,2},{32,64},{... | collective-permute-start | bytes 3145736 | tf_op jit(solution)/shard_map/ppermute | solution.py:44
  60.7 31.4 %collective-permute-start.13 = (bf16[8,64,1024]{2,1,0:T(8,128)(2,1)}, bf16[8,64,1024]{2,1,0:T(8,128)(2,1)}, u32[]{:S(2)}, u32[]{:S(2)}) collective-permute-start(bf16[8,64,1024]{2,1,0:T(8,128)(2,1)} %get-tuple-element.85), channel_id=1, source_target_pairs={{0,64},{2,10},{4,68},{6,14},{8,72},{10,2},{12,76},{14,6},{32,96},{... | collective-permute-start | bytes 3145736 | tf_op jit(solution)/shard_map/ppermute | solution.py:44
  63.6 28.5 %collective-permute-start.14 = (bf16[8,64,1024]{2,1,0:T(8,128)(2,1)}, bf16[8,64,1024]{2,1,0:T(8,128)(2,1)}, u32[]{:S(2)}, u32[]{:S(2)}) collective-permute-start(bf16[8,64,1024]{2,1,0:T(8,128)(2,1)} %get-tuple-element.86), channel_id=1, source_target_pairs={{0,96},{2,14},{4,100},{6,2},{8,104},{10,6},{12,108},{14,10},{32,0}... | collective-permute-start | bytes 3145736 | tf_op jit(solution)/shard_map/ppermute | solution.py:44
  83.7 16.9 %copy-start.3 = (bf16[1024,1024]{1,0:T(8,128)(2,1)S(1)}, bf16[1024,1024]{1,0:T(8,128)(2,1)}, u32[]{:S(2)}) copy-start(bf16[1024,1024]{1,0:T(8,128)(2,1)} %cotangent.3) | copy-start | bytes 6291460
  86.7 29.0 %collective-permute-start.19 = (f16[1040,512]{1,0:T(8,128)(2,1)}, f16[1040,512]{1,0:T(8,128)(2,1)}, u32[]{:S(2)}, u32[]{:S(2)}) collective-permute-start(f16[1040,512]{1,0:T(8,128)(2,1)} %convert_element_type.56), channel_id=1, source_target_pairs={{0,1},{1,0},{2,3},{3,2},{4,5},{5,4},{6,7},{7,6},{8,9},{9,8},{10,11... | collective-permute-start | bytes 3194888 | tf_op jit(solution)/shard_map/ppermute | solution.py:34
  95.6 11.6 %collective-permute-start.15 = (bf16[2,64,1024]{2,1,0:T(8,128)(2,1)S(1)}, bf16[2,64,1024]{2,1,0:T(8,128)(2,1)S(1)}, u32[]{:S(2)}, u32[]{:S(2)}) collective-permute-start(bf16[2,64,1024]{2,1,0:T(8,128)(2,1)S(1)} %get-tuple-element.105), channel_id=1, source_target_pairs={{0,4},{2,34},{4,8},{6,38},{8,12},{10,42},{12,0},{14,46},{32,36},{3... | collective-permute-start | bytes 786440 | tf_op jit(solution)/shard_map/ppermute | solution.py:44
  96.6 10.6 %collective-permute-start.16 = (bf16[2,64,1024]{2,1,0:T(8,128)(2,1)S(1)}, bf16[2,64,1024]{2,1,0:T(8,128)(2,1)S(1)}, u32[]{:S(2)}, u32[]{:S(2)}) collective-permute-start(bf16[2,64,1024]{2,1,0:T(8,128)(2,1)S(1)} %get-tuple-element.106), channel_id=1, source_target_pairs={{0,8},{2,66},{4,12},{6,70},{8,0},{10,74},{12,4},{14,78},{32,40},{3... | collective-permute-start | bytes 786440 | tf_op jit(solution)/shard_map/ppermute | solution.py:44
  99.2 8.0 %collective-permute-start.17 = (bf16[2,64,1024]{2,1,0:T(8,128)(2,1)S(1)}, bf16[2,64,1024]{2,1,0:T(8,128)(2,1)S(1)}, u32[]{:S(2)}, u32[]{:S(2)}) collective-permute-start(bf16[2,64,1024]{2,1,0:T(8,128)(2,1)S(1)} %get-tuple-element.107), channel_id=1, source_target_pairs={{0,12},{2,98},{4,0},{6,102},{8,4},{10,106},{12,8},{14,110},{32,44}... | collective-permute-start | bytes 786440 | tf_op jit(solution)/shard_map/ppermute | solution.py:44
  107.4 8.6 %collective-permute-start.18 = (bf16[64,1024]{1,0:T(8,128)(2,1)S(1)}, bf16[64,1024]{1,0:T(8,128)(2,1)S(1)}, u32[]{:S(2)}, u32[]{:S(2)}) collective-permute-start(bf16[64,1024]{1,0:T(8,128)(2,1)S(1)} %fusion), channel_id=1, source_target_pairs={{0,16},{16,0},{1,17},{17,1},{2,18},{18,2},{3,19},{19,3},{4,20},{20... | collective-permute-start | bytes 393224 | tf_op jit(solution)/shard_map/ppermute | solution.py:34
  (6 other events, 33.9 us)
